TPU v7x, 512 devices: a whole 4x4x16 slice. The times are simulated.
512 devices in a mesh: dp: 16 (over x_lo, y, core), fsdp: 32 (over z, x_hi).
Axes of the slice: x: 4 (x_hi: 2, x_lo: 2; x = x_hi * 2 + x_lo), y: 4, z: 16, core: 2. Of those that a mesh axis runs over, the one named last changes fastest.
Arguments:
- activations: bfloat16 [57344, 8192], P('dp', 'fsdp'), may hold values from -6 to 6
- key_grads: bfloat16 [57344, 512], P(('dp', 'fsdp')), may hold values from -0.0234375 to 0.0234375
- partners: int32 [32], replicated, may hold values from 0 to 31, each once
- master_weight: float32 [8192, 512], P('fsdp'), may hold values from -6 to 6
- first_moment: float32 [8192, 512], P('fsdp'), may hold values from -1.75 to 1.75
- second_moment: float32 [8192, 512], P('fsdp'), may hold values from 0.05 to 2
Outputs:
- new_weight: float32 [8192, 512], P('fsdp')
- new_first: float32 [8192, 512], P('fsdp')
- new_second: float32 [8192, 512], P('fsdp')
Inputs may be any that keep to these rules, and one draw needn't show every extreme that they name: `partners`: each old shard index appears exactly once.
All inputs are finite; a program needn't handle non-finite values.
Results may differ from a plain program's by a relative error of at most 0.0003.
Values may be sent and summed in bfloat16 or wider, within the bound.
No kernel may reach another device: no remote copies, remote signals or barrier semaphores. Data moves between devices by JAX's collectives and lax.ppermute only.
A program may use at most 64 MiB of HBM per device.

v0:
```python
import jax
import jax.numpy as jnp
from jax import lax
from jax.sharding import PartitionSpec as P

beta_first = 0.9
beta_second = 0.95
learn_rate = 0.01
weight_decay = 0.1
correct_first = 1.0 - 0.9**10
correct_second = 1.0 - 0.95**10


def to_pieces(array, number):
    return array.reshape(number, array.shape[0] // number, array.shape[1])


def from_pieces(array):
    return array.reshape(array.shape[0] * array.shape[1], array.shape[2])


def relocate_states(states, partners):
    number = partners.shape[0]
    pieces = tuple((to_pieces(item, number) for item in states))
    spread = lax.all_to_all(pieces, "fsdp", split_axis=0, concat_axis=0, tiled=True)
    shuffled = tuple((jnp.take(item, partners, axis=0) for item in spread))
    arrived = lax.all_to_all(shuffled, "fsdp", split_axis=0, concat_axis=0, tiled=True)
    return tuple((from_pieces(item) for item in arrived))


def relocate_gradient(gradient, partners):
    number = partners.shape[0]
    spread = lax.all_to_all(
        to_pieces(gradient, number), "fsdp", split_axis=0, concat_axis=0, tiled=True
    )
    shuffled = jnp.take(spread, partners, axis=0)
    arrived = lax.all_to_all(shuffled, "fsdp", split_axis=0, concat_axis=0, tiled=True)
    return from_pieces(arrived)


def partial_gradient(features, key_grads):
    return lax.dot_general(
        features,
        lax.all_gather(key_grads, "fsdp", axis=0, tiled=True),
        (((0,), (0,)), ((), ())),
        preferred_element_type=jnp.float32,
    )


def local_gradient(features, key_grads):
    return lax.psum(partial_gradient(features, key_grads), "dp")


def adam_update(weight, first_moment, second_moment, gradient):
    new_first = beta_first * first_moment + (1.0 - beta_first) * gradient
    new_second = beta_second * second_moment + (1.0 - beta_second) * gradient * gradient
    step_size = new_first / correct_first / (jnp.sqrt(new_second / correct_second) + 1e-08)
    new_weight = weight - learn_rate * (step_size + weight_decay * weight)
    return (new_weight, new_first, new_second)


def on_device(activations, key_grads, partners, master_weight, first_moment, second_moment):
    weight, moment_one, moment_two = relocate_states(
        (master_weight, first_moment, second_moment), partners
    )
    gradient = relocate_gradient(local_gradient(activations, key_grads), partners)
    return adam_update(weight, moment_one, moment_two, gradient)


def solution(mesh):
    return jax.shard_map(
        on_device,
        mesh=mesh,
        in_specs=(
            P("dp", "fsdp"),
            P(("dp", "fsdp"), None),
            P(),
            P("fsdp", None),
            P("fsdp", None),
            P("fsdp", None),
        ),
        out_specs=(P("fsdp", None), P("fsdp", None), P("fsdp", None)),
        check_vma=False,
    )
```

profile of v0, /device:TPU:1, one launch (start us, length us, event | category | flops | bytes accessed | tf_op | source)
XLA Modules:
  0.0 530.7 jit_solution(948260479487875256)
XLA Ops:
  7.2 0.0 copy-start
  7.2 0.0 all-gather.2.cloned.1.call-start
  7.2 0.7 all-gather.2.cloned.1.call-update
  7.9 52.6 %all_to_all.40 = f32[32,8,512]{2,1,0:T(8,128)S(1)} all-to-all(f32[32,8,512]{2,1,0:T(8,128)} %bitcast.29), channel_id=1, replica_groups=mesh['dp'=16,'fsdp'=32] {'fsdp'}, dimensions={0} | all-to-all | bytes 1048576 | tf_op jit(solution)/shard_map/all_to_all | solution.py:25
  60.5 39.7 %all_to_all.41 = f32[32,8,512]{2,1,0:T(8,128)S(1)} all-to-all(f32[32,8,512]{2,1,0:T(8,128)} %bitcast.30), channel_id=1, replica_groups=mesh['dp'=16,'fsdp'=32] {'fsdp'}, dimensions={0} | all-to-all | bytes 1048576 | tf_op jit(solution)/shard_map/all_to_all | solution.py:25
  100.2 7.4 %all-to-all-start.6 = ((f32[32,8,512]{2,1,0:T(8,128)}), f32[32,8,512]{2,1,0:T(8,128)S(1)}, u32[]{:S(2)}, u32[]{:S(2)}) async-start(f32[32,8,512]{2,1,0:T(8,128)} %bitcast.31), calls=%async_computation.6 | async-start | bytes 1048576 | tf_op jit(solution)/shard_map/all_to_all | solution.py:25
  107.6 0.0 copy-start.2
  107.6 0.0 all-reduce.2.cloned.1.call-start
  107.7 75.3 %all-gather.2.cloned.1.call-done = bf16[3584,512]{1,0:T(8,128)(2,1)} async-done(((bf16[112,512]{1,0:T(8,128)(2,1)}), bf16[3584,512]{1,0:T(8,128)(2,1)}) %all-gather.2.cloned.1.call-update) | async-done | bytes 3670032 | tf_op jit(solution)/shard_map/all_gather | solution.py:44
  183.0 0.0 copy-done
  183.0 4.0 convolution_bitcast_fusion
  186.9 0.0 all-reduce.2.cloned.1.call-update
  187.0 0.0 all-to-all-done.6
  187.0 0.0 copy-start.1
  187.0 136.4 %all-reduce.2.cloned.1.call-done = f32[32,8,512]{2,1,0:T(8,128)} async-done(((f32[32,8,512]{2,1,0:T(8,128)}), f32[32,8,512]{2,1,0:T(8,128)}) %all-reduce.2.cloned.1.call-update) | async-done | bytes 524304 | tf_op jit(solution)/shard_map/psum | solution.py:51
  323.4 14.5 %all-to-all-start.4 = ((f32[32,8,512]{2,1,0:T(8,128)}), f32[32,8,512]{2,1,0:T(8,128)}, u32[]{:S(2)}, u32[]{:S(2)}) async-start(f32[32,8,512]{2,1,0:T(8,128)} %all-reduce.2.cloned.1.call-done), calls=%async_computation.4 | async-start | bytes 1048576 | tf_op jit(solution)/shard_map/all_to_all | solution.py:33
  337.9 0.0 copy-done.2
  337.9 0.0 copy-done.1
  338.0 0.6 gather_fusion
  338.6 0.6 gather_fusion.1
  339.1 1.6 gather_fusion.3
  340.8 27.9 %all-to-all-done.4 = f32[32,8,512]{2,1,0:T(8,128)} async-done(((f32[32,8,512]{2,1,0:T(8,128)}), f32[32,8,512]{2,1,0:T(8,128)}, u32[]{:S(2)}, u32[]{:S(2)}) %all-to-all-start.4) | async-done | bytes 524320 | tf_op jit(solution)/shard_map/all_to_all | solution.py:33
  368.7 2.4 gather_fusion.2
  371.1 1.2 broadcast_select_fusion
  372.3 37.4 %all_to_all.42 = f32[32,8,512]{2,1,0:T(8,128)S(1)} all-to-all(f32[32,8,512]{2,1,0:T(8,128)S(1)} %get-tuple-element.7), channel_id=1, replica_groups=mesh['dp'=16,'fsdp'=32] {'fsdp'}, dimensions={0} | all-to-all | bytes 1048576 | tf_op jit(solution)/shard_map/all_to_all | solution.py:27
  409.7 37.5 %all_to_all.43 = f32[32,8,512]{2,1,0:T(8,128)S(1)} all-to-all(f32[32,8,512]{2,1,0:T(8,128)S(1)} %get-tuple-element.8), channel_id=1, replica_groups=mesh['dp'=16,'fsdp'=32] {'fsdp'}, dimensions={0} | all-to-all | bytes 1048576 | tf_op jit(solution)/shard_map/all_to_all | solution.py:27
  447.3 37.6 %all_to_all.44 = f32[32,8,512]{2,1,0:T(8,128)S(1)} all-to-all(f32[32,8,512]{2,1,0:T(8,128)S(1)} %get-tuple-element.9), channel_id=1, replica_groups=mesh['dp'=16,'fsdp'=32] {'fsdp'}, dimensions={0} | all-to-all | bytes 1048576 | tf_op jit(solution)/shard_map/all_to_all | solution.py:37
  484.9 37.5 %all_to_all.45 = f32[32,8,512]{2,1,0:T(8,128)S(1)} all-to-all(f32[32,8,512]{2,1,0:T(8,128)S(1)} %get-tuple-element.10), channel_id=1, replica_groups=mesh['dp'=16,'fsdp'=32] {'fsdp'}, dimensions={0} | all-to-all | bytes 1048576 | tf_op jit(solution)/shard_map/all_to_all | solution.py:27
  522.4 1.4 bitcast_subtract_fusion
  (3 shorter events, 0.0 us)
Async XLA Ops:
  7.2 175.8 %copy-start = (bf16[3584,256]{1,0:T(8,128)(2,1)S(1)}, bf16[3584,256]{1,0:T(8,128)(2,1)}, u32[]{:S(2)}) copy-start(bf16[3584,256]{1,0:T(8,128)(2,1)} %param.8) | copy-start | bytes 5505028
  7.2 175.8 %all-gather.2.cloned.1.call-start = ((), (), s32[]{:S(2)}) async-start(), calls=%async_computation.8 | async-start | bytes 3784704 | tf_op jit(solution)/shard_map/all_gather | solution.py:44
  100.2 86.8 %all-to-all-start.6 = ((f32[32,8,512]{2,1,0:T(8,128)}), f32[32,8,512]{2,1,0:T(8,128)S(1)}, u32[]{:S(2)}, u32[]{:S(2)}) async-start(f32[32,8,512]{2,1,0:T(8,128)} %bitcast.31), calls=%async_computation.6 | async-start | bytes 1048576 | tf_op jit(solution)/shard_map/all_to_all | solution.py:25
  107.6 230.3 %copy-start.2 = (s32[32]{0:T(128)S(1)}, s32[32]{0:T(128)}, u32[]{:S(2)}) copy-start(s32[32]{0:T(128)} %param.10) | copy-start | bytes 388
  107.6 215.7 %all-reduce.2.cloned.1.call-start = ((), (), s32[]{:S(2)}) async-start(), calls=%async_computation.9 | async-start | bytes 1048576 | tf_op jit(solution)/shard_map/psum | solution.py:51
  187.0 151.0 %copy-start.1 = (f32[32,8,512]{2,1,0:T(8,128)}, f32[32,8,512]{2,1,0:T(8,128)S(1)}, u32[]{:S(2)}) copy-start(f32[32,8,512]{2,1,0:T(8,128)S(1)} %all-to-all-done.6) | copy-start | bytes 1572868
  323.4 45.3 %all-to-all-start.4 = ((f32[32,8,512]{2,1,0:T(8,128)}), f32[32,8,512]{2,1,0:T(8,128)}, u32[]{:S(2)}, u32[]{:S(2)}) async-start(f32[32,8,512]{2,1,0:T(8,128)} %all-reduce.2.cloned.1.call-done), calls=%async_computation.4 | async-start | bytes 1048576 | tf_op jit(solution)/shard_map/all_to_all | solution.py:33
Sparse Core Ops, SparseCore 0:
  11.1 171.8 all-gather.1
  187.1 136.2 all-reduce.1
where the time goes:
time: 533 us; the launch traced here: 531 us
  blocking collectives  242 us (45%)
  waiting for transfers between devices  240 us (45%)
  starting transfers between devices  22 us (4%)
  between operations  14.2 us (3%)
    psum x1, waiting for transfers between devices, local_gradient(): return lax.psum(partial_gradient(features, key_grads), 'dp')  136 us
    all_to_all x3, blocking collectives, relocate_states(): lax.all_to_all(shuffled, 'fsdp', split_axis=0, concat_axis=0, tiled=True)  112 us
    all_to_all x2, blocking collectives, relocate_states(): lax.all_to_all(pieces, 'fsdp', split_axis=0, concat_axis=0, tiled=True)  92.3 us
    all_gather x1, waiting for transfers between devices, partial_gradient(): lax.all_gather(key_grads, 'fsdp', axis=0, tiled=True)  75.3 us
    all_to_all x1, blocking collectives, relocate_gradient(): lax.all_to_all(shuffled, 'fsdp', split_axis=0, concat_axis=0, tiled=True)  37.6 us
    all_to_all x1, waiting for transfers between devices, relocate_gradient(): lax.all_to_all(to_pieces(gradient, number), 'fsdp', split_axis=0, concat_...  27.9 us
    all_to_all x1, starting transfers between devices, relocate_gradient(): lax.all_to_all(to_pieces(gradient, number), 'fsdp', split_axis=0, concat_...  14.5 us
  transfers between devices with their start and end apart: 4, of which 3 were waited for; matrix products, arithmetic and copies ran while one was open for 1% of the time, Pallas kernels for 0%

commit v1 on v0

v1 whole, which is shorter than its diff:
```python
import jax
import jax.numpy as jnp
from jax import lax
from jax.sharding import Mesh
from jax.sharding import PartitionSpec as P

beta_first = 0.9
beta_second = 0.95
learn_rate = 0.01
weight_decay = 0.1
correct_first = 1.0 - 0.9**10
correct_second = 1.0 - 0.95**10

PARTS = (("xl", 2), ("y", 4), ("c", 2), ("z", 16), ("xh", 2))
DP = ("xl", "y", "c")
FSDP = ("z", "xh")
PLANE = ("xl", "y", "c", "xh")
SWAP = [(0, 1), (1, 0)]


def exchange(array, axes):
    return lax.all_to_all(array, axes, split_axis=0, concat_axis=0, tiled=True)


def adam_update(weight, first_moment, second_moment, gradient):
    new_first = beta_first * first_moment + (1.0 - beta_first) * gradient
    new_second = beta_second * second_moment + (1.0 - beta_second) * gradient * gradient
    step_size = new_first / correct_first / (jnp.sqrt(new_second / correct_second) + 1e-08)
    new_weight = weight - learn_rate * (step_size + weight_decay * weight)
    return (new_weight, new_first, new_second)


def on_device(activations, key_grads, partners, master_weight, first_moment, second_moment):
    mine = lax.axis_index("xh")
    other = 1 - mine
    flat = lax.axis_index(DP)

    tokens = activations.reshape(16, 2, 112, 256)
    kept = lax.dynamic_index_in_dim(tokens, mine, axis=1, keepdims=False)
    sent = lax.dynamic_index_in_dim(tokens, other, axis=1, keepdims=False)
    got = lax.ppermute(sent, "xh", SWAP)

    states = jnp.stack((master_weight, first_moment, second_moment)).reshape(3, 16, 2, 8, 512)
    rows = lax.dynamic_index_in_dim(states, flat, axis=1, keepdims=False)
    own_rows = lax.dynamic_index_in_dim(rows, mine, axis=1, keepdims=False)
    peer_rows = lax.ppermute(
        lax.dynamic_index_in_dim(rows, other, axis=1, keepdims=False), "xh", SWAP
    )

    def gather(columns):
        return lax.all_gather(columns, "z", axis=0, tiled=True)

    cotangents = (gather(key_grads[:, :256]), gather(key_grads[:, 256:]))

    def product(features):
        features = features.reshape(1792, 256)
        parts = [
            lax.dot_general(
                features, half, (((0,), (0,)), ((), ())), preferred_element_type=jnp.float32
            )
            for half in cotangents
        ]
        return jnp.concatenate(parts, axis=1)

    def by_block(own, peer):
        return jnp.where(mine == 0, own, peer), jnp.where(mine == 0, peer, own)

    low, high = by_block(product(kept), product(got))
    partial = jnp.stack((low.reshape(32, 8, 512), high.reshape(32, 8, 512)), axis=1)
    gradient = jnp.sum(exchange(partial, PLANE).reshape(32, 2, 8, 512), axis=0)

    low_rows, high_rows = by_block(own_rows, peer_rows)
    old = jnp.stack((low_rows, high_rows), axis=1)
    new = jnp.stack(adam_update(old[0], old[1], old[2], gradient))

    pieces = new.reshape(3, 2, 8, 2, 256).transpose(2, 3, 1, 0, 4).reshape(16, 12, 128)
    spread = exchange(pieces, "z").reshape(32, 6, 128)
    shuffled = jnp.take(spread, partners, axis=0).reshape(16, 12, 128)
    arrived = exchange(shuffled, "z").reshape(8, 2, 2, 3, 256)
    placed = arrived.transpose(2, 3, 0, 1, 4).reshape(1, 2, 24, 512)

    shared = jnp.broadcast_to(placed, (16, 2, 24, 512)).reshape(32, 24, 512)
    whole = exchange(shared, PLANE).reshape(32, 3, 8, 512)
    return tuple(whole[:, i].reshape(256, 512) for i in range(3))


def solution(mesh):
    names = tuple(name for name, _ in PARTS)
    sizes = tuple(size for _, size in PARTS)
    fine = Mesh(mesh.devices.reshape(sizes), names)
    return jax.shard_map(
        on_device,
        mesh=fine,
        in_specs=(
            P(DP, FSDP),
            P(DP + FSDP, None),
            P(),
            P(FSDP, None),
            P(FSDP, None),
            P(FSDP, None),
        ),
        out_specs=(P(FSDP, None), P(FSDP, None), P(FSDP, None)),
        check_vma=False,
    )
```

time: 533 us -> 180 us (0.34)
  waiting for transfers between devices: 240 us -> 22.4 us
  blocking collectives: 242 us -> 108 us
  starting transfers between devices: 22 us -> 35.6 us
  between operations: 14.2 us -> 0.95 us
    all_to_all x6 -> x2, blocking collectives: 242 us -> 47.9 us  [exchange(): return lax.all_to_all(array, axes, split_axis=0, concat_axis=0, tiled=True)]
    psum x1 -> x0, waiting for transfers between devices: 136 us -> none  [local_gradient(): return lax.psum(partial_gradient(features, key_grads), 'dp')]
    all_gather x1 -> x0, waiting for transfers between devices: 75.3 us -> none  [partial_gradient(): lax.all_gather(key_grads, 'fsdp', axis=0, tiled=True)]
    all_gather x0 -> x2, blocking collectives: none -> 60.2 us  [gather(): return lax.all_gather(columns, 'z', axis=0, tiled=True)]
    all_to_all x2, waiting for transfers between devices: 27.9 us -> 12.6 us  [exchange(): return lax.all_to_all(array, axes, split_axis=0, concat_axis=0, tiled=True)]
    ppermute x0 -> x2, starting transfers between devices: none -> 10.3 us  [the longest x1 5.47 us: on_device(): got = lax.ppermute(sent, 'xh', SWAP)]
    ppermute x0 -> x2, waiting for transfers between devices: none -> 9.82 us  [the longest x1 9.81 us: on_device(): lax.ppermute(lax.dynamic_index_in_dim(rows, other, axis=1, keepdims=False...]
  transfers between devices with their start and end apart: 4 -> 4, of which waited for: 3 -> 3; matrix products, arithmetic and copies ran while one was open for 1% -> 2% of each run, Pallas kernels for 0% -> 0%
where the time goes in v1:
time: 180 us
  blocking collectives  108 us (60%)
  starting transfers between devices  35.6 us (20%)
  waiting for transfers between devices  22.4 us (12%)
  local copies, waits for them, and re-layouts  9.03 us (5%)
  other arithmetic  1.86 us (1%)
    all_gather x2, blocking collectives, gather(): return lax.all_gather(columns, 'z', axis=0, tiled=True)  60.2 us
    all_to_all x2, blocking collectives, exchange(): return lax.all_to_all(array, axes, split_axis=0, concat_axis=0, tiled=True)  47.9 us
    all_to_all x2, starting transfers between devices, exchange(): return lax.all_to_all(array, axes, split_axis=0, concat_axis=0, tiled=True)  25.4 us
    all_to_all x2, waiting for transfers between devices, exchange(): return lax.all_to_all(array, axes, split_axis=0, concat_axis=0, tiled=True)  12.6 us
    ppermute x1, waiting for transfers between devices, on_device(): lax.ppermute(lax.dynamic_index_in_dim(rows, other, axis=1, keepdims=False...  9.81 us
    ppermute x1, starting transfers between devices, on_device(): got = lax.ppermute(sent, 'xh', SWAP)  5.47 us
    ppermute x1, starting transfers between devices, on_device(): lax.ppermute(lax.dynamic_index_in_dim(rows, other, axis=1, keepdims=False...  4.8 us
  transfers between devices with their start and end apart: 4, of which 3 were waited for; matrix products, arithmetic and copies ran while one was open for 2% of the time, Pallas kernels for 0%

profile of v1, /device:TPU:1, one launch (start us, length us, event | category | flops | bytes accessed | tf_op | source)
XLA Modules:
  0.0 179.7 jit_solution(17742343593606919432)
XLA Ops:
  0.6 0.0 copy-start.1
  0.6 2.5 %constant_dynamic-slice_fusion = (bf16[16,1,112,256]{3,2,1,0:T(8,128)(2,1)S(1)}, bf16[16,112,256]{2,1,0:T(8,128)(2,1)}) fusion(bf16[16,2,112,256]{3,2,1,0:T(8,128)(2,1)} %bitcast.84, s32[]{:T(128)S(6)} %select_n.72, s32[]{:T(128)S(6)} %select_n.74), kind=kLoop, calls=%fused_computation.47 | loop fusion | bytes 3670024 | tf_op jit(solution)/shard_map/jit(dynamic_index_in_dim)/dynamic_slice | solution.py:39
  3.2 5.5 %collective-permute-start.1 = (bf16[16,112,256]{2,1,0:T(8,128)(2,1)}, bf16[16,112,256]{2,1,0:T(8,128)(2,1)}, u32[]{:S(2)}, u32[]{:S(2)}) collective-permute-start(bf16[16,112,256]{2,1,0:T(8,128)(2,1)} %get-tuple-element.7), channel_id=1, source_target_pairs={{0,1},{1,0},{2,3},{3,2},{4,5},{5,4},{6,7},{7,6},{8,9},{9,8},{10,11... | collective-permute-start | bytes 2752520 | tf_op jit(solution)/shard_map/ppermute | solution.py:41
  8.7 0.0 copy-done.1
  8.7 35.5 %all_gather.7 = bf16[1792,256]{1,0:T(8,128)(2,1)S(1)} all-gather(bf16[112,256]{1,0:T(8,128)(2,1)S(1)} %get-tuple-element.16), channel_id=1, replica_groups=mesh['xl'=2,'y'=4,'c'=2,'z'=16,'xh'=2] {'z'}, dimensions={0}, use_global_device_ids=true | all-gather | bytes 974848 | tf_op jit(solution)/shard_map/all_gather | solution.py:51
  44.2 0.6 copy.31
  44.8 0.4 convolution_bitcast_fusion.2
  45.3 24.7 %all_gather.6 = bf16[1792,256]{1,0:T(8,128)(2,1)S(1)} all-gather(bf16[112,256]{1,0:T(8,128)(2,1)S(1)} %get-tuple-element.15), channel_id=1, replica_groups=mesh['xl'=2,'y'=4,'c'=2,'z'=16,'xh'=2] {'z'}, dimensions={0}, use_global_device_ids=true | all-gather | bytes 974848 | tf_op jit(solution)/shard_map/all_gather | solution.py:51
  70.0 0.4 convolution_bitcast_fusion.3
  70.4 0.0 collective-permute-done.1
  70.4 1.5 copy.32
  71.9 0.4 convolution_bitcast_fusion
  72.3 0.4 convolution_bitcast_fusion.1
  72.7 0.1 fusion.9
  72.8 0.1 pad_maximum_fusion.1
  72.9 1.1 copy.33
  74.0 0.0 copy-start
  74.0 18.3 %all-to-all-start = ((f32[32,2,8,512]{3,2,1,0:T(8,128)}), f32[32,2,8,512]{3,2,1,0:T(8,128)S(1)}, u32[]{:S(2)}, u32[]{:S(2)}) async-start(f32[32,2,8,512]{3,2,1,0:T(8,128)} %copy.33), calls=%async_computation | async-start | bytes 2097152 | tf_op jit(solution)/shard_map/all_to_all | solution.py:22
  92.3 0.0 copy-done
  92.3 1.4 pad_maximum_fusion
  93.7 0.0 copy-start.2
  93.7 4.8 %collective-permute-start = (f32[3,8,512]{2,1,0:T(8,128)S(1)}, f32[3,8,512]{2,1,0:T(8,128)S(1)}, u32[]{:S(2)}, u32[]{:S(2)}) collective-permute-start(f32[3,8,512]{2,1,0:T(8,128)S(1)} %dynamic-slice_bitcast_fusion.1), channel_id=1, source_target_pairs={{0,1},{1,0},{2,3},{3,2},{4,5},{5,4},{6,7},{7,6},{8,9},{9,8},{10,11... | collective-permute-start | bytes 147464 | tf_op jit(solution)/shard_map/ppermute | solution.py:46
  98.5 9.8 %collective-permute-done = f32[3,8,512]{2,1,0:T(8,128)S(1)} collective-permute-done((f32[3,8,512]{2,1,0:T(8,128)S(1)}, f32[3,8,512]{2,1,0:T(8,128)S(1)}, u32[]{:S(2)}, u32[]{:S(2)}) %collective-permute-start) | collective-permute-done | bytes 49184 | tf_op jit(solution)/shard_map/ppermute | solution.py:46
  108.3 1.0 all-to-all-done
  109.3 0.1 reduce_sum.11
  109.6 0.1 copy.34
  109.7 0.7 reshape.212
  110.4 7.1 %all-to-all-start.1 = ((f32[16,12,128]{2,1,0:T(8,128)}), f32[16,12,128]{2,1,0:T(8,128)S(1)}, u32[]{:S(2)}, u32[]{:S(2)}) async-start(f32[16,12,128]{2,1,0:T(8,128)} %reshape.212), calls=%async_computation.1 | async-start | bytes 262144 | tf_op jit(solution)/shard_map/all_to_all | solution.py:22
  117.5 0.0 copy-done.2
  117.5 0.1 broadcast_in_dim.25
  117.6 0.1 copy.28
  117.7 0.1 copy.29
  117.9 11.6 %all-to-all-done.1 = f32[16,12,128]{2,1,0:T(8,128)S(1)} async-done(((f32[16,12,128]{2,1,0:T(8,128)}), f32[16,12,128]{2,1,0:T(8,128)S(1)}, u32[]{:S(2)}, u32[]{:S(2)}) %all-to-all-start.1) | async-done | bytes 98336 | tf_op jit(solution)/shard_map/all_to_all | solution.py:22
  129.5 0.6 gather_fusion
  130.1 0.1 broadcast_select_fusion
  130.2 17.5 %all_to_all.20 = f32[16,12,128]{2,1,0:T(8,128)S(1)} all-to-all(f32[16,12,128]{2,1,0:T(8,128)S(1)} %broadcast_select_fusion), channel_id=1, replica_groups=mesh['xl'=2,'y'=4,'c'=2,'z'=16,'xh'=2] {'z'}, dimensions={0} | all-to-all | bytes 196608 | tf_op jit(solution)/shard_map/all_to_all | solution.py:22
  147.7 0.1 reshape.214
  147.7 0.1 copy.35
  147.8 0.1 broadcast_in_dim.31
  147.9 0.2 broadcast_in_dim.32
  148.1 30.4 %all_to_all.21 = f32[32,24,512]{2,1,0:T(8,128)S(1)} all-to-all(f32[32,24,512]{2,1,0:T(8,128)S(1)} %bitcast.82), channel_id=1, replica_groups=mesh['xl'=2,'y'=4,'c'=2,'z'=16,'xh'=2] {'xl','y','c','xh'}, dimensions={0} | all-to-all | bytes 3145728 | tf_op jit(solution)/shard_map/all_to_all | solution.py:22
  178.5 1.2 slice_bitcast_fusion
  (15 shorter events, 0.3 us)
Async XLA Ops:
  0.6 8.0 %copy-start.1 = (bf16[112,512]{1,0:T(8,128)(2,1)S(1)}, bf16[112,512]{1,0:T(8,128)(2,1)}, u32[]{:S(2)}) copy-start(bf16[112,512]{1,0:T(8,128)(2,1)} %param.7) | copy-start | bytes 344068
  3.2 67.2 %collective-permute-start.1 = (bf16[16,112,256]{2,1,0:T(8,128)(2,1)}, bf16[16,112,256]{2,1,0:T(8,128)(2,1)}, u32[]{:S(2)}, u32[]{:S(2)}) collective-permute-start(bf16[16,112,256]{2,1,0:T(8,128)(2,1)} %get-tuple-element.7), channel_id=1, source_target_pairs={{0,1},{1,0},{2,3},{3,2},{4,5},{5,4},{6,7},{7,6},{8,9},{9,8},{10,11... | collective-permute-start | bytes 2752520 | tf_op jit(solution)/shard_map/ppermute | solution.py:41
  74.0 18.3 %copy-start = (f32[256,512]{1,0:T(8,128)S(1)}, f32[256,512]{1,0:T(8,128)}, u32[]{:S(2)}) copy-start(f32[256,512]{1,0:T(8,128)} %param.11) | copy-start | bytes 1572868
  74.0 35.3 %all-to-all-start = ((f32[32,2,8,512]{3,2,1,0:T(8,128)}), f32[32,2,8,512]{3,2,1,0:T(8,128)S(1)}, u32[]{:S(2)}, u32[]{:S(2)}) async-start(f32[32,2,8,512]{3,2,1,0:T(8,128)} %copy.33), calls=%async_computation | async-start | bytes 2097152 | tf_op jit(solution)/shard_map/all_to_all | solution.py:22
  93.7 23.8 %copy-start.2 = (s32[32]{0:T(128)S(1)}, s32[32]{0:T(128)}, u32[]{:S(2)}) copy-start(s32[32]{0:T(128)} %param.8) | copy-start | bytes 388
  93.7 14.6 %collective-permute-start = (f32[3,8,512]{2,1,0:T(8,128)S(1)}, f32[3,8,512]{2,1,0:T(8,128)S(1)}, u32[]{:S(2)}, u32[]{:S(2)}) collective-permute-start(f32[3,8,512]{2,1,0:T(8,128)S(1)} %dynamic-slice_bitcast_fusion.1), channel_id=1, source_target_pairs={{0,1},{1,0},{2,3},{3,2},{4,5},{5,4},{6,7},{7,6},{8,9},{9,8},{10,11... | collective-permute-start | bytes 147464 | tf_op jit(solution)/shard_map/ppermute | solution.py:46
  110.4 19.1 %all-to-all-start.1 = ((f32[16,12,128]{2,1,0:T(8,128)}), f32[16,12,128]{2,1,0:T(8,128)S(1)}, u32[]{:S(2)}, u32[]{:S(2)}) async-start(f32[16,12,128]{2,1,0:T(8,128)} %reshape.212), calls=%async_computation.1 | async-start | bytes 262144 | tf_op jit(solution)/shard_map/all_to_all | solution.py:22

commit v2 on v1

--- a/solution.py
+++ b/solution.py
@@ -40,13 +40,14 @@
     sent = lax.dynamic_index_in_dim(tokens, other, axis=1, keepdims=False)
     got = lax.ppermute(sent, "xh", SWAP)
 
-    states = jnp.stack((master_weight, first_moment, second_moment)).reshape(3, 16, 2, 8, 512)
-    rows = lax.dynamic_index_in_dim(states, flat, axis=1, keepdims=False)
-    own_rows = lax.dynamic_index_in_dim(rows, mine, axis=1, keepdims=False)
-    peer_rows = lax.ppermute(
-        lax.dynamic_index_in_dim(rows, other, axis=1, keepdims=False), "xh", SWAP
+    row = 16 * flat
+    rows = jnp.stack(
+        [
+            lax.dynamic_slice_in_dim(item, row, 16, axis=0)
+            for item in (master_weight, first_moment, second_moment)
+        ]
     )
-
+    along = lax.all_gather(rows, "z", axis=0, tiled=False)
     def gather(columns):
         return lax.all_gather(columns, "z", axis=0, tiled=True)
 
@@ -67,21 +68,29 @@
 
     low, high = by_block(product(kept), product(got))
     partial = jnp.stack((low.reshape(32, 8, 512), high.reshape(32, 8, 512)), axis=1)
+    along, partial = lax.optimization_barrier((along, partial))
+    here = 2 * lax.axis_index("z")
+    wanted = partners[here + mine]
+    wanted_there = partners[here + other]
+    from_here = lax.dynamic_index_in_dim(along, wanted // 2, axis=0, keepdims=False)
+    for_there = lax.dynamic_index_in_dim(along, wanted_there // 2, axis=0, keepdims=False)
+    from_there = lax.ppermute(for_there, "xh", SWAP)
+    picked = jnp.where(wanted % 2 == mine, from_here, from_there)
+    states = lax.all_gather(picked, DP, axis=0, tiled=False)
+    weight, moment_one, moment_two = (states[:, i].reshape(256, 512) for i in range(3))
+
     gradient = jnp.sum(exchange(partial, PLANE).reshape(32, 2, 8, 512), axis=0)
 
-    low_rows, high_rows = by_block(own_rows, peer_rows)
-    old = jnp.stack((low_rows, high_rows), axis=1)
-    new = jnp.stack(adam_update(old[0], old[1], old[2], gradient))
-
-    pieces = new.reshape(3, 2, 8, 2, 256).transpose(2, 3, 1, 0, 4).reshape(16, 12, 128)
-    spread = exchange(pieces, "z").reshape(32, 6, 128)
-    shuffled = jnp.take(spread, partners, axis=0).reshape(16, 12, 128)
-    arrived = exchange(shuffled, "z").reshape(8, 2, 2, 3, 256)
-    placed = arrived.transpose(2, 3, 0, 1, 4).reshape(1, 2, 24, 512)
-
-    shared = jnp.broadcast_to(placed, (16, 2, 24, 512)).reshape(32, 24, 512)
-    whole = exchange(shared, PLANE).reshape(32, 3, 8, 512)
-    return tuple(whole[:, i].reshape(256, 512) for i in range(3))
+    blocks = lax.all_gather(gradient, "z", axis=0, tiled=True)
+    placed = jnp.stack(
+        [
+            lax.dynamic_index_in_dim(blocks, partners[here + i], axis=0, keepdims=False)
+            for i in range(2)
+        ]
+    )
+    shared = jnp.broadcast_to(placed[None], (16, 2, 8, 512)).reshape(32, 8, 512)
+    merged = exchange(shared, PLANE).reshape(256, 512)
+    return adam_update(weight, moment_one, moment_two, merged)
 
 
 def solution(mesh):

time: 180 us -> 195 us (1.083)
  between operations: 0.95 us -> 22.7 us
  blocking collectives: 108 us -> 90.6 us
  other arithmetic: 1.86 us -> 5.44 us
  starting transfers between devices: 35.6 us -> 37.9 us
  waiting for transfers between devices: 22.4 us -> 24.5 us
  local copies, waits for them, and re-layouts: 9.03 us -> 11.1 us
    all_to_all x2 -> x0, blocking collectives: 47.9 us -> none  [exchange(): return lax.all_to_all(array, axes, split_axis=0, concat_axis=0, tiled=True)]
    all_gather x0 -> x1, blocking collectives: none -> 22.7 us  [on_device(): blocks = lax.all_gather(gradient, 'z', axis=0, tiled=True)]
    all_to_all x2, waiting for transfers between devices: 12.6 us -> 23.9 us  [exchange(): return lax.all_to_all(array, axes, split_axis=0, concat_axis=0, tiled=True)]
    ppermute x1, waiting for transfers between devices: 9.81 us -> 0.59 us  [on_device(): from_there = lax.ppermute(for_there, 'xh', SWAP)]
    all_gather x2, blocking collectives: 60.2 us -> 67.9 us  [gather(): return lax.all_gather(columns, 'z', axis=0, tiled=True)]
    all_to_all x2, starting transfers between devices: 25.4 us -> 28.3 us  [exchange(): return lax.all_to_all(array, axes, split_axis=0, concat_axis=0, tiled=True)]
  transfers between devices with their start and end apart: 4 -> 6, of which waited for: 3 -> 3; matrix products, arithmetic and copies ran while one was open for 2% -> 6% of each run, Pallas kernels for 0% -> 0%
where the time goes in v2:
time: 195 us
  blocking collectives  90.6 us (46%)
  starting transfers between devices  37.9 us (19%)
  waiting for transfers between devices  24.5 us (13%)
  between operations  22.7 us (12%)
  local copies, waits for them, and re-layouts  11.1 us (6%)
  other arithmetic  5.44 us (3%)
  matrix products  2.35 us (1%)
    all_gather x2, blocking collectives, gather(): return lax.all_gather(columns, 'z', axis=0, tiled=True)  67.9 us
    all_to_all x2, starting transfers between devices, exchange(): return lax.all_to_all(array, axes, split_axis=0, concat_axis=0, tiled=True)  28.3 us
    all_to_all x2, waiting for transfers between devices, exchange(): return lax.all_to_all(array, axes, split_axis=0, concat_axis=0, tiled=True)  23.9 us
    all_gather x1, blocking collectives, on_device(): blocks = lax.all_gather(gradient, 'z', axis=0, tiled=True)  22.7 us
    ppermute x1, starting transfers between devices, on_device(): got = lax.ppermute(sent, 'xh', SWAP)  5.47 us
    ppermute x1, starting transfers between devices, on_device(): from_there = lax.ppermute(for_there, 'xh', SWAP)  4.06 us
  transfers between devices with their start and end apart: 6, of which 3 were waited for; matrix products, arithmetic and copies ran while one was open for 6% of the time, Pallas kernels for 0%

profile of v2, /device:TPU:1, one launch (start us, length us, event | category | flops | bytes accessed | tf_op | source)
XLA Modules:
  0.0 194.6 jit_solution(14684087733494798660)
XLA Ops:
  7.2 0.0 copy-start
  7.2 0.0 all-gather.5.cloned.1.call-start
  7.2 1.0 copy-done
  8.2 0.8 dynamic-slice_bitcast_fusion.2
  9.0 0.6 pad_maximum_fusion.3
  9.6 0.0 all-gather.5.cloned.1.call-update
  9.7 0.0 all-gather.7.cloned.1.call-start
  9.7 0.0 copy-start.2
  9.7 0.0 copy-start.3
  9.7 2.6 %constant_dynamic-slice_fusion.2 = (bf16[16,1,112,256]{3,2,1,0:T(8,128)(2,1)S(1)}, bf16[16,112,256]{2,1,0:T(8,128)(2,1)}) fusion(bf16[16,2,112,256]{3,2,1,0:T(8,128)(2,1)} %bitcast.77, s32[]{:T(128)S(6)} %select_n.91, s32[]{:T(128)S(6)} %select_n.92), kind=kLoop, calls=%fused_computation.37 | loop fusion | bytes 3670024 | tf_op jit(solution)/shard_map/jit(dynamic_index_in_dim)/dynamic_slice | solution.py:39
  12.3 5.5 %collective-permute-start = (bf16[16,112,256]{2,1,0:T(8,128)(2,1)}, bf16[16,112,256]{2,1,0:T(8,128)(2,1)}, u32[]{:S(2)}, u32[]{:S(2)}) collective-permute-start(bf16[16,112,256]{2,1,0:T(8,128)(2,1)} %get-tuple-element.11), channel_id=1, source_target_pairs={{0,1},{1,0},{2,3},{3,2},{4,5},{5,4},{6,7},{7,6},{8,9},{9,8},{10,11... | collective-permute-start | bytes 2752520 | tf_op jit(solution)/shard_map/ppermute | solution.py:41
  17.8 0.0 copy-done.2
  17.8 0.6 fusion.16
  18.4 38.8 %all_gather.24 = bf16[1792,256]{1,0:T(8,128)(2,1)S(1)} all-gather(bf16[112,256]{1,0:T(8,128)(2,1)S(1)} %get-tuple-element.20), channel_id=1, replica_groups=mesh['xl'=2,'y'=4,'c'=2,'z'=16,'xh'=2] {'z'}, dimensions={0}, use_global_device_ids=true | all-gather | bytes 974848 | tf_op jit(solution)/shard_map/all_gather | solution.py:52
  57.2 0.0 copy-done.3
  57.2 0.7 fusion.17
  60.2 0.6 copy.14
  60.8 0.4 convolution_bitcast_fusion.2
  61.2 29.1 %all_gather.23 = bf16[1792,256]{1,0:T(8,128)(2,1)S(1)} all-gather(bf16[112,256]{1,0:T(8,128)(2,1)} %get-tuple-element.19), channel_id=1, replica_groups=mesh['xl'=2,'y'=4,'c'=2,'z'=16,'xh'=2] {'z'}, dimensions={0}, use_global_device_ids=true | all-gather | bytes 974848 | tf_op jit(solution)/shard_map/all_gather | solution.py:52
  90.4 1.1 convolution_bitcast_fusion.3
  91.5 0.0 collective-permute-done
  91.5 1.5 copy.15
  92.9 0.4 convolution_bitcast_fusion
  93.4 0.0 copy-start.1
  93.4 0.4 convolution_bitcast_fusion.1
  93.8 0.5 copy-done.1
  94.3 0.1 fusion.13
  94.5 0.1 pad_maximum_fusion
  94.5 0.0 all-gather.5.cloned.1.call-done
  94.6 0.9 dynamic-slice_bitcast_fusion.1
  95.5 4.1 %collective-permute-start.1 = (f32[3,16,512]{2,1,0:T(8,128)S(1)}, f32[3,16,512]{2,1,0:T(8,128)S(1)}, u32[]{:S(2)}, u32[]{:S(2)}) collective-permute-start(f32[3,16,512]{2,1,0:T(8,128)S(1)} %dynamic-slice_bitcast_fusion.1), channel_id=1, source_target_pairs={{0,1},{1,0},{2,3},{3,2},{4,5},{5,4},{6,7},{7,6},{8,9},{9,8},{10,11... | collective-permute-start | bytes 294920 | tf_op jit(solution)/shard_map/ppermute | solution.py:77
  101.7 0.6 collective-permute-done.1
  102.3 1.5 bitcast_select_fusion
  103.9 0.0 all-gather.7.cloned.1.call-update
  103.9 1.1 copy.16
  105.0 17.4 %all-to-all-start = ((f32[32,2,8,512]{3,2,1,0:T(8,128)}), f32[32,2,8,512]{3,2,1,0:T(8,128)S(1)}, u32[]{:S(2)}, u32[]{:S(2)}) async-start(f32[32,2,8,512]{3,2,1,0:T(8,128)} %copy.16), calls=%async_computation | async-start | bytes 2097152 | tf_op jit(solution)/shard_map/all_to_all | solution.py:22
  126.4 14.0 %all-to-all-done = f32[32,2,8,512]{3,2,1,0:T(8,128)S(1)} async-done(((f32[32,2,8,512]{3,2,1,0:T(8,128)}), f32[32,2,8,512]{3,2,1,0:T(8,128)S(1)}, u32[]{:S(2)}, u32[]{:S(2)}) %all-to-all-start) | async-done | bytes 1048608 | tf_op jit(solution)/shard_map/all_to_all | solution.py:22
  140.4 0.1 reduce_sum.9
  140.4 22.7 %all_gather.27 = f32[32,8,512]{2,1,0:T(8,128)S(1)} all-gather(f32[2,8,512]{2,1,0:T(8,128)S(1)} %reduce_sum.9), channel_id=1, replica_groups=mesh['xl'=2,'y'=4,'c'=2,'z'=16,'xh'=2] {'z'}, dimensions={0}, use_global_device_ids=true | all-gather | bytes 557056 | tf_op jit(solution)/shard_map/all_gather | solution.py:84
  163.1 0.9 broadcast_in_dim.2
  164.0 10.9 %all-to-all-start.1 = ((f32[32,8,512]{2,1,0:T(8,128)}), f32[32,8,512]{2,1,0:T(8,128)S(1)}, u32[]{:S(2)}, u32[]{:S(2)}) async-start(f32[32,8,512]{2,1,0:T(8,128)} %bitcast.27), calls=%async_computation.1 | async-start | bytes 1048576 | tf_op jit(solution)/shard_map/all_to_all | solution.py:22
  174.9 0.0 all-gather.7.cloned.1.call-done
  174.9 1.6 slice_multiply_fusion
  176.5 9.9 %all-to-all-done.1 = f32[32,8,512]{2,1,0:T(8,128)S(1)} async-done(((f32[32,8,512]{2,1,0:T(8,128)}), f32[32,8,512]{2,1,0:T(8,128)S(1)}, u32[]{:S(2)}, u32[]{:S(2)}) %all-to-all-start.1) | async-done | bytes 524320 | tf_op jit(solution)/shard_map/all_to_all | solution.py:22
  186.3 1.4 bitcast_subtract_fusion
  (3 shorter events, 0.0 us)
Async XLA Ops:
  7.2 1.0 copy-start
  7.2 87.4 %all-gather.5.cloned.1.call-start = ((), (), s32[]{:S(2)}) async-start(), calls=%async_computation.2 | async-start | bytes 1671168 | tf_op jit(solution)/shard_map/all_gather | solution.py:50
  9.7 165.2 %all-gather.7.cloned.1.call-start = ((), (), s32[]{:S(2)}) async-start(), calls=%async_computation.3 | async-start | bytes 1671168 | tf_op jit(solution)/shard_map/all_gather | solution.py:79
  9.7 8.1 %copy-start.2 = (bf16[112,512]{1,0:T(8,128)(2,1)S(1)}, bf16[112,512]{1,0:T(8,128)(2,1)}, u32[]{:S(2)}) copy-start(bf16[112,512]{1,0:T(8,128)(2,1)} %param.7) | copy-start | bytes 344068
  9.7 47.5 %copy-start.3 = (s32[32]{0:T(128)S(1)}, s32[32]{0:T(128)}, u32[]{:S(2)}) copy-start(s32[32]{0:T(128)} %param.8) | copy-start | bytes 388
  12.3 79.2 %collective-permute-start = (bf16[16,112,256]{2,1,0:T(8,128)(2,1)}, bf16[16,112,256]{2,1,0:T(8,128)(2,1)}, u32[]{:S(2)}, u32[]{:S(2)}) collective-permute-start(bf16[16,112,256]{2,1,0:T(8,128)(2,1)} %get-tuple-element.11), channel_id=1, source_target_pairs={{0,1},{1,0},{2,3},{3,2},{4,5},{5,4},{6,7},{7,6},{8,9},{9,8},{10,11... | collective-permute-start | bytes 2752520 | tf_op jit(solution)/shard_map/ppermute | solution.py:41
  93.4 1.0 copy-start.1
  95.5 6.9 %collective-permute-start.1 = (f32[3,16,512]{2,1,0:T(8,128)S(1)}, f32[3,16,512]{2,1,0:T(8,128)S(1)}, u32[]{:S(2)}, u32[]{:S(2)}) collective-permute-start(f32[3,16,512]{2,1,0:T(8,128)S(1)} %dynamic-slice_bitcast_fusion.1), channel_id=1, source_target_pairs={{0,1},{1,0},{2,3},{3,2},{4,5},{5,4},{6,7},{7,6},{8,9},{9,8},{10,11... | collective-permute-start | bytes 294920 | tf_op jit(solution)/shard_map/ppermute | solution.py:77
  105.0 35.4 %all-to-all-start = ((f32[32,2,8,512]{3,2,1,0:T(8,128)}), f32[32,2,8,512]{3,2,1,0:T(8,128)S(1)}, u32[]{:S(2)}, u32[]{:S(2)}) async-start(f32[32,2,8,512]{3,2,1,0:T(8,128)} %copy.16), calls=%async_computation | async-start | bytes 2097152 | tf_op jit(solution)/shard_map/all_to_all | solution.py:22
  164.0 22.4 %all-to-all-start.1 = ((f32[32,8,512]{2,1,0:T(8,128)}), f32[32,8,512]{2,1,0:T(8,128)S(1)}, u32[]{:S(2)}, u32[]{:S(2)}) async-start(f32[32,8,512]{2,1,0:T(8,128)} %bitcast.27), calls=%async_computation.1 | async-start | bytes 1048576 | tf_op jit(solution)/shard_map/all_to_all | solution.py:22
Sparse Core Ops, SparseCore 0:
  10.7 70.4 all-gather.4
  104.0 54.0 all-gather.6

commit v3 on v1

v3 whole, which is shorter than its diff:
```python
import jax
import jax.numpy as jnp
from jax import lax
from jax.sharding import Mesh
from jax.sharding import PartitionSpec as P

beta_first = 0.9
beta_second = 0.95
learn_rate = 0.01
weight_decay = 0.1
correct_first = 1.0 - 0.9**10
correct_second = 1.0 - 0.95**10

PARTS = (("xl", 2), ("y", 4), ("c", 2), ("z", 16), ("xh", 2))
DP = ("xl", "y", "c")
FSDP = ("z", "xh")
CHIPS = ("xl", "y", "xh")
SWAP = [(0, 1), (1, 0)]
KEY_SCALE = 2.0**21
REST_SCALE = 2.0**11
SECOND_SCALE = 2.0**-6


def exchange(array):
    return lax.all_to_all(array, CHIPS, split_axis=0, concat_axis=0, tiled=True)


def pick(array, index, axis):
    return lax.dynamic_index_in_dim(array, index, axis=axis, keepdims=False)


def split_halves(values):
    high = lax.reduce_precision(values, exponent_bits=5, mantissa_bits=10)
    rest = (values - high) * REST_SCALE
    return jnp.stack((high.astype(jnp.float16), rest.astype(jnp.float16)))


def join_halves(halves):
    wide = halves.astype(jnp.float32)
    return wide[0] + wide[1] * (1.0 / REST_SCALE)


def adam_update(weight, first_moment, second_moment, gradient):
    new_first = beta_first * first_moment + (1.0 - beta_first) * gradient
    new_second = beta_second * second_moment + (1.0 - beta_second) * gradient * gradient
    step_size = new_first / correct_first / (jnp.sqrt(new_second / correct_second) + 1e-08)
    new_weight = weight - learn_rate * (step_size + weight_decay * weight)
    return (new_weight, new_first, new_second)


def on_device(activations, key_grads, partners, master_weight, first_moment, second_moment):
    mine = lax.axis_index("xh")
    other = 1 - mine
    core = lax.axis_index("c")
    column = lax.axis_index(("xl", "y"))

    def by_block(own, peer):
        return jnp.where(mine == 0, own, peer), jnp.where(mine == 0, peer, own)

    tokens = activations.reshape(16, 2, 112, 256)
    kept = pick(tokens, mine, 1)
    got = lax.ppermute(pick(tokens, other, 1), "xh", SWAP)

    first_row = 128 * core + 16 * column

    def eight(side):
        return jnp.stack(
            [
                lax.dynamic_slice_in_dim(item, first_row + 8 * side, 8, axis=0)
                for item in (master_weight, first_moment, second_moment)
            ]
        )

    own_rows = eight(mine)
    peer_rows = lax.ppermute(eight(other), "xh", SWAP)

    scaled = (key_grads.astype(jnp.float32) * KEY_SCALE).astype(jnp.float16)
    cotangents = lax.all_gather(scaled, "z", axis=0, tiled=True)
    cotangents, got, peer_rows = lax.optimization_barrier((cotangents, got, peer_rows))
    cotangents = (cotangents.astype(jnp.float32) * (1.0 / KEY_SCALE)).astype(jnp.bfloat16)

    def product(features):
        return lax.dot_general(
            features.reshape(1792, 256),
            cotangents,
            (((0,), (0,)), ((), ())),
            preferred_element_type=jnp.float32,
        ).reshape(2, 16, 8, 512)

    partial = jnp.stack(by_block(product(kept), product(got)), axis=2)
    summed = pick(partial, core, 0) + lax.ppermute(pick(partial, 1 - core, 0), "c", SWAP)
    gradient = jnp.sum(exchange(summed), axis=0)

    old = jnp.stack(by_block(own_rows, peer_rows), axis=1)
    weight, moment_one, moment_two = adam_update(old[0], old[1], old[2], gradient)

    slices = jnp.stack((weight, moment_one, moment_two * SECOND_SCALE), axis=1)
    along = lax.all_gather(split_halves(slices), "z", axis=0, tiled=False)
    here = 2 * lax.axis_index("z")

    def wanted(index):
        place = partners[index]
        return join_halves(pick(pick(along, place // 2, 0), place % 2, 1))

    placed = jnp.stack([wanted(here + i) for i in range(2)]).reshape(1, 2, 3, 8, 512)
    half = exchange(jnp.broadcast_to(placed, (8, 2, 3, 8, 512)).reshape(16, 3, 8, 512))
    sibling = lax.ppermute(half, "c", SWAP)
    lower = jnp.where(core == 0, half, sibling)
    upper = jnp.where(core == 0, sibling, half)

    def whole(i):
        return jnp.concatenate(
            (lower[:, i].reshape(128, 512), upper[:, i].reshape(128, 512)), axis=0
        )

    return whole(0), whole(1), whole(2) * (1.0 / SECOND_SCALE)


def solution(mesh):
    names = tuple(name for name, _ in PARTS)
    sizes = tuple(size for _, size in PARTS)
    fine = Mesh(mesh.devices.reshape(sizes), names)
    return jax.shard_map(
        on_device,
        mesh=fine,
        in_specs=(
            P(DP, FSDP),
            P(DP + FSDP, None),
            P(),
            P(FSDP, None),
            P(FSDP, None),
            P(FSDP, None),
        ),
        out_specs=(P(FSDP, None), P(FSDP, None), P(FSDP, None)),
        check_vma=False,
    )
```

time: 180 us -> 150 us (0.83)
  blocking collectives: 108 us -> 86.2 us
  waiting for transfers between devices: 22.4 us -> 7.05 us
  between operations: 0.95 us -> 6.12 us
  other arithmetic: 1.86 us -> 3.93 us
    all_to_all x2 -> x1, blocking collectives: 47.9 us -> 13.8 us  [exchange(): return lax.all_to_all(array, CHIPS, split_axis=0, concat_axis=0, tiled=True)]
    all_to_all x2 -> x1, starting transfers between devices: 25.4 us -> 6.8 us  [exchange(): return lax.all_to_all(array, CHIPS, split_axis=0, concat_axis=0, tiled=True)]
    ppermute x2 -> x4, starting transfers between devices: 10.3 us -> 28.5 us  [the longest x1 12.7 us: on_device(): sibling = lax.ppermute(half, 'c', SWAP)]
    all_gather x2, blocking collectives: 60.2 us -> 72.4 us  [the longest x1 42.6 us: on_device(): cotangents = lax.all_gather(scaled, 'z', axis=0, tiled=True)]
    all_to_all x2 -> x1, waiting for transfers between devices: 12.6 us -> 3.65 us  [exchange(): return lax.all_to_all(array, CHIPS, split_axis=0, concat_axis=0, tiled=True)]
    ppermute x2 -> x4, waiting for transfers between devices: 9.82 us -> 3.41 us  [the longest x1 1.89 us: on_device(): sibling = lax.ppermute(half, 'c', SWAP)]
  transfers between devices with their start and end apart: 4 -> 5, of which waited for: 3 -> 3; matrix products, arithmetic and copies ran while one was open for 2% -> 3% of each run, Pallas kernels for 0% -> 0%
where the time goes in v3:
time: 150 us; the launch traced here: 149 us
  blocking collectives  86.2 us (57%)
  starting transfers between devices  35.3 us (24%)
  local copies, waits for them, and re-layouts  7.73 us (5%)
  waiting for transfers between devices  7.05 us (5%)
  between operations  6.12 us (4%)
  other arithmetic  3.93 us (3%)
  matrix products  2.56 us (2%)
    all_gather x1, blocking collectives, on_device(): cotangents = lax.all_gather(scaled, 'z', axis=0, tiled=True)  42.6 us
    all_gather x1, blocking collectives, on_device(): along = lax.all_gather(split_halves(slices), 'z', axis=0, tiled=False)  29.8 us
    all_to_all x1, blocking collectives, exchange(): return lax.all_to_all(array, CHIPS, split_axis=0, concat_axis=0, tiled=True)  13.8 us
    ppermute x1, starting transfers between devices, on_device(): sibling = lax.ppermute(half, 'c', SWAP)  12.7 us
    ppermute x1, starting transfers between devices, on_device(): lax.ppermute(pick(partial, 1 - core, 0), 'c', SWAP)  8.49 us
    all_to_all x1, starting transfers between devices, exchange(): return lax.all_to_all(array, CHIPS, split_axis=0, concat_axis=0, tiled=True)  6.8 us
    ppermute x1, starting transfers between devices, on_device(): peer_rows = lax.ppermute(eight(other), 'xh', SWAP)  5.48 us
    all_to_all x1, waiting for transfers between devices, exchange(): return lax.all_to_all(array, CHIPS, split_axis=0, concat_axis=0, tiled=True)  3.65 us
  transfers between devices with their start and end apart: 5, of which 3 were waited for; matrix products, arithmetic and copies ran while one was open for 3% of the time, Pallas kernels for 0%

profile of v3, /device:TPU:1, one launch (start us, length us, event | category | flops | bytes accessed | tf_op | source)
XLA Modules:
  0.0 148.9 jit_solution(6171606550308994454)
XLA Ops:
  0.6 0.7 dynamic-slice_bitcast_fusion.6
  1.4 0.8 dynamic-slice_bitcast_fusion.4
  2.2 5.5 %collective-permute-start.1 = (f32[3,8,512]{2,1,0:T(8,128)S(1)}, f32[3,8,512]{2,1,0:T(8,128)S(1)}, u32[]{:S(2)}, u32[]{:S(2)}) collective-permute-start(f32[3,8,512]{2,1,0:T(8,128)S(1)} %pad_maximum_fusion.6), channel_id=1, source_target_pairs={{0,1},{1,0},{2,3},{3,2},{4,5},{5,4},{6,7},{7,6},{8,9},{9,8},{10,11... | collective-permute-start | bytes 147464 | tf_op jit(solution)/shard_map/ppermute | solution.py:75
  7.7 0.0 copy-start
  7.7 2.6 %constant_dynamic-slice_fusion = (bf16[16,1,112,256]{3,2,1,0:T(8,128)(2,1)S(1)}, bf16[16,112,256]{2,1,0:T(8,128)(2,1)}) fusion(bf16[16,2,112,256]{3,2,1,0:T(8,128)(2,1)} %bitcast.108, s32[]{:T(128)S(6)} %select_n.114, s32[]{:T(128)S(6)} %select_n.109), kind=kLoop, calls=%fused_computation.70 | loop fusion | bytes 3670024 | tf_op jit(solution)/shard_map/jit(dynamic_index_in_dim)/dynamic_slice | solution.py:29
  10.2 1.9 %collective-permute-start = (bf16[16,112,256]{2,1,0:T(8,128)(2,1)}, bf16[16,112,256]{2,1,0:T(8,128)(2,1)}, u32[]{:S(2)}, u32[]{:S(2)}) collective-permute-start(bf16[16,112,256]{2,1,0:T(8,128)(2,1)} %get-tuple-element.12), channel_id=1, source_target_pairs={{0,1},{1,0},{2,3},{3,2},{4,5},{5,4},{6,7},{7,6},{8,9},{9,8},{10,11... | collective-permute-start | bytes 2752520 | tf_op jit(solution)/shard_map/ppermute | solution.py:62
  12.1 0.0 copy-done
  12.2 42.6 %all-gather.3 = f16[1792,512]{1,0:T(8,128)(2,1)S(1)} all-gather(f16[112,512]{1,0:T(8,128)(2,1)S(1)} %multiply_convert_fusion.1), channel_id=1, replica_groups=mesh['xl'=2,'y'=4,'c'=2,'z'=16,'xh'=2] {'z'}, dimensions={0}, use_global_device_ids=true | all-gather | bytes 1949696 | tf_op jit(solution)/shard_map/all_gather | solution.py:78
  54.8 1.4 copy.32
  56.1 0.0 collective-permute-done.1
  56.1 0.0 collective-permute-done
  56.2 1.5 copy.33
  57.6 1.9 %fusion.3 = f32[2,16,8,512]{3,2,1,0:T(8,128)S(1)} fusion(bf16[2,16,8,1792]{3,2,1,0:T(8,128)(2,1)} %bitcast.110, f16[1792,512]{1,0:T(8,128)(2,1)S(1)} %all-gather.3), kind=kOutput, calls=%fused_computation.3 | convolution fusion | flops 472514560 | bytes 3276800 | tf_op jit(solution)/shard_map/dot_general | solution.py:83
  59.5 0.7 select_bitcast_fusion
  60.2 0.1 fusion.6
  60.3 0.0 copy-start.1
  60.3 8.5 %collective-permute-start.2 = (f32[16,2,8,512]{3,2,1,0:T(8,128)S(1)}, f32[16,2,8,512]{3,2,1,0:T(8,128)S(1)}, u32[]{:S(2)}, u32[]{:S(2)}) collective-permute-start(f32[16,2,8,512]{3,2,1,0:T(8,128)S(1)} %bitcast.111), channel_id=1, source_target_pairs={{0,32},{32,0},{1,33},{33,1},{2,34},{34,2},{3,35},{35,3},{4,36},{36... | collective-permute-start | bytes 1572872 | tf_op jit(solution)/shard_map/ppermute | solution.py:91
  68.8 1.5 %collective-permute-done.2 = f32[16,2,8,512]{3,2,1,0:T(8,128)S(1)} collective-permute-done((f32[16,2,8,512]{3,2,1,0:T(8,128)S(1)}, f32[16,2,8,512]{3,2,1,0:T(8,128)S(1)}, u32[]{:S(2)}, u32[]{:S(2)}) %collective-permute-start.2) | collective-permute-done | bytes 524320 | tf_op jit(solution)/shard_map/ppermute | solution.py:91
  70.3 0.9 bitcast_add_fusion
  71.2 6.8 %all-to-all-start = ((f32[16,2,8,512]{3,2,1,0:T(8,128)}), f32[16,2,8,512]{3,2,1,0:T(8,128)S(1)}, u32[]{:S(2)}, u32[]{:S(2)}) async-start(f32[16,2,8,512]{3,2,1,0:T(8,128)} %bitcast_add_fusion), calls=%async_computation | async-start | bytes 1048576 | tf_op jit(solution)/shard_map/all_to_all | solution.py:25
  78.0 0.0 copy-done.1
  78.0 0.6 fusion.26
  83.9 3.6 %all-to-all-done = f32[16,2,8,512]{3,2,1,0:T(8,128)S(1)} async-done(((f32[16,2,8,512]{3,2,1,0:T(8,128)}), f32[16,2,8,512]{3,2,1,0:T(8,128)S(1)}, u32[]{:S(2)}, u32[]{:S(2)}) %all-to-all-start) | async-done | bytes 524320 | tf_op jit(solution)/shard_map/all_to_all | solution.py:25
  87.6 0.1 reduce-precision_convert_fusion
  87.8 29.8 %all-gather.4 = f16[32,2,3,8,512]{4,3,2,1,0:T(8,128)(2,1)S(1)} all-gather(f16[2,2,3,8,512]{4,3,2,1,0:T(8,128)(2,1)S(1)} %pad_maximum_fusion.3), channel_id=2, replica_groups=mesh['xl'=2,'y'=4,'c'=2,'z'=16,'xh'=2] {'z'}, dimensions={0}, use_global_device_ids=true | all-gather | bytes 1671168 | tf_op jit(solution)/shard_map/all_gather | solution.py:98
  117.7 0.1 broadcast_in_dim.2
  117.8 13.8 %all_to_all.10 = f32[16,3,8,512]{3,2,1,0:T(8,128)S(1)} all-to-all(f32[16,3,8,512]{3,2,1,0:T(8,128)S(1)} %bitcast.107), channel_id=1, replica_groups=mesh['xl'=2,'y'=4,'c'=2,'z'=16,'xh'=2] {'xl','y','xh'}, dimensions={0} | all-to-all | bytes 1572864 | tf_op jit(solution)/shard_map/all_to_all | solution.py:25
  131.5 12.7 %collective-permute-start.3 = (f32[16,3,8,512]{3,2,1,0:T(8,128)S(1)}, f32[16,3,8,512]{3,2,1,0:T(8,128)S(1)}, u32[]{:S(2)}, u32[]{:S(2)}) collective-permute-start(f32[16,3,8,512]{3,2,1,0:T(8,128)S(1)} %all_to_all.10), channel_id=1, source_target_pairs={{0,32},{32,0},{1,33},{33,1},{2,34},{34,2},{3,35},{35,3},{4,36},{36... | collective-permute-start | bytes 2359304 | tf_op jit(solution)/shard_map/ppermute | solution.py:107
  144.2 1.9 %collective-permute-done.3 = f32[16,3,8,512]{3,2,1,0:T(8,128)S(1)} collective-permute-done((f32[16,3,8,512]{3,2,1,0:T(8,128)S(1)}, f32[16,3,8,512]{3,2,1,0:T(8,128)S(1)}, u32[]{:S(2)}, u32[]{:S(2)}) %collective-permute-start.3) | collective-permute-done | bytes 786464 | tf_op jit(solution)/shard_map/ppermute | solution.py:107
  146.1 0.2 broadcast_select_fusion.1
  146.3 0.1 slice_bitcast_fusion.1
  146.4 0.1 slice_bitcast_fusion
  146.4 0.8 maximum_multiply_fusion
  147.3 0.8 pad_maximum_fusion.1
  148.1 0.8 pad_maximum_fusion
  (12 shorter events, 0.2 us)
Async XLA Ops:
  2.2 54.0 %collective-permute-start.1 = (f32[3,8,512]{2,1,0:T(8,128)S(1)}, f32[3,8,512]{2,1,0:T(8,128)S(1)}, u32[]{:S(2)}, u32[]{:S(2)}) collective-permute-start(f32[3,8,512]{2,1,0:T(8,128)S(1)} %pad_maximum_fusion.6), channel_id=1, source_target_pairs={{0,1},{1,0},{2,3},{3,2},{4,5},{5,4},{6,7},{7,6},{8,9},{9,8},{10,11... | collective-permute-start | bytes 147464 | tf_op jit(solution)/shard_map/ppermute | solution.py:75
  7.7 4.5 %copy-start = (bf16[112,512]{1,0:T(8,128)(2,1)S(1)}, bf16[112,512]{1,0:T(8,128)(2,1)}, u32[]{:S(2)}) copy-start(bf16[112,512]{1,0:T(8,128)(2,1)} %param.7) | copy-start | bytes 344068
  10.2 45.9 %collective-permute-start = (bf16[16,112,256]{2,1,0:T(8,128)(2,1)}, bf16[16,112,256]{2,1,0:T(8,128)(2,1)}, u32[]{:S(2)}, u32[]{:S(2)}) collective-permute-start(bf16[16,112,256]{2,1,0:T(8,128)(2,1)} %get-tuple-element.12), channel_id=1, source_target_pairs={{0,1},{1,0},{2,3},{3,2},{4,5},{5,4},{6,7},{7,6},{8,9},{9,8},{10,11... | collective-permute-start | bytes 2752520 | tf_op jit(solution)/shard_map/ppermute | solution.py:62
  60.3 17.8 %copy-start.1 = (s32[32]{0:T(128)S(1)}, s32[32]{0:T(128)}, u32[]{:S(2)}) copy-start(s32[32]{0:T(128)} %param.8) | copy-start | bytes 388
  60.3 10.0 %collective-permute-start.2 = (f32[16,2,8,512]{3,2,1,0:T(8,128)S(1)}, f32[16,2,8,512]{3,2,1,0:T(8,128)S(1)}, u32[]{:S(2)}, u32[]{:S(2)}) collective-permute-start(f32[16,2,8,512]{3,2,1,0:T(8,128)S(1)} %bitcast.111), channel_id=1, source_target_pairs={{0,32},{32,0},{1,33},{33,1},{2,34},{34,2},{3,35},{35,3},{4,36},{36... | collective-permute-start | bytes 1572872 | tf_op jit(solution)/shard_map/ppermute | solution.py:91
  71.2 16.3 %all-to-all-start = ((f32[16,2,8,512]{3,2,1,0:T(8,128)}), f32[16,2,8,512]{3,2,1,0:T(8,128)S(1)}, u32[]{:S(2)}, u32[]{:S(2)}) async-start(f32[16,2,8,512]{3,2,1,0:T(8,128)} %bitcast_add_fusion), calls=%async_computation | async-start | bytes 1048576 | tf_op jit(solution)/shard_map/all_to_all | solution.py:25
  131.5 14.6 %collective-permute-start.3 = (f32[16,3,8,512]{3,2,1,0:T(8,128)S(1)}, f32[16,3,8,512]{3,2,1,0:T(8,128)S(1)}, u32[]{:S(2)}, u32[]{:S(2)}) collective-permute-start(f32[16,3,8,512]{3,2,1,0:T(8,128)S(1)} %all_to_all.10), channel_id=1, source_target_pairs={{0,32},{32,0},{1,33},{33,1},{2,34},{34,2},{3,35},{35,3},{4,36},{36... | collective-permute-start | bytes 2359304 | tf_op jit(solution)/shard_map/ppermute | solution.py:107

commit v4 on v3

--- a/solution.py
+++ b/solution.py
@@ -15,14 +15,16 @@
 DP = ("xl", "y", "c")
 FSDP = ("z", "xh")
 CHIPS = ("xl", "y", "xh")
+PLANE = ("c", "xl", "y", "xh")
 SWAP = [(0, 1), (1, 0)]
 KEY_SCALE = 2.0**21
 REST_SCALE = 2.0**11
 SECOND_SCALE = 2.0**-6
+PARTIAL_SCALE = 2.0**7
 
 
-def exchange(array):
-    return lax.all_to_all(array, CHIPS, split_axis=0, concat_axis=0, tiled=True)
+def exchange(array, axes):
+    return lax.all_to_all(array, axes, split_axis=0, concat_axis=0, tiled=True)
 
 
 def pick(array, index, axis):
@@ -58,7 +60,6 @@
         return jnp.where(mine == 0, own, peer), jnp.where(mine == 0, peer, own)
 
     tokens = activations.reshape(16, 2, 112, 256)
-    kept = pick(tokens, mine, 1)
     got = lax.ppermute(pick(tokens, other, 1), "xh", SWAP)
 
     first_row = 128 * core + 16 * column
@@ -76,7 +77,10 @@
 
     scaled = (key_grads.astype(jnp.float32) * KEY_SCALE).astype(jnp.float16)
     cotangents = lax.all_gather(scaled, "z", axis=0, tiled=True)
-    cotangents, got, peer_rows = lax.optimization_barrier((cotangents, got, peer_rows))
+    cotangents, got, peer_rows, tokens = lax.optimization_barrier(
+        (cotangents, got, peer_rows, tokens)
+    )
+    kept = pick(tokens, mine, 1)
     cotangents = (cotangents.astype(jnp.float32) * (1.0 / KEY_SCALE)).astype(jnp.bfloat16)
 
     def product(features):
@@ -85,11 +89,11 @@
             cotangents,
             (((0,), (0,)), ((), ())),
             preferred_element_type=jnp.float32,
-        ).reshape(2, 16, 8, 512)
+        ).reshape(32, 8, 512)
 
-    partial = jnp.stack(by_block(product(kept), product(got)), axis=2)
-    summed = pick(partial, core, 0) + lax.ppermute(pick(partial, 1 - core, 0), "c", SWAP)
-    gradient = jnp.sum(exchange(summed), axis=0)
+    partial = jnp.stack(by_block(product(kept), product(got)), axis=1)
+    pieces = exchange((partial * PARTIAL_SCALE).astype(jnp.float16), PLANE)
+    gradient = jnp.sum(pieces.astype(jnp.float32), axis=0) * (1.0 / PARTIAL_SCALE)
 
     old = jnp.stack(by_block(own_rows, peer_rows), axis=1)
     weight, moment_one, moment_two = adam_update(old[0], old[1], old[2], gradient)
@@ -103,7 +107,7 @@
         return join_halves(pick(pick(along, place // 2, 0), place % 2, 1))
 
     placed = jnp.stack([wanted(here + i) for i in range(2)]).reshape(1, 2, 3, 8, 512)
-    half = exchange(jnp.broadcast_to(placed, (8, 2, 3, 8, 512)).reshape(16, 3, 8, 512))
+    half = exchange(jnp.broadcast_to(placed, (8, 2, 3, 8, 512)).reshape(16, 3, 8, 512), CHIPS)
     sibling = lax.ppermute(half, "c", SWAP)
     lower = jnp.where(core == 0, half, sibling)
     upper = jnp.where(core == 0, sibling, half)

time: 150 us -> 149 us (level)
  starting transfers between devices: 35.3 us -> 30.8 us
  local copies, waits for them, and re-layouts: 7.73 us -> 9.5 us
  blocking collectives: 86.2 us -> 87.7 us
    ppermute x1 -> x0, starting transfers between devices: 8.49 us -> none  [on_device(): lax.ppermute(pick(partial, 1 - core, 0), 'c', SWAP)]
    all_to_all x1, starting transfers between devices: 6.8 us -> 14.4 us  [exchange(): return lax.all_to_all(array, axes, split_axis=0, concat_axis=0, tiled=True)]
    ppermute x1, starting transfers between devices: 12.7 us -> 8.94 us  [on_device(): sibling = lax.ppermute(half, 'c', SWAP)]
    ppermute x1, starting transfers between devices: 5.48 us -> 1.92 us  [on_device(): peer_rows = lax.ppermute(eight(other), 'xh', SWAP)]
    ppermute x1, starting transfers between devices: 1.91 us -> 5.47 us  [on_device(): got = lax.ppermute(pick(tokens, other, 1), 'xh', SWAP)]
    all_to_all x1, waiting for transfers between devices: 3.65 us -> 5.83 us  [exchange(): return lax.all_to_all(array, axes, split_axis=0, concat_axis=0, tiled=True)]
    dynamic_slice x2 -> x1, local copies, waits for them, and re-layouts: 2.59 us -> 0.99 us  [pick(): return lax.dynamic_index_in_dim(array, index, axis=axis, keepdims=False)]
    ppermute x1 -> x0, waiting for transfers between devices: 1.51 us -> none  [on_device(): lax.ppermute(pick(partial, 1 - core, 0), 'c', SWAP)]
  transfers between devices with their start and end apart: 5 -> 4, of which waited for: 3 -> 2; matrix products, arithmetic and copies ran while one was open for 3% -> 1% of each run, Pallas kernels for 0% -> 0%
where the time goes in v4:
time: 149 us; the launch traced here: 148 us
  blocking collectives  87.7 us (59%)
  starting transfers between devices  30.8 us (21%)
  local copies, waits for them, and re-layouts  9.5 us (6%)
  waiting for transfers between devices  7.72 us (5%)
  between operations  6.13 us (4%)
  matrix products  3.29 us (2%)
  other arithmetic  3.14 us (2%)
    all_gather x1, blocking collectives, on_device(): cotangents = lax.all_gather(scaled, 'z', axis=0, tiled=True)  43.7 us
    all_gather x1, blocking collectives, on_device(): along = lax.all_gather(split_halves(slices), 'z', axis=0, tiled=False)  31.1 us
    all_to_all x1, starting transfers between devices, exchange(): return lax.all_to_all(array, axes, split_axis=0, concat_axis=0, tiled=True)  14.4 us
    all_to_all x1, blocking collectives, exchange(): return lax.all_to_all(array, axes, split_axis=0, concat_axis=0, tiled=True)  12.9 us
    ppermute x1, starting transfers between devices, on_device(): sibling = lax.ppermute(half, 'c', SWAP)  8.94 us
    all_to_all x1, waiting for transfers between devices, exchange(): return lax.all_to_all(array, axes, split_axis=0, concat_axis=0, tiled=True)  5.83 us
    ppermute x1, starting transfers between devices, on_device(): got = lax.ppermute(pick(tokens, other, 1), 'xh', SWAP)  5.47 us
    dot_general x2, matrix products, product(): lax.dot_general(features.reshape(1792, 256), cotangents, (((0,), (0,)), (...  3.29 us
  transfers between devices with their start and end apart: 4, of which 2 were waited for; matrix products, arithmetic and copies ran while one was open for 1% of the time, Pallas kernels for 0%

profile of v4, /device:TPU:1, one launch (start us, length us, event | category | flops | bytes accessed | tf_op | source)
XLA Modules:
  0.0 148.3 jit_solution(9491273126730094420)
XLA Ops:
  0.6 0.0 copy-start
  0.6 0.0 copy-start.2
  0.7 1.5 copy-done
  2.1 1.0 dynamic-slice_bitcast_fusion
  3.1 5.5 %collective-permute-start = (bf16[16,112,256]{2,1,0:T(8,128)(2,1)}, bf16[16,112,256]{2,1,0:T(8,128)(2,1)S(1)}, u32[]{:S(2)}, u32[]{:S(2)}) collective-permute-start(bf16[16,112,256]{2,1,0:T(8,128)(2,1)} %dynamic-slice_bitcast_fusion), channel_id=1, source_target_pairs={{0,1},{1,0},{2,3},{3,2},{4,5},{5,4},{6,7},{7,6},{8,9},{9,8},{10,11... | collective-permute-start | bytes 2752520 | tf_op jit(solution)/shard_map/ppermute | solution.py:63
  8.6 0.7 dynamic-slice_bitcast_fusion.6
  9.4 0.8 dynamic-slice_bitcast_fusion.4
  10.1 1.9 %collective-permute-start.1 = (f32[3,8,512]{2,1,0:T(8,128)S(1)}, f32[3,8,512]{2,1,0:T(8,128)S(1)}, u32[]{:S(2)}, u32[]{:S(2)}) collective-permute-start(f32[3,8,512]{2,1,0:T(8,128)S(1)} %pad_maximum_fusion.6), channel_id=1, source_target_pairs={{0,1},{1,0},{2,3},{3,2},{4,5},{5,4},{6,7},{7,6},{8,9},{9,8},{10,11... | collective-permute-start | bytes 147464 | tf_op jit(solution)/shard_map/ppermute | solution.py:76
  12.1 0.0 copy-done.2
  12.1 43.7 %all-gather.3 = f16[1792,512]{1,0:T(8,128)(2,1)} all-gather(f16[112,512]{1,0:T(8,128)(2,1)S(1)} %multiply_convert_fusion.1), channel_id=1, replica_groups=mesh['xl'=2,'y'=4,'c'=2,'z'=16,'xh'=2] {'z'}, dimensions={0}, use_global_device_ids=true | all-gather | bytes 1949696 | tf_op jit(solution)/shard_map/all_gather | solution.py:79
  55.8 0.0 collective-permute-done.1
  55.8 0.0 collective-permute-done
  55.8 1.4 copy.28
  57.2 1.0 constant_dynamic-slice_fusion
  58.2 1.5 copy.27
  59.6 0.0 copy-start.1
  59.6 2.6 %fusion.1 = f32[32,8,512]{2,1,0:T(8,128)S(1)} fusion(f16[1792,512]{1,0:T(8,128)(2,1)} %all-gather.3, bf16[256,1792]{1,0:T(8,128)(2,1)} %copy.28), kind=kOutput, calls=%fused_computation.2 | convolution fusion | flops 472514560 | bytes 3276800 | tf_op jit(solution)/shard_map/dot_general | solution.py:87
  62.2 0.0 copy-done.1
  62.3 0.7 select_bitcast_fusion.1
  63.0 0.0 copy-start.3
  63.0 0.1 fusion.5
  63.1 0.9 copy.29
  64.0 14.4 %all-to-all-start = ((f16[32,2,8,512]{3,2,1,0:T(8,128)(2,1)}), f16[32,2,8,512]{3,2,1,0:T(8,128)(2,1)S(1)}, u32[]{:S(2)}, u32[]{:S(2)}) async-start(f16[32,2,8,512]{3,2,1,0:T(8,128)(2,1)} %copy.29), calls=%async_computation | async-start | bytes 1048576 | tf_op jit(solution)/shard_map/all_to_all | solution.py:27
  78.5 0.0 copy-done.3
  78.5 0.6 fusion.27
  84.3 5.8 %all-to-all-done = f16[32,2,8,512]{3,2,1,0:T(8,128)(2,1)S(1)} async-done(((f16[32,2,8,512]{3,2,1,0:T(8,128)(2,1)}), f16[32,2,8,512]{3,2,1,0:T(8,128)(2,1)S(1)}, u32[]{:S(2)}, u32[]{:S(2)}) %all-to-all-start) | async-done | bytes 524320 | tf_op jit(solution)/shard_map/all_to_all | solution.py:27
  90.2 0.1 convert_reduce_fusion
  90.3 0.1 reduce-precision_convert_fusion
  90.4 31.1 %all-gather.4 = f16[32,2,3,8,512]{4,3,2,1,0:T(8,128)(2,1)S(1)} all-gather(f16[2,2,3,8,512]{4,3,2,1,0:T(8,128)(2,1)S(1)} %pad_maximum_fusion.3), channel_id=2, replica_groups=mesh['xl'=2,'y'=4,'c'=2,'z'=16,'xh'=2] {'z'}, dimensions={0}, use_global_device_ids=true | all-gather | bytes 1671168 | tf_op jit(solution)/shard_map/all_gather | solution.py:102
  121.6 0.1 broadcast_in_dim.2
  121.7 12.9 %all_to_all.10 = f32[16,3,8,512]{3,2,1,0:T(8,128)S(1)} all-to-all(f32[16,3,8,512]{3,2,1,0:T(8,128)S(1)} %bitcast.104), channel_id=1, replica_groups=mesh['xl'=2,'y'=4,'c'=2,'z'=16,'xh'=2] {'xl','y','xh'}, dimensions={0} | all-to-all | bytes 1572864 | tf_op jit(solution)/shard_map/all_to_all | solution.py:27
  134.6 8.9 %collective-permute-start.2 = (f32[16,3,8,512]{3,2,1,0:T(8,128)S(1)}, f32[16,3,8,512]{3,2,1,0:T(8,128)S(1)}, u32[]{:S(2)}, u32[]{:S(2)}) collective-permute-start(f32[16,3,8,512]{3,2,1,0:T(8,128)S(1)} %all_to_all.10), channel_id=1, source_target_pairs={{0,32},{32,0},{1,33},{33,1},{2,34},{34,2},{3,35},{35,3},{4,36},{36... | collective-permute-start | bytes 2359304 | tf_op jit(solution)/shard_map/ppermute | solution.py:111
  143.6 1.9 %collective-permute-done.2 = f32[16,3,8,512]{3,2,1,0:T(8,128)S(1)} collective-permute-done((f32[16,3,8,512]{3,2,1,0:T(8,128)S(1)}, f32[16,3,8,512]{3,2,1,0:T(8,128)S(1)}, u32[]{:S(2)}, u32[]{:S(2)}) %collective-permute-start.2) | collective-permute-done | bytes 786464 | tf_op jit(solution)/shard_map/ppermute | solution.py:111
  145.5 0.2 broadcast_select_fusion.1
  145.7 0.1 slice_bitcast_fusion
  145.7 0.1 slice_bitcast_fusion.1
  145.8 0.8 pad_maximum_fusion
  146.6 0.8 pad_maximum_fusion.1
  147.5 0.8 maximum_multiply_fusion.1
  (10 shorter events, 0.2 us)
Async XLA Ops:
  0.6 1.5 %copy-start = (bf16[3584,256]{1,0:T(8,128)(2,1)S(1)}, bf16[3584,256]{1,0:T(8,128)(2,1)}, u32[]{:S(2)}) copy-start(bf16[3584,256]{1,0:T(8,128)(2,1)} %param.6) | copy-start | bytes 5505028
  0.6 11.4 %copy-start.2 = (bf16[112,512]{1,0:T(8,128)(2,1)S(1)}, bf16[112,512]{1,0:T(8,128)(2,1)}, u32[]{:S(2)}) copy-start(bf16[112,512]{1,0:T(8,128)(2,1)} %param.7) | copy-start | bytes 344068
  3.1 52.7 %collective-permute-start = (bf16[16,112,256]{2,1,0:T(8,128)(2,1)}, bf16[16,112,256]{2,1,0:T(8,128)(2,1)S(1)}, u32[]{:S(2)}, u32[]{:S(2)}) collective-permute-start(bf16[16,112,256]{2,1,0:T(8,128)(2,1)} %dynamic-slice_bitcast_fusion), channel_id=1, source_target_pairs={{0,1},{1,0},{2,3},{3,2},{4,5},{5,4},{6,7},{7,6},{8,9},{9,8},{10,11... | collective-permute-start | bytes 2752520 | tf_op jit(solution)/shard_map/ppermute | solution.py:63
  10.1 45.7 %collective-permute-start.1 = (f32[3,8,512]{2,1,0:T(8,128)S(1)}, f32[3,8,512]{2,1,0:T(8,128)S(1)}, u32[]{:S(2)}, u32[]{:S(2)}) collective-permute-start(f32[3,8,512]{2,1,0:T(8,128)S(1)} %pad_maximum_fusion.6), channel_id=1, source_target_pairs={{0,1},{1,0},{2,3},{3,2},{4,5},{5,4},{6,7},{7,6},{8,9},{9,8},{10,11... | collective-permute-start | bytes 147464 | tf_op jit(solution)/shard_map/ppermute | solution.py:76
  59.6 2.6 %copy-start.1 = (f16[1792,512]{1,0:T(8,128)(2,1)S(1)}, f16[1792,512]{1,0:T(8,128)(2,1)}, u32[]{:S(2)}) copy-start(f16[1792,512]{1,0:T(8,128)(2,1)} %all-gather.3) | copy-start | bytes 5505028
  63.0 15.5 %copy-start.3 = (s32[32]{0:T(128)S(1)}, s32[32]{0:T(128)}, u32[]{:S(2)}) copy-start(s32[32]{0:T(128)} %param.8) | copy-start | bytes 388
  64.0 26.1 %all-to-all-start = ((f16[32,2,8,512]{3,2,1,0:T(8,128)(2,1)}), f16[32,2,8,512]{3,2,1,0:T(8,128)(2,1)S(1)}, u32[]{:S(2)}, u32[]{:S(2)}) async-start(f16[32,2,8,512]{3,2,1,0:T(8,128)(2,1)} %copy.29), calls=%async_computation | async-start | bytes 1048576 | tf_op jit(solution)/shard_map/all_to_all | solution.py:27
  134.6 10.8 %collective-permute-start.2 = (f32[16,3,8,512]{3,2,1,0:T(8,128)S(1)}, f32[16,3,8,512]{3,2,1,0:T(8,128)S(1)}, u32[]{:S(2)}, u32[]{:S(2)}) collective-permute-start(f32[16,3,8,512]{3,2,1,0:T(8,128)S(1)} %all_to_all.10), channel_id=1, source_target_pairs={{0,32},{32,0},{1,33},{33,1},{2,34},{34,2},{3,35},{35,3},{4,36},{36... | collective-permute-start | bytes 2359304 | tf_op jit(solution)/shard_map/ppermute | solution.py:111

commit v5 on v4

--- a/solution.py
+++ b/solution.py
@@ -1,6 +1,8 @@
 import jax
 import jax.numpy as jnp
 from jax import lax
+from jax.experimental import pallas as pl
+from jax.experimental.pallas import tpu as pltpu
 from jax.sharding import Mesh
 from jax.sharding import PartitionSpec as P
 
@@ -28,7 +30,9 @@
 
 
 def pick(array, index, axis):
-    return lax.dynamic_index_in_dim(array, index, axis=axis, keepdims=False)
+    return lax.dynamic_index_in_dim(
+        array, index, axis=axis, keepdims=False, allow_negative_indices=False
+    )
 
 
 def split_halves(values):
@@ -50,6 +54,75 @@
     return (new_weight, new_first, new_second)
 
 
+def products_kernel(mine_ref, tokens_ref, got_ref, cotangents_ref, out_ref, kept, arrived):
+    mine = mine_ref[0]
+    fetch = pltpu.make_async_copy(tokens_ref.at[:, mine], kept, arrived)
+    fetch.start()
+
+    def product(features):
+        return lax.dot_general(
+            features,
+            cotangents_ref[...],
+            (((0,), (0,)), ((), ())),
+            preferred_element_type=jnp.float32,
+        ).reshape(32, 8, 512)
+
+    out_ref[:, 1 - mine] = product(got_ref[...])
+    fetch.wait()
+    out_ref[:, mine] = product(kept[...].reshape(1792, 256))
+
+
+def products(mine, tokens, got, cotangents):
+    in_vmem = pl.BlockSpec(memory_space=pltpu.VMEM)
+    return pl.pallas_call(
+        products_kernel,
+        out_shape=jax.ShapeDtypeStruct((32, 2, 8, 512), jnp.float32),
+        in_specs=[
+            pl.BlockSpec(memory_space=pltpu.SMEM),
+            pl.BlockSpec(memory_space=pl.ANY),
+            in_vmem,
+            in_vmem,
+        ],
+        out_specs=in_vmem,
+        scratch_shapes=[
+            pltpu.VMEM((16, 112, 256), jnp.bfloat16),
+            pltpu.SemaphoreType.DMA,
+        ],
+        compiler_params=pltpu.CompilerParams(vmem_limit_bytes=40 * 1024 * 1024),
+        cost_estimate=pl.CostEstimate(
+            flops=2 * 2 * 1792 * 256 * 512, bytes_accessed=6 * 1024 * 1024, transcendentals=0
+        ),
+    )(mine.reshape(1), tokens, got, cotangents)
+
+
+def assemble_kernel(core_ref, half_ref, sibling_ref, *refs):
+    outs, done = refs[:3], refs[3]
+    core = core_ref[0]
+    copies = []
+    for i in range(3):
+        for j, (source, place) in enumerate(((half_ref, core), (sibling_ref, 1 - core))):
+            copies.append(
+                pltpu.make_async_copy(source.at[:, i], outs[i].at[place], done.at[2 * i + j])
+            )
+    for copy in copies:
+        copy.start()
+    for copy in copies:
+        copy.wait()
+
+
+def assemble(core, half, sibling):
+    in_vmem = pl.BlockSpec(memory_space=pltpu.VMEM)
+    outs = pl.pallas_call(
+        assemble_kernel,
+        out_shape=[jax.ShapeDtypeStruct((2, 16, 8, 512), jnp.float32)] * 3,
+        in_specs=[pl.BlockSpec(memory_space=pltpu.SMEM), in_vmem, in_vmem],
+        out_specs=[pl.BlockSpec(memory_space=pl.ANY)] * 3,
+        scratch_shapes=[pltpu.SemaphoreType.DMA((6,))],
+        compiler_params=pltpu.CompilerParams(vmem_limit_bytes=40 * 1024 * 1024),
+    )(core.reshape(1), half, sibling)
+    return tuple(item.reshape(256, 512) for item in outs)
+
+
 def on_device(activations, key_grads, partners, master_weight, first_moment, second_moment):
     mine = lax.axis_index("xh")
     other = 1 - mine
@@ -67,31 +140,22 @@
     def eight(side):
         return jnp.stack(
             [
-                lax.dynamic_slice_in_dim(item, first_row + 8 * side, 8, axis=0)
+                lax.dynamic_slice_in_dim(
+                    item, first_row + 8 * side, 8, axis=0, allow_negative_indices=False
+                )
                 for item in (master_weight, first_moment, second_moment)
             ]
         )
 
-    own_rows = eight(mine)
-    peer_rows = lax.ppermute(eight(other), "xh", SWAP)
-
     scaled = (key_grads.astype(jnp.float32) * KEY_SCALE).astype(jnp.float16)
     cotangents = lax.all_gather(scaled, "z", axis=0, tiled=True)
-    cotangents, got, peer_rows, tokens = lax.optimization_barrier(
-        (cotangents, got, peer_rows, tokens)
+    own_rows, outgoing, cotangents = lax.optimization_barrier(
+        (eight(mine), eight(other), cotangents)
     )
-    kept = pick(tokens, mine, 1)
+    peer_rows = lax.ppermute(outgoing, "xh", SWAP)
     cotangents = (cotangents.astype(jnp.float32) * (1.0 / KEY_SCALE)).astype(jnp.bfloat16)
 
-    def product(features):
-        return lax.dot_general(
-            features.reshape(1792, 256),
-            cotangents,
-            (((0,), (0,)), ((), ())),
-            preferred_element_type=jnp.float32,
-        ).reshape(32, 8, 512)
-
-    partial = jnp.stack(by_block(product(kept), product(got)), axis=1)
+    partial = products(mine, tokens, got.reshape(1792, 256), cotangents)
     pieces = exchange((partial * PARTIAL_SCALE).astype(jnp.float16), PLANE)
     gradient = jnp.sum(pieces.astype(jnp.float32), axis=0) * (1.0 / PARTIAL_SCALE)
 
@@ -102,22 +166,16 @@
     along = lax.all_gather(split_halves(slices), "z", axis=0, tiled=False)
     here = 2 * lax.axis_index("z")
 
+    scales = jnp.array([1.0, 1.0, 1.0 / SECOND_SCALE], jnp.float32).reshape(3, 1, 1)
+
     def wanted(index):
-        place = partners[index]
-        return join_halves(pick(pick(along, place // 2, 0), place % 2, 1))
+        place = pick(partners, index, 0)
+        return join_halves(pick(pick(along, place >> 1, 0), place & 1, 1)) * scales
 
     placed = jnp.stack([wanted(here + i) for i in range(2)]).reshape(1, 2, 3, 8, 512)
     half = exchange(jnp.broadcast_to(placed, (8, 2, 3, 8, 512)).reshape(16, 3, 8, 512), CHIPS)
     sibling = lax.ppermute(half, "c", SWAP)
-    lower = jnp.where(core == 0, half, sibling)
-    upper = jnp.where(core == 0, sibling, half)
-
-    def whole(i):
-        return jnp.concatenate(
-            (lower[:, i].reshape(128, 512), upper[:, i].reshape(128, 512)), axis=0
-        )
-
-    return whole(0), whole(1), whole(2) * (1.0 / SECOND_SCALE)
+    return assemble(core, half, sibling)
 
 
 def solution(mesh):

time: 149 us -> 136 us (0.913)
  local copies, waits for them, and re-layouts: 9.5 us -> 4.56 us
  matrix products: 3.29 us -> 0 us
  between operations: 6.13 us -> 3.41 us
  Pallas kernels: 0 us -> 2.6 us
  waiting for transfers between devices: 7.72 us -> 5.78 us
    all_to_all x1, waiting for transfers between devices: 5.83 us -> 1.49 us  [exchange(): return lax.all_to_all(array, axes, split_axis=0, concat_axis=0, tiled=True)]
    dot_general x2 -> x0, matrix products: 3.29 us -> none  [product(): lax.dot_general(features.reshape(1792, 256), cotangents, (((0,), (0,)), (...]
    ppermute x1, starting transfers between devices: 1.92 us -> 4.79 us  [on_device(): peer_rows = lax.ppermute(outgoing, 'xh', SWAP)]
    dot_general x2 -> x0, local copies, waits for them, and re-layouts: 2.83 us -> none  [product(): lax.dot_general(features.reshape(1792, 256), cotangents, (((0,), (0,)), (...]
    pallas_call x0 -> x2, Pallas kernels: none -> 2.6 us  [the longest x1 1.42 us: products(): pl.pallas_call(products_kernel, out_shape=jax.ShapeDtypeStruct((32, 2, 8,...]
    ppermute x1, waiting for transfers between devices: 0.01 us -> 2.39 us  [on_device(): peer_rows = lax.ppermute(outgoing, 'xh', SWAP)]
    all_to_all x1, starting transfers between devices: 14.4 us -> 12.3 us  [exchange(): return lax.all_to_all(array, axes, split_axis=0, concat_axis=0, tiled=True)]
    all_gather x1, blocking collectives: 43.7 us -> 41.7 us  [on_device(): cotangents = lax.all_gather(scaled, 'z', axis=0, tiled=True)]
  transfers between devices with their start and end apart: 4 -> 4, of which waited for: 2 -> 3; matrix products, arithmetic and copies ran while one was open for 1% -> 2% of each run, Pallas kernels for 0% -> 0%
where the time goes in v5:
time: 136 us
  blocking collectives  86.4 us (64%)
  starting transfers between devices  31.3 us (23%)
  waiting for transfers between devices  5.78 us (4%)
  local copies, waits for them, and re-layouts  4.56 us (3%)
  between operations  3.41 us (3%)
  Pallas kernels  2.6 us (2%)
  other arithmetic  1.75 us (1%)
    all_gather x1, blocking collectives, on_device(): cotangents = lax.all_gather(scaled, 'z', axis=0, tiled=True)  41.7 us
    all_gather x1, blocking collectives, on_device(): along = lax.all_gather(split_halves(slices), 'z', axis=0, tiled=False)  31.1 us
    all_to_all x1, blocking collectives, exchange(): return lax.all_to_all(array, axes, split_axis=0, concat_axis=0, tiled=True)  13.6 us
    all_to_all x1, starting transfers between devices, exchange(): return lax.all_to_all(array, axes, split_axis=0, concat_axis=0, tiled=True)  12.3 us
    ppermute x1, starting transfers between devices, on_device(): sibling = lax.ppermute(half, 'c', SWAP)  8.73 us
    ppermute x1, starting transfers between devices, on_device(): got = lax.ppermute(pick(tokens, other, 1), 'xh', SWAP)  5.48 us
    ppermute x1, starting transfers between devices, on_device(): peer_rows = lax.ppermute(outgoing, 'xh', SWAP)  4.79 us
  transfers between devices with their start and end apart: 4, of which 3 were waited for; matrix products, arithmetic and copies ran while one was open for 2% of the time, Pallas kernels for 0%

profile of v5, /device:TPU:1, one launch (start us, length us, event | category | flops | bytes accessed | tf_op | source)
XLA Modules:
  0.0 135.7 jit_solution(818365528875505474)
XLA Ops:
  0.6 0.0 copy-start.1
  0.6 1.3 dynamic-slice_bitcast_fusion
  1.9 5.5 %collective-permute-start.1 = (bf16[16,112,256]{2,1,0:T(8,128)(2,1)S(1)}, bf16[16,112,256]{2,1,0:T(8,128)(2,1)S(1)}, u32[]{:S(2)}, u32[]{:S(2)}) collective-permute-start(bf16[16,112,256]{2,1,0:T(8,128)(2,1)S(1)} %dynamic-slice_bitcast_fusion), channel_id=1, source_target_pairs={{0,1},{1,0},{2,3},{3,2},{4,5},{5,4},{6,7},{7,6},{8,9},{9,8},{10,11... | collective-permute-start | bytes 2752520 | tf_op jit(solution)/shard_map/ppermute | solution.py:136
  7.4 0.0 copy-done.1
  7.5 41.7 %all-gather.3 = f16[1792,512]{1,0:T(8,128)(2,1)S(1)} all-gather(f16[112,512]{1,0:T(8,128)(2,1)S(1)} %multiply_convert_fusion.2), channel_id=1, replica_groups=mesh['xl'=2,'y'=4,'c'=2,'z'=16,'xh'=2] {'z'}, dimensions={0}, use_global_device_ids=true | all-gather | bytes 1949696 | tf_op jit(solution)/shard_map/all_gather | solution.py:151
  49.2 0.7 dynamic-slice_bitcast_fusion.3
  49.9 0.8 dynamic-slice_bitcast_fusion.1
  50.7 0.0 copy-start
  50.8 0.4 multiply_convert_fusion.cotangents_ref
  51.2 0.0 collective-permute-done.1
  51.2 1.0 copy-done
  52.2 1.4 %shard_map.94 = f32[32,2,8,512]{3,2,1,0:T(8,128)S(1)} custom-call(s32[1]{0:T(128)} %bitcast.12.mine_ref, bf16[16,2,112,256]{3,2,1,0:T(8,128)(2,1)S(1)} %bitcast.78, bf16[1792,256]{1,0:T(8,128)(2,1)S(1)} %bitcast.79, bf16[1792,512]{1,0:T(8,128)(2,1)S(1)} %multiply_convert_fusion.cotangents_ref), custom_call_target="tpu_custom_call" | custom-call | flops 939524096 | bytes 6291456 | tf_op jit(solution)/shard_map/pallas_call | solution.py:77
  53.7 0.0 copy-start.2
  53.7 0.9 multiply_convert_fusion.1
  54.6 12.3 %all-to-all-start = ((f16[32,2,8,512]{3,2,1,0:T(8,128)(2,1)}), f16[32,2,8,512]{3,2,1,0:T(8,128)(2,1)S(1)}, u32[]{:S(2)}, u32[]{:S(2)}) async-start(f16[32,2,8,512]{3,2,1,0:T(8,128)(2,1)} %multiply_convert_fusion.1), calls=%async_computation | async-start | bytes 1048576 | tf_op jit(solution)/shard_map/all_to_all | solution.py:29
  66.9 0.0 copy-start.3
  66.9 4.8 %collective-permute-start = (f32[3,8,512]{2,1,0:T(8,128)S(1)}, f32[3,8,512]{2,1,0:T(8,128)S(1)}, u32[]{:S(2)}, u32[]{:S(2)}) collective-permute-start(f32[3,8,512]{2,1,0:T(8,128)S(1)} %pad_maximum_fusion.4), channel_id=1, source_target_pairs={{0,1},{1,0},{2,3},{3,2},{4,5},{5,4},{6,7},{7,6},{8,9},{9,8},{10,11... | collective-permute-start | bytes 147464 | tf_op jit(solution)/shard_map/ppermute | solution.py:155
  71.7 0.0 copy-done.2
  71.7 0.6 fusion.19
  74.9 2.4 %collective-permute-done = f32[3,8,512]{2,1,0:T(8,128)S(1)} collective-permute-done((f32[3,8,512]{2,1,0:T(8,128)S(1)}, f32[3,8,512]{2,1,0:T(8,128)S(1)}, u32[]{:S(2)}, u32[]{:S(2)}) %collective-permute-start) | collective-permute-done | bytes 49184 | tf_op jit(solution)/shard_map/ppermute | solution.py:155
  77.3 1.5 %all-to-all-done = f16[32,2,8,512]{3,2,1,0:T(8,128)(2,1)S(1)} async-done(((f16[32,2,8,512]{3,2,1,0:T(8,128)(2,1)}), f16[32,2,8,512]{3,2,1,0:T(8,128)(2,1)S(1)}, u32[]{:S(2)}, u32[]{:S(2)}) %all-to-all-start) | async-done | bytes 524320 | tf_op jit(solution)/shard_map/all_to_all | solution.py:29
  78.8 0.1 convert_reduce_fusion
  78.9 0.1 reduce-precision_convert_fusion
  79.1 31.1 %all-gather.4 = f16[32,2,3,8,512]{4,3,2,1,0:T(8,128)(2,1)S(1)} all-gather(f16[2,2,3,8,512]{4,3,2,1,0:T(8,128)(2,1)S(1)} %pad_maximum_fusion.1), channel_id=2, replica_groups=mesh['xl'=2,'y'=4,'c'=2,'z'=16,'xh'=2] {'z'}, dimensions={0}, use_global_device_ids=true | all-gather | bytes 1671168 | tf_op jit(solution)/shard_map/all_gather | solution.py:166
  110.1 0.0 copy-done.3
  110.1 0.1 fusion.7
  110.2 0.1 broadcast_in_dim.2
  110.3 13.6 %all_to_all.10.half_ref = f32[16,3,8,512]{3,2,1,0:T(8,128)S(1)} all-to-all(f32[16,3,8,512]{3,2,1,0:T(8,128)S(1)} %bitcast.80), channel_id=1, replica_groups=mesh['xl'=2,'y'=4,'c'=2,'z'=16,'xh'=2] {'xl','y','xh'}, dimensions={0} | all-to-all | bytes 1572864 | tf_op jit(solution)/shard_map/all_to_all | solution.py:29
  123.9 8.7 %collective-permute-start.2 = (f32[16,3,8,512]{3,2,1,0:T(8,128)S(1)}, f32[16,3,8,512]{3,2,1,0:T(8,128)S(1)}, u32[]{:S(2)}, u32[]{:S(2)}) collective-permute-start(f32[16,3,8,512]{3,2,1,0:T(8,128)S(1)} %all_to_all.10.half_ref), channel_id=1, source_target_pairs={{0,32},{32,0},{1,33},{33,1},{2,34},{34,2},{3,35},{35,3},{4,36},{36... | collective-permute-start | bytes 2359304 | tf_op jit(solution)/shard_map/ppermute | solution.py:177
  132.7 1.9 %collective-permute-done.2.sibling_ref = f32[16,3,8,512]{3,2,1,0:T(8,128)S(1)} collective-permute-done((f32[16,3,8,512]{3,2,1,0:T(8,128)S(1)}, f32[16,3,8,512]{3,2,1,0:T(8,128)S(1)}, u32[]{:S(2)}, u32[]{:S(2)}) %collective-permute-start.2) | collective-permute-done | bytes 786464 | tf_op jit(solution)/shard_map/ppermute | solution.py:177
  134.5 1.2 shard_map.95
  (9 shorter events, 0.1 us)
Async XLA Ops:
  0.6 6.8 %copy-start.1 = (bf16[112,512]{1,0:T(8,128)(2,1)S(1)}, bf16[112,512]{1,0:T(8,128)(2,1)}, u32[]{:S(2)}) copy-start(bf16[112,512]{1,0:T(8,128)(2,1)} %param.8) | copy-start | bytes 344068
  1.9 49.3 %collective-permute-start.1 = (bf16[16,112,256]{2,1,0:T(8,128)(2,1)S(1)}, bf16[16,112,256]{2,1,0:T(8,128)(2,1)S(1)}, u32[]{:S(2)}, u32[]{:S(2)}) collective-permute-start(bf16[16,112,256]{2,1,0:T(8,128)(2,1)S(1)} %dynamic-slice_bitcast_fusion), channel_id=1, source_target_pairs={{0,1},{1,0},{2,3},{3,2},{4,5},{5,4},{6,7},{7,6},{8,9},{9,8},{10,11... | collective-permute-start | bytes 2752520 | tf_op jit(solution)/shard_map/ppermute | solution.py:136
  50.7 1.5 %copy-start = (bf16[3584,256]{1,0:T(8,128)(2,1)S(1)}, bf16[3584,256]{1,0:T(8,128)(2,1)}, u32[]{:S(2)}) copy-start(bf16[3584,256]{1,0:T(8,128)(2,1)} %param.7) | copy-start | bytes 5505028
  53.7 18.0 %copy-start.2 = (s32[32]{0:T(128)S(1)}, s32[32]{0:T(128)}, u32[]{:S(2)}) copy-start(s32[32]{0:T(128)} %param.9) | copy-start | bytes 388
  54.6 24.2 %all-to-all-start = ((f16[32,2,8,512]{3,2,1,0:T(8,128)(2,1)}), f16[32,2,8,512]{3,2,1,0:T(8,128)(2,1)S(1)}, u32[]{:S(2)}, u32[]{:S(2)}) async-start(f16[32,2,8,512]{3,2,1,0:T(8,128)(2,1)} %multiply_convert_fusion.1), calls=%async_computation | async-start | bytes 1048576 | tf_op jit(solution)/shard_map/all_to_all | solution.py:29
  66.9 43.3 %copy-start.3 = (f32[3]{0:T(128)S(1)}, f32[3]{0:T(128)}, u32[]{:S(2)}) copy-start(f32[3]{0:T(128)} %constant.154.clone) | copy-start | bytes 40
  66.9 10.4 %collective-permute-start = (f32[3,8,512]{2,1,0:T(8,128)S(1)}, f32[3,8,512]{2,1,0:T(8,128)S(1)}, u32[]{:S(2)}, u32[]{:S(2)}) collective-permute-start(f32[3,8,512]{2,1,0:T(8,128)S(1)} %pad_maximum_fusion.4), channel_id=1, source_target_pairs={{0,1},{1,0},{2,3},{3,2},{4,5},{5,4},{6,7},{7,6},{8,9},{9,8},{10,11... | collective-permute-start | bytes 147464 | tf_op jit(solution)/shard_map/ppermute | solution.py:155
  123.9 10.6 %collective-permute-start.2 = (f32[16,3,8,512]{3,2,1,0:T(8,128)S(1)}, f32[16,3,8,512]{3,2,1,0:T(8,128)S(1)}, u32[]{:S(2)}, u32[]{:S(2)}) collective-permute-start(f32[16,3,8,512]{3,2,1,0:T(8,128)S(1)} %all_to_all.10.half_ref), channel_id=1, source_target_pairs={{0,32},{32,0},{1,33},{33,1},{2,34},{34,2},{3,35},{35,3},{4,36},{36... | collective-permute-start | bytes 2359304 | tf_op jit(solution)/shard_map/ppermute | solution.py:177

commit v6 on v5

--- a/solution.py
+++ b/solution.py
@@ -38,7 +38,7 @@
 def split_halves(values):
     high = lax.reduce_precision(values, exponent_bits=5, mantissa_bits=10)
     rest = (values - high) * REST_SCALE
-    return jnp.stack((high.astype(jnp.float16), rest.astype(jnp.float16)))
+    return jnp.stack((high.astype(jnp.float16), rest.astype(jnp.float16)), axis=1)
 
 
 def join_halves(halves):
@@ -54,7 +54,57 @@
     return (new_weight, new_first, new_second)
 
 
-def products_kernel(mine_ref, tokens_ref, got_ref, cotangents_ref, out_ref, kept, arrived):
+def message_kernel(
+    where_ref, tokens_ref, weight_ref, one_ref, two_ref, out_ref, rows, tail, sent, read, last
+):
+    other, row = where_ref[0], pl.multiple_of(where_ref[1], 8)
+    copies = [pltpu.make_async_copy(tokens_ref.at[:, other], out_ref.at[pl.ds(0, 16)], sent)]
+    for i, state_ref in enumerate((weight_ref, one_ref, two_ref)):
+        copies.append(
+            pltpu.make_async_copy(state_ref.at[pl.ds(row, 8)], rows.at[i], read.at[i])
+        )
+    for copy in copies:
+        copy.start()
+    for copy in copies[1:]:
+        copy.wait()
+    values = rows[...].reshape(24, 512)
+    values = jnp.concatenate((values[:, :256], values[:, 256:]), axis=0)
+    first = values.astype(jnp.bfloat16)
+    values = values - first.astype(jnp.float32)
+    second = values.astype(jnp.bfloat16)
+    third = (values - second.astype(jnp.float32)).astype(jnp.bfloat16)
+    tail[0, 0:48] = first
+    tail[0, 48:96] = second
+    tail[0, 96:112] = jnp.zeros((16, 256), jnp.bfloat16)
+    tail[1, 0:48] = third
+    tail[1, 48:112] = jnp.zeros((64, 256), jnp.bfloat16)
+    end = pltpu.make_async_copy(tail, out_ref.at[pl.ds(16, 2)], last)
+    end.start()
+    copies[0].wait()
+    end.wait()
+
+
+def message(other, row, tokens, states):
+    return pl.pallas_call(
+        message_kernel,
+        out_shape=jax.ShapeDtypeStruct((18, 112, 256), jnp.bfloat16),
+        in_specs=[pl.BlockSpec(memory_space=pltpu.SMEM)]
+        + [pl.BlockSpec(memory_space=pltpu.HBM)] * 4,
+        out_specs=pl.BlockSpec(memory_space=pltpu.HBM),
+        scratch_shapes=[
+            pltpu.VMEM((3, 8, 512), jnp.float32),
+            pltpu.VMEM((2, 112, 256), jnp.bfloat16),
+            pltpu.SemaphoreType.DMA,
+            pltpu.SemaphoreType.DMA((3,)),
+            pltpu.SemaphoreType.DMA,
+        ],
+        compiler_params=pltpu.CompilerParams(vmem_limit_bytes=60 * 1024 * 1024),
+    )(jnp.stack((other, row)), tokens, *states)
+
+
+def products_kernel(
+    mine_ref, tokens_ref, got_ref, cotangents_ref, out_ref, rows_ref, kept, arrived
+):
     mine = mine_ref[0]
     fetch = pltpu.make_async_copy(tokens_ref.at[:, mine], kept, arrived)
     fetch.start()
@@ -67,7 +117,11 @@
             preferred_element_type=jnp.float32,
         ).reshape(32, 8, 512)
 
-    out_ref[:, 1 - mine] = product(got_ref[...])
+    out_ref[:, 1 - mine] = product(got_ref[0:16].reshape(1792, 256))
+    rows = (
+        got_ref[16, 0:48].astype(jnp.float32) + got_ref[16, 48:96].astype(jnp.float32)
+    ) + got_ref[17, 0:48].astype(jnp.float32)
+    rows_ref[...] = jnp.concatenate((rows[:24], rows[24:]), axis=1).reshape(3, 8, 512)
     fetch.wait()
     out_ref[:, mine] = product(kept[...].reshape(1792, 256))
 
@@ -76,14 +130,17 @@
     in_vmem = pl.BlockSpec(memory_space=pltpu.VMEM)
     return pl.pallas_call(
         products_kernel,
-        out_shape=jax.ShapeDtypeStruct((32, 2, 8, 512), jnp.float32),
+        out_shape=[
+            jax.ShapeDtypeStruct((32, 2, 8, 512), jnp.float32),
+            jax.ShapeDtypeStruct((3, 8, 512), jnp.float32),
+        ],
         in_specs=[
             pl.BlockSpec(memory_space=pltpu.SMEM),
-            pl.BlockSpec(memory_space=pl.ANY),
+            pl.BlockSpec(memory_space=pltpu.HBM),
             in_vmem,
             in_vmem,
         ],
-        out_specs=in_vmem,
+        out_specs=[in_vmem, in_vmem],
         scratch_shapes=[
             pltpu.VMEM((16, 112, 256), jnp.bfloat16),
             pltpu.SemaphoreType.DMA,
@@ -116,7 +173,7 @@
         assemble_kernel,
         out_shape=[jax.ShapeDtypeStruct((2, 16, 8, 512), jnp.float32)] * 3,
         in_specs=[pl.BlockSpec(memory_space=pltpu.SMEM), in_vmem, in_vmem],
-        out_specs=[pl.BlockSpec(memory_space=pl.ANY)] * 3,
+        out_specs=[pl.BlockSpec(memory_space=pltpu.HBM)] * 3,
         scratch_shapes=[pltpu.SemaphoreType.DMA((6,))],
         compiler_params=pltpu.CompilerParams(vmem_limit_bytes=40 * 1024 * 1024),
     )(core.reshape(1), half, sibling)
@@ -132,30 +189,25 @@
     def by_block(own, peer):
         return jnp.where(mine == 0, own, peer), jnp.where(mine == 0, peer, own)
 
+    states = (master_weight, first_moment, second_moment)
+    first_row = 128 * core + 16 * column
     tokens = activations.reshape(16, 2, 112, 256)
-    got = lax.ppermute(pick(tokens, other, 1), "xh", SWAP)
-
-    first_row = 128 * core + 16 * column
-
-    def eight(side):
-        return jnp.stack(
-            [
-                lax.dynamic_slice_in_dim(
-                    item, first_row + 8 * side, 8, axis=0, allow_negative_indices=False
-                )
-                for item in (master_weight, first_moment, second_moment)
-            ]
-        )
+    got = lax.ppermute(message(other, first_row + 8 * other, tokens, states), "xh", SWAP)
 
     scaled = (key_grads.astype(jnp.float32) * KEY_SCALE).astype(jnp.float16)
     cotangents = lax.all_gather(scaled, "z", axis=0, tiled=True)
-    own_rows, outgoing, cotangents = lax.optimization_barrier(
-        (eight(mine), eight(other), cotangents)
+    cotangents = (cotangents.astype(jnp.float32) * (1.0 / KEY_SCALE)).astype(jnp.bfloat16)
+
+    partial, peer_rows = products(mine, tokens, got, cotangents)
+    states, partial = lax.optimization_barrier((states, partial))
+    own_rows = jnp.stack(
+        [
+            lax.dynamic_slice_in_dim(
+                item, first_row + 8 * mine, 8, axis=0, allow_negative_indices=False
+            )
+            for item in states
+        ]
     )
-    peer_rows = lax.ppermute(outgoing, "xh", SWAP)
-    cotangents = (cotangents.astype(jnp.float32) * (1.0 / KEY_SCALE)).astype(jnp.bfloat16)
-
-    partial = products(mine, tokens, got.reshape(1792, 256), cotangents)
     pieces = exchange((partial * PARTIAL_SCALE).astype(jnp.float16), PLANE)
     gradient = jnp.sum(pieces.astype(jnp.float32), axis=0) * (1.0 / PARTIAL_SCALE)
 
@@ -163,14 +215,14 @@
     weight, moment_one, moment_two = adam_update(old[0], old[1], old[2], gradient)
 
     slices = jnp.stack((weight, moment_one, moment_two * SECOND_SCALE), axis=1)
-    along = lax.all_gather(split_halves(slices), "z", axis=0, tiled=False)
+    along = lax.all_gather(split_halves(slices).reshape(2, 48, 512), "z", axis=0)
+    along = along.reshape(32, 2, 3, 8, 512)
     here = 2 * lax.axis_index("z")
 
-    scales = jnp.array([1.0, 1.0, 1.0 / SECOND_SCALE], jnp.float32).reshape(3, 1, 1)
+    scales = jnp.where(jnp.arange(3) == 2, 1.0 / SECOND_SCALE, 1.0).reshape(3, 1, 1)
 
     def wanted(index):
-        place = pick(partners, index, 0)
-        return join_halves(pick(pick(along, place >> 1, 0), place & 1, 1)) * scales
+        return join_halves(pick(along, pick(partners, index, 0), 0)) * scales
 
     placed = jnp.stack([wanted(here + i) for i in range(2)]).reshape(1, 2, 3, 8, 512)
     half = exchange(jnp.broadcast_to(placed, (8, 2, 3, 8, 512)).reshape(16, 3, 8, 512), CHIPS)

time: 136 us -> 165 us (1.21)
  Pallas kernels: 2.6 us -> 32.3 us
  waiting for transfers between devices: 5.78 us -> 11.5 us
  starting transfers between devices: 31.3 us -> 26.7 us
  between operations: 3.41 us -> 0.81 us
  other arithmetic: 1.75 us -> 3.63 us
    pallas_call x1 -> x2, Pallas kernels: 1.42 us -> 31.1 us  [the longest x1 29.7 us: message(): pl.pallas_call(message_kernel, out_shape=jax.ShapeDtypeStruct((18, 112, 2...]
    all_to_all x1, waiting for transfers between devices: 1.49 us -> 9.6 us  [exchange(): return lax.all_to_all(array, axes, split_axis=0, concat_axis=0, tiled=True)]
    ppermute x2 -> x1, starting transfers between devices: 10.3 us -> 5.48 us  [on_device(): lax.ppermute(message(other, first_row + 8 * other, tokens, states), 'xh',...]
    ppermute x2 -> x1, waiting for transfers between devices: 2.4 us -> 0.01 us  [on_device(): lax.ppermute(message(other, first_row + 8 * other, tokens, states), 'xh',...]
  transfers between devices with their start and end apart: 4 -> 3, of which waited for: 3 -> 2; matrix products, arithmetic and copies ran while one was open for 2% -> 2% of each run, Pallas kernels for 0% -> 0%
where the time goes in v6:
time: 165 us; the launch traced here: 164 us
  blocking collectives  85.8 us (52%)
  Pallas kernels  32.3 us (20%)
  starting transfers between devices  26.7 us (16%)
  waiting for transfers between devices  11.5 us (7%)
  other arithmetic  3.63 us (2%)
  local copies, waits for them, and re-layouts  3.2 us (2%)
    all_gather x1, blocking collectives, on_device(): cotangents = lax.all_gather(scaled, 'z', axis=0, tiled=True)  41.7 us
    all_gather x1, blocking collectives, on_device(): lax.all_gather(split_halves(slices).reshape(2, 48, 512), 'z', axis=0)  31.1 us
    pallas_call x1, Pallas kernels, message(): pl.pallas_call(message_kernel, out_shape=jax.ShapeDtypeStruct((18, 112, 2...  29.7 us
    all_to_all x1, blocking collectives, exchange(): return lax.all_to_all(array, axes, split_axis=0, concat_axis=0, tiled=True)  12.9 us
    all_to_all x1, starting transfers between devices, exchange(): return lax.all_to_all(array, axes, split_axis=0, concat_axis=0, tiled=True)  12.3 us
    all_to_all x1, waiting for transfers between devices, exchange(): return lax.all_to_all(array, axes, split_axis=0, concat_axis=0, tiled=True)  9.6 us
    ppermute x1, starting transfers between devices, on_device(): sibling = lax.ppermute(half, 'c', SWAP)  8.94 us
    ppermute x1, starting transfers between devices, on_device(): lax.ppermute(message(other, first_row + 8 * other, tokens, states), 'xh',...  5.48 us
  transfers between devices with their start and end apart: 3, of which 2 were waited for; matrix products, arithmetic and copies ran while one was open for 2% of the time, Pallas kernels for 0%

profile of v6, /device:TPU:1, one launch (start us, length us, event | category | flops | bytes accessed | tf_op | source)
XLA Modules:
  0.0 163.9 jit_solution(7555398153400950059)
XLA Ops:
  0.6 0.6 pad_add_fusion.where_ref
  1.2 0.0 copy-start.1
  1.2 29.7 %shard_map.85 = bf16[18,112,256]{2,1,0:T(8,128)(2,1)} custom-call(s32[2]{0:T(128)} %pad_add_fusion.where_ref, bf16[16,2,112,256]{3,2,1,0:T(8,128)(2,1)} %bitcast.77, f32[256,512]{1,0:T(8,128)} %weight_ref.1, f32[256,512]{1,0:T(8,128)} %one_ref.1, f32[256,512]{1,0:T(8,128)} %two_ref.1), custom_call_target="tpu_custom_call" | custom-call | tf_op jit(solution)/shard_map/pallas_call | solution.py:88
  31.0 5.5 %collective-permute-start = (bf16[18,112,256]{2,1,0:T(8,128)(2,1)}, bf16[18,112,256]{2,1,0:T(8,128)(2,1)S(1)}, u32[]{:S(2)}, u32[]{:S(2)}) collective-permute-start(bf16[18,112,256]{2,1,0:T(8,128)(2,1)} %shard_map.85), channel_id=1, source_target_pairs={{0,1},{1,0},{2,3},{3,2},{4,5},{5,4},{6,7},{7,6},{8,9},{9,8},{10,11... | collective-permute-start | bytes 3096584 | tf_op jit(solution)/shard_map/ppermute | solution.py:195
  36.5 0.0 copy-done.1
  36.5 41.7 %all-gather.2 = f16[1792,512]{1,0:T(8,128)(2,1)S(1)} all-gather(f16[112,512]{1,0:T(8,128)(2,1)S(1)} %multiply_convert_fusion.2), channel_id=1, replica_groups=mesh['xl'=2,'y'=4,'c'=2,'z'=16,'xh'=2] {'z'}, dimensions={0}, use_global_device_ids=true | all-gather | bytes 1949696 | tf_op jit(solution)/shard_map/all_gather | solution.py:198
  78.2 0.0 copy-start
  78.2 0.4 multiply_convert_fusion.cotangents_ref
  78.7 0.0 collective-permute-done.got_ref
  78.7 1.0 copy-done
  79.7 1.4 shard_map.86
  81.2 0.0 copy-start.2
  81.2 0.9 multiply_convert_fusion.1
  82.1 12.3 %all-to-all-start = ((f16[32,2,8,512]{3,2,1,0:T(8,128)(2,1)}), f16[32,2,8,512]{3,2,1,0:T(8,128)(2,1)S(1)}, u32[]{:S(2)}, u32[]{:S(2)}) async-start(f16[32,2,8,512]{3,2,1,0:T(8,128)(2,1)} %multiply_convert_fusion.1), calls=%async_computation | async-start | bytes 1048576 | tf_op jit(solution)/shard_map/all_to_all | solution.py:29
  94.4 0.0 copy-done.2
  94.4 0.6 fusion.20
  95.0 0.7 dynamic-slice_bitcast_fusion.2
  95.7 0.7 dynamic-slice_bitcast_fusion
  96.5 9.6 %all-to-all-done = f16[32,2,8,512]{3,2,1,0:T(8,128)(2,1)S(1)} async-done(((f16[32,2,8,512]{3,2,1,0:T(8,128)(2,1)}), f16[32,2,8,512]{3,2,1,0:T(8,128)(2,1)S(1)}, u32[]{:S(2)}, u32[]{:S(2)}) %all-to-all-start) | async-done | bytes 524320 | tf_op jit(solution)/shard_map/all_to_all | solution.py:29
  106.1 0.1 convert_reduce_fusion
  106.2 0.1 reduce-precision_convert_fusion
  106.4 31.1 %all-gather.3 = f16[16,2,48,512]{3,2,1,0:T(8,128)(2,1)S(1)} all-gather(f16[1,2,48,512]{3,2,1,0:T(8,128)(2,1)S(1)} %bitcast.81), channel_id=1, replica_groups=mesh['xl'=2,'y'=4,'c'=2,'z'=16,'xh'=2] {'z'}, dimensions={0}, use_global_device_ids=true | all-gather | bytes 1671168 | tf_op jit(solution)/shard_map/all_gather | solution.py:218
  137.5 1.3 dynamic-slice_convert_fusion.1
  138.8 0.1 fusion.7
  138.9 0.1 broadcast_in_dim.15
  139.0 12.9 %all_to_all.10.half_ref = f32[16,3,8,512]{3,2,1,0:T(8,128)S(1)} all-to-all(f32[16,3,8,512]{3,2,1,0:T(8,128)S(1)} %bitcast.79), channel_id=1, replica_groups=mesh['xl'=2,'y'=4,'c'=2,'z'=16,'xh'=2] {'xl','y','xh'}, dimensions={0} | all-to-all | bytes 1572864 | tf_op jit(solution)/shard_map/all_to_all | solution.py:29
  151.9 8.9 %collective-permute-start.1 = (f32[16,3,8,512]{3,2,1,0:T(8,128)S(1)}, f32[16,3,8,512]{3,2,1,0:T(8,128)S(1)}, u32[]{:S(2)}, u32[]{:S(2)}) collective-permute-start(f32[16,3,8,512]{3,2,1,0:T(8,128)S(1)} %all_to_all.10.half_ref), channel_id=1, source_target_pairs={{0,32},{32,0},{1,33},{33,1},{2,34},{34,2},{3,35},{35,3},{4,36},{36... | collective-permute-start | bytes 2359304 | tf_op jit(solution)/shard_map/ppermute | solution.py:229
  160.8 1.9 %collective-permute-done.1.sibling_ref = f32[16,3,8,512]{3,2,1,0:T(8,128)S(1)} collective-permute-done((f32[16,3,8,512]{3,2,1,0:T(8,128)S(1)}, f32[16,3,8,512]{3,2,1,0:T(8,128)S(1)}, u32[]{:S(2)}, u32[]{:S(2)}) %collective-permute-start.1) | collective-permute-done | bytes 786464 | tf_op jit(solution)/shard_map/ppermute | solution.py:229
  162.7 1.2 shard_map.87
  (8 shorter events, 0.1 us)
Async XLA Ops:
  1.2 35.2 %copy-start.1 = (bf16[112,512]{1,0:T(8,128)(2,1)S(1)}, bf16[112,512]{1,0:T(8,128)(2,1)}, u32[]{:S(2)}) copy-start(bf16[112,512]{1,0:T(8,128)(2,1)} %param.7) | copy-start | bytes 344068
  31.0 47.7 %collective-permute-start = (bf16[18,112,256]{2,1,0:T(8,128)(2,1)}, bf16[18,112,256]{2,1,0:T(8,128)(2,1)S(1)}, u32[]{:S(2)}, u32[]{:S(2)}) collective-permute-start(bf16[18,112,256]{2,1,0:T(8,128)(2,1)} %shard_map.85), channel_id=1, source_target_pairs={{0,1},{1,0},{2,3},{3,2},{4,5},{5,4},{6,7},{7,6},{8,9},{9,8},{10,11... | collective-permute-start | bytes 3096584 | tf_op jit(solution)/shard_map/ppermute | solution.py:195
  78.2 1.5 copy-start
  81.2 13.3 %copy-start.2 = (s32[32]{0:T(128)S(1)}, s32[32]{0:T(128)}, u32[]{:S(2)}) copy-start(s32[32]{0:T(128)} %param.8) | copy-start | bytes 388
  82.1 24.0 %all-to-all-start = ((f16[32,2,8,512]{3,2,1,0:T(8,128)(2,1)}), f16[32,2,8,512]{3,2,1,0:T(8,128)(2,1)S(1)}, u32[]{:S(2)}, u32[]{:S(2)}) async-start(f16[32,2,8,512]{3,2,1,0:T(8,128)(2,1)} %multiply_convert_fusion.1), calls=%async_computation | async-start | bytes 1048576 | tf_op jit(solution)/shard_map/all_to_all | solution.py:29
  151.9 10.8 %collective-permute-start.1 = (f32[16,3,8,512]{3,2,1,0:T(8,128)S(1)}, f32[16,3,8,512]{3,2,1,0:T(8,128)S(1)}, u32[]{:S(2)}, u32[]{:S(2)}) collective-permute-start(f32[16,3,8,512]{3,2,1,0:T(8,128)S(1)} %all_to_all.10.half_ref), channel_id=1, source_target_pairs={{0,32},{32,0},{1,33},{33,1},{2,34},{34,2},{3,35},{35,3},{4,36},{36... | collective-permute-start | bytes 2359304 | tf_op jit(solution)/shard_map/ppermute | solution.py:229

commit v7 on v5

v7 whole, which is shorter than its diff:
```python
import jax
import jax.numpy as jnp
from jax import lax
from jax.experimental import pallas as pl
from jax.experimental.pallas import tpu as pltpu
from jax.sharding import Mesh
from jax.sharding import PartitionSpec as P

beta_first = 0.9
beta_second = 0.95
learn_rate = 0.01
weight_decay = 0.1
correct_first = 1.0 - 0.9**10
correct_second = 1.0 - 0.95**10

PARTS = (("xl", 2), ("y", 4), ("c", 2), ("z", 16), ("xh", 2))
DP = ("xl", "y", "c")
FSDP = ("z", "xh")
CHIPS = ("xl", "y", "xh")
SWAP = [(0, 1), (1, 0)]
KEY_SCALE = 2.0**21
REST_SCALE = 2.0**11
SECOND_SCALE = 2.0**-6
PARTIAL_SCALE = 2.0**6


def exchange(array, axes):
    return lax.all_to_all(array, axes, split_axis=0, concat_axis=0, tiled=True)


def pick(array, index, axis):
    return lax.dynamic_index_in_dim(
        array, index, axis=axis, keepdims=False, allow_negative_indices=False
    )


def split_halves(values):
    high = lax.reduce_precision(values, exponent_bits=5, mantissa_bits=10)
    rest = (values - high) * REST_SCALE
    return jnp.stack((high.astype(jnp.float16), rest.astype(jnp.float16)), axis=1)


def join_halves(halves):
    wide = halves.astype(jnp.float32)
    return wide[0] + wide[1] * (1.0 / REST_SCALE)


def adam_update(weight, first_moment, second_moment, gradient):
    new_first = beta_first * first_moment + (1.0 - beta_first) * gradient
    new_second = beta_second * second_moment + (1.0 - beta_second) * gradient * gradient
    step_size = new_first / correct_first / (jnp.sqrt(new_second / correct_second) + 1e-08)
    new_weight = weight - learn_rate * (step_size + weight_decay * weight)
    return (new_weight, new_first, new_second)


def products_kernel(where_ref, tokens_ref, got_ref, cotangents_ref, out_ref, kept, arrived):
    mine = where_ref[0]
    features = pl.ds(pl.multiple_of(128 * where_ref[1], 128), 128)
    fetch = pltpu.make_async_copy(tokens_ref.at[:, mine, :, features], kept, arrived)
    fetch.start()

    def product(block):
        return lax.dot_general(
            block,
            cotangents_ref[...],
            (((0,), (0,)), ((), ())),
            preferred_element_type=jnp.float32,
        ).reshape(16, 8, 512)

    out_ref[:, 1 - mine] = product(got_ref[:, features])
    fetch.wait()
    out_ref[:, mine] = product(kept[...].reshape(1792, 128))


def products(mine, half, tokens, got, cotangents):
    in_vmem = pl.BlockSpec(memory_space=pltpu.VMEM)
    return pl.pallas_call(
        products_kernel,
        out_shape=jax.ShapeDtypeStruct((16, 2, 8, 512), jnp.float32),
        in_specs=[
            pl.BlockSpec(memory_space=pltpu.SMEM),
            pl.BlockSpec(memory_space=pl.ANY),
            in_vmem,
            in_vmem,
        ],
        out_specs=in_vmem,
        scratch_shapes=[
            pltpu.VMEM((16, 112, 128), jnp.bfloat16),
            pltpu.SemaphoreType.DMA,
        ],
        compiler_params=pltpu.CompilerParams(vmem_limit_bytes=40 * 1024 * 1024),
        cost_estimate=pl.CostEstimate(
            flops=2 * 1792 * 256 * 512, bytes_accessed=4 * 1024 * 1024, transcendentals=0
        ),
    )(jnp.stack((mine, half)), tokens, got, cotangents)


def place_kernel(where_ref, source_ref, *refs):
    outs, done = refs[-4:-1], refs[-1]
    half = where_ref[0]
    copies = [
        pltpu.make_async_copy(source_ref.at[:, i], outs[i].at[half], done.at[i])
        for i in range(3)
    ]
    for copy in copies:
        copy.start()
    for copy in copies:
        copy.wait()


def place(half, source, outs=()):
    return pl.pallas_call(
        place_kernel,
        out_shape=[jax.ShapeDtypeStruct((2, 16, 8, 512), jnp.float32)] * 3,
        in_specs=[
            pl.BlockSpec(memory_space=pltpu.SMEM),
            pl.BlockSpec(memory_space=pltpu.VMEM),
        ]
        + [pl.BlockSpec(memory_space=pltpu.HBM)] * len(outs),
        out_specs=[pl.BlockSpec(memory_space=pltpu.HBM)] * 3,
        input_output_aliases={2 + i: i for i in range(len(outs))},
        scratch_shapes=[pltpu.SemaphoreType.DMA((3,))],
        compiler_params=pltpu.CompilerParams(vmem_limit_bytes=40 * 1024 * 1024),
        cost_estimate=pl.CostEstimate(
            flops=0, bytes_accessed=2 * 1024 * 1024, transcendentals=0
        ),
    )(half.reshape(1), source, *outs)


def on_device(activations, key_grads, partners, master_weight, first_moment, second_moment):
    mine = lax.axis_index("xh")
    other = 1 - mine
    core = lax.axis_index("c")
    column = lax.axis_index(("xl", "y"))

    def by_block(own, peer):
        return jnp.where(mine == 0, own, peer), jnp.where(mine == 0, peer, own)

    tokens = activations.reshape(16, 2, 112, 256)
    got = lax.ppermute(pick(tokens, other, 1), "xh", SWAP)

    first_row = 128 * core + 16 * column

    def eight(side, states):
        return jnp.stack(
            [
                lax.dynamic_slice_in_dim(
                    item, first_row + 8 * side, 8, axis=0, allow_negative_indices=False
                )
                for item in states
            ]
        )

    scaled = (key_grads.astype(jnp.float32) * KEY_SCALE).astype(jnp.float16)
    cotangents = lax.all_gather(scaled, "z", axis=0, tiled=True)
    cotangents = (cotangents.astype(jnp.float32) * (1.0 / KEY_SCALE)).astype(jnp.bfloat16)

    got = got.reshape(1792, 256)
    passed = lax.ppermute(products(mine, 1 - core, tokens, got, cotangents), "c", SWAP)
    partial = passed + products(mine, core, tokens, got, cotangents)
    pieces = exchange((partial * PARTIAL_SCALE).astype(jnp.float16), CHIPS)
    gradient = jnp.sum(pieces.astype(jnp.float32), axis=0) * (1.0 / PARTIAL_SCALE)

    states, partial = lax.optimization_barrier(
        ((master_weight, first_moment, second_moment), partial)
    )
    own_rows = eight(mine, states)
    peer_rows = lax.ppermute(eight(other, states), "xh", SWAP)

    old = jnp.stack(by_block(own_rows, peer_rows), axis=1)
    weight, moment_one, moment_two = adam_update(old[0], old[1], old[2], gradient)

    slices = jnp.stack((weight, moment_one, moment_two * SECOND_SCALE), axis=1)
    along = lax.all_gather(split_halves(slices).reshape(2, 48, 512), "z", axis=0)
    along = along.reshape(32, 2, 3, 8, 512)
    here = 2 * lax.axis_index("z")

    scales = jnp.where(jnp.arange(3) == 2, 1.0 / SECOND_SCALE, 1.0).reshape(3, 1, 1)

    def wanted(index):
        return join_halves(pick(along, pick(partners, index, 0), 0)) * scales

    placed = jnp.stack([wanted(here + i) for i in range(2)]).reshape(1, 2, 3, 8, 512)
    half = exchange(jnp.broadcast_to(placed, (8, 2, 3, 8, 512)).reshape(16, 3, 8, 512), CHIPS)
    sibling = lax.ppermute(half, "c", SWAP)
    outs = place(1 - core, sibling, place(core, half))
    return tuple(item.reshape(256, 512) for item in outs)


def solution(mesh):
    names = tuple(name for name, _ in PARTS)
    sizes = tuple(size for _, size in PARTS)
    fine = Mesh(mesh.devices.reshape(sizes), names)
    return jax.shard_map(
        on_device,
        mesh=fine,
        in_specs=(
            P(DP, FSDP),
            P(DP + FSDP, None),
            P(),
            P(FSDP, None),
            P(FSDP, None),
            P(FSDP, None),
        ),
        out_specs=(P(FSDP, None), P(FSDP, None), P(FSDP, None)),
        check_vma=False,
    )
```

time: 136 us -> 149 us (1.096)
  starting transfers between devices: 31.3 us -> 35.4 us
  other arithmetic: 1.75 us -> 5.65 us
  between operations: 3.41 us -> 0.86 us
  waiting for transfers between devices: 5.78 us -> 8.11 us
  Pallas kernels: 2.6 us -> 4.83 us
    ppermute x1 -> x2, starting transfers between devices: 4.79 us -> 10.8 us  [the longest x1 8.86 us: on_device(): lax.ppermute(products(mine, 1 - core, tokens, got, cotangents), 'c', SWAP)]
    all_to_all x1, waiting for transfers between devices: 1.49 us -> 7.12 us  [exchange(): return lax.all_to_all(array, axes, split_axis=0, concat_axis=0, tiled=True)]
    all_to_all x1, starting transfers between devices: 12.3 us -> 7.04 us  [exchange(): return lax.all_to_all(array, axes, split_axis=0, concat_axis=0, tiled=True)]
    ppermute x1, starting transfers between devices: 8.73 us -> 12.1 us  [on_device(): sibling = lax.ppermute(half, 'c', SWAP)]
    ppermute x1 -> x2, waiting for transfers between devices: 2.39 us -> 0.01 us  [the longest x1 0.01 us: on_device(): peer_rows = lax.ppermute(eight(other, states), 'xh', SWAP)]
    pallas_call x2 -> x4, Pallas kernels: 2.6 us -> 4.83 us  [the longest x2 3.02 us: products(): pl.pallas_call(products_kernel, out_shape=jax.ShapeDtypeStruct((16, 2, 8,...]
    all_gather x1, blocking collectives: 41.7 us -> 43.8 us  [on_device(): cotangents = lax.all_gather(scaled, 'z', axis=0, tiled=True)]
    convert_element_type x1, other arithmetic: 0.43 us -> 2.02 us  [on_device(): (cotangents.astype(jnp.float32) * (1.0 / KEY_SCALE)).astype(jnp.bfloat16)]
  transfers between devices with their start and end apart: 4 -> 5, of which waited for: 3 -> 2; matrix products, arithmetic and copies ran while one was open for 2% -> 2% of each run, Pallas kernels for 0% -> 2%
where the time goes in v7:
time: 149 us; the launch traced here: 148 us
  blocking collectives  87 us (58%)
  starting transfers between devices  35.4 us (24%)
  waiting for transfers between devices  8.11 us (5%)
  local copies, waits for them, and re-layouts  5.92 us (4%)
  other arithmetic  5.65 us (4%)
  Pallas kernels  4.83 us (3%)
    all_gather x1, blocking collectives, on_device(): cotangents = lax.all_gather(scaled, 'z', axis=0, tiled=True)  43.8 us
    all_gather x1, blocking collectives, on_device(): lax.all_gather(split_halves(slices).reshape(2, 48, 512), 'z', axis=0)  29.7 us
    all_to_all x1, blocking collectives, exchange(): return lax.all_to_all(array, axes, split_axis=0, concat_axis=0, tiled=True)  13.5 us
    ppermute x1, starting transfers between devices, on_device(): sibling = lax.ppermute(half, 'c', SWAP)  12.1 us
    ppermute x1, starting transfers between devices, on_device(): lax.ppermute(products(mine, 1 - core, tokens, got, cotangents), 'c', SWAP)  8.86 us
    all_to_all x1, waiting for transfers between devices, exchange(): return lax.all_to_all(array, axes, split_axis=0, concat_axis=0, tiled=True)  7.12 us
    all_to_all x1, starting transfers between devices, exchange(): return lax.all_to_all(array, axes, split_axis=0, concat_axis=0, tiled=True)  7.04 us
    ppermute x1, starting transfers between devices, on_device(): got = lax.ppermute(pick(tokens, other, 1), 'xh', SWAP)  5.47 us
  transfers between devices with their start and end apart: 5, of which 2 were waited for; matrix products, arithmetic and copies ran while one was open for 2% of the time, Pallas kernels for 2%

profile of v7, /device:TPU:1, one launch (start us, length us, event | category | flops | bytes accessed | tf_op | source)
XLA Modules:
  0.0 147.8 jit_solution(4716768836075801404)
XLA Ops:
  0.6 0.0 copy-start.2
  0.6 2.2 %dynamic-slice_bitcast_fusion = bf16[16,112,256]{2,1,0:T(8,128)(2,1)} fusion(bf16[16,2,112,256]{3,2,1,0:T(8,128)(2,1)} %bitcast.77, s32[]{:T(128)S(6)} %sub.37), kind=kLoop, calls=%fused_computation.1 | loop fusion | bytes 1835012 | tf_op jit(solution)/shard_map/jit(dynamic_index_in_dim)/squeeze | solution.py:32
  2.9 5.5 %collective-permute-start = (bf16[16,112,256]{2,1,0:T(8,128)(2,1)}, bf16[16,112,256]{2,1,0:T(8,128)(2,1)S(1)}, u32[]{:S(2)}, u32[]{:S(2)}) collective-permute-start(bf16[16,112,256]{2,1,0:T(8,128)(2,1)} %dynamic-slice_bitcast_fusion), channel_id=1, source_target_pairs={{0,1},{1,0},{2,3},{3,2},{4,5},{5,4},{6,7},{7,6},{8,9},{9,8},{10,11... | collective-permute-start | bytes 2752520 | tf_op jit(solution)/shard_map/ppermute | solution.py:140
  8.3 0.0 copy-done.2
  8.4 43.8 %all-gather.2 = f16[1792,512]{1,0:T(8,128)(2,1)} all-gather(f16[112,512]{1,0:T(8,128)(2,1)S(1)} %multiply_convert_fusion.2), channel_id=1, replica_groups=mesh['xl'=2,'y'=4,'c'=2,'z'=16,'xh'=2] {'z'}, dimensions={0}, use_global_device_ids=true | all-gather | bytes 1949696 | tf_op jit(solution)/shard_map/all_gather | solution.py:155
  52.2 0.1 pad_add_fusion.where_ref
  52.3 0.0 copy-start
  52.3 2.0 %multiply_convert_fusion.cotangents_ref = bf16[1792,512]{1,0:T(8,128)(2,1)S(1)} fusion(f16[1792,512]{1,0:T(8,128)(2,1)} %all-gather.2), kind=kLoop, calls=%fused_computation | loop fusion | flops 2752512 | bytes 3670016 | tf_op jit(solution)/shard_map/convert_element_type | solution.py:156
  54.3 0.0 collective-permute-done
  54.3 0.0 copy-done
  54.3 1.5 %shard_map.85 = f32[16,2,8,512]{3,2,1,0:T(8,128)S(1)} custom-call(s32[2]{0:T(128)S(1)} %pad_add_fusion.where_ref, bf16[16,2,112,256]{3,2,1,0:T(8,128)(2,1)S(1)} %bitcast.78, bf16[1792,256]{1,0:T(8,128)(2,1)S(1)} %bitcast.80, bf16[1792,512]{1,0:T(8,128)(2,1)S(1)} %multiply_convert_fusion.cotangents_ref), custom_call_target="tpu_custom_call" | custom-call | flops 469762048 | bytes 4194304 | tf_op jit(solution)/shard_map/pallas_call | solution.py:77
  55.9 8.9 %collective-permute-start.1 = (f32[16,2,8,512]{3,2,1,0:T(8,128)S(1)}, f32[16,2,8,512]{3,2,1,0:T(8,128)}, u32[]{:S(2)}, u32[]{:S(2)}) collective-permute-start(f32[16,2,8,512]{3,2,1,0:T(8,128)S(1)} %shard_map.85), channel_id=1, source_target_pairs={{0,32},{32,0},{1,33},{33,1},{2,34},{34,2},{3,35},{35,3},{4,36},{36... | collective-permute-start | bytes 1572872 | tf_op jit(solution)/shard_map/ppermute | solution.py:159
  64.7 0.1 pad_add_fusion.1.where_ref
  64.8 0.0 copy-start.1
  64.8 1.5 %copy-done.1 = bf16[3584,256]{1,0:T(8,128)(2,1)S(1)} copy-done((bf16[3584,256]{1,0:T(8,128)(2,1)S(1)}, bf16[3584,256]{1,0:T(8,128)(2,1)}, u32[]{:S(2)}) %copy-start.1) | copy-done | bytes 1835032
  66.3 1.5 %shard_map.86 = f32[16,2,8,512]{3,2,1,0:T(8,128)S(1)} custom-call(s32[2]{0:T(128)S(1)} %pad_add_fusion.1.where_ref, bf16[16,2,112,256]{3,2,1,0:T(8,128)(2,1)S(1)} %bitcast.79, bf16[1792,256]{1,0:T(8,128)(2,1)S(1)} %bitcast.81, bf16[1792,512]{1,0:T(8,128)(2,1)S(1)} %multiply_convert_fusion.cotangents_ref), custom_call_target="tpu_custom_call" | custom-call | flops 469762048 | bytes 4194304 | tf_op jit(solution)/shard_map/pallas_call | solution.py:77
  67.8 0.0 copy-start.3
  67.9 0.0 collective-permute-done.1
  67.9 1.9 %multiply_convert_fusion.1 = f16[16,2,8,512]{3,2,1,0:T(8,128)(2,1)} fusion(f32[16,2,8,512]{3,2,1,0:T(8,128)} %collective-permute-done.1, f32[16,2,8,512]{3,2,1,0:T(8,128)S(1)} %shard_map.86), kind=kLoop, calls=%fused_computation.3 | loop fusion | flops 393216 | bytes 1310720 | tf_op jit(solution)/shard_map/convert_element_type | solution.py:161
  69.7 0.7 dynamic-slice_bitcast_fusion.6
  70.5 0.8 dynamic-slice_bitcast_fusion.4
  71.2 1.9 %collective-permute-start.2 = (f32[3,8,512]{2,1,0:T(8,128)S(1)}, f32[3,8,512]{2,1,0:T(8,128)S(1)}, u32[]{:S(2)}, u32[]{:S(2)}) collective-permute-start(f32[3,8,512]{2,1,0:T(8,128)S(1)} %pad_maximum_fusion.4), channel_id=1, source_target_pairs={{0,1},{1,0},{2,3},{3,2},{4,5},{5,4},{6,7},{7,6},{8,9},{9,8},{10,11... | collective-permute-start | bytes 147464 | tf_op jit(solution)/shard_map/ppermute | solution.py:168
  73.2 7.0 %all-to-all-start = ((f16[16,2,8,512]{3,2,1,0:T(8,128)(2,1)}), f16[16,2,8,512]{3,2,1,0:T(8,128)(2,1)S(1)}, u32[]{:S(2)}, u32[]{:S(2)}) async-start(f16[16,2,8,512]{3,2,1,0:T(8,128)(2,1)} %multiply_convert_fusion.1), calls=%async_computation | async-start | bytes 524288 | tf_op jit(solution)/shard_map/all_to_all | solution.py:28
  80.2 0.0 copy-done.3
  80.2 0.6 fusion.19
  80.8 0.0 collective-permute-done.2
  80.9 7.1 %all-to-all-done = f16[16,2,8,512]{3,2,1,0:T(8,128)(2,1)S(1)} async-done(((f16[16,2,8,512]{3,2,1,0:T(8,128)(2,1)}), f16[16,2,8,512]{3,2,1,0:T(8,128)(2,1)S(1)}, u32[]{:S(2)}, u32[]{:S(2)}) %all-to-all-start) | async-done | bytes 262176 | tf_op jit(solution)/shard_map/all_to_all | solution.py:28
  88.1 0.1 reduce-precision_convert_fusion
  88.2 29.7 %all-gather.3 = f16[16,2,48,512]{3,2,1,0:T(8,128)(2,1)S(1)} all-gather(f16[1,2,48,512]{3,2,1,0:T(8,128)(2,1)S(1)} %bitcast.87), channel_id=1, replica_groups=mesh['xl'=2,'y'=4,'c'=2,'z'=16,'xh'=2] {'z'}, dimensions={0}, use_global_device_ids=true | all-gather | bytes 1671168 | tf_op jit(solution)/shard_map/all_gather | solution.py:174
  117.9 1.3 dynamic-slice_convert_fusion.1
  119.2 0.1 fusion.7
  119.3 0.1 broadcast_in_dim.15
  119.4 13.5 %all_to_all.10.source_ref = f32[16,3,8,512]{3,2,1,0:T(8,128)S(1)} all-to-all(f32[16,3,8,512]{3,2,1,0:T(8,128)S(1)} %bitcast.82), channel_id=1, replica_groups=mesh['xl'=2,'y'=4,'c'=2,'z'=16,'xh'=2] {'xl','y','xh'}, dimensions={0} | all-to-all | bytes 1572864 | tf_op jit(solution)/shard_map/all_to_all | solution.py:28
  132.9 12.1 %collective-permute-start.3 = (f32[16,3,8,512]{3,2,1,0:T(8,128)S(1)}, f32[16,3,8,512]{3,2,1,0:T(8,128)S(1)}, u32[]{:S(2)}, u32[]{:S(2)}) collective-permute-start(f32[16,3,8,512]{3,2,1,0:T(8,128)S(1)} %all_to_all.10.source_ref), channel_id=1, source_target_pairs={{0,32},{32,0},{1,33},{33,1},{2,34},{34,2},{3,35},{35,3},{4,36},{36... | collective-permute-start | bytes 2359304 | tf_op jit(solution)/shard_map/ppermute | solution.py:185
  145.0 0.9 shard_map.87
  146.0 1.0 collective-permute-done.3.source_ref
  146.9 0.9 shard_map.88
  (9 shorter events, 0.2 us)
Async XLA Ops:
  0.6 7.7 %copy-start.2 = (bf16[112,512]{1,0:T(8,128)(2,1)S(1)}, bf16[112,512]{1,0:T(8,128)(2,1)}, u32[]{:S(2)}) copy-start(bf16[112,512]{1,0:T(8,128)(2,1)} %param.7) | copy-start | bytes 344068
  2.9 51.5 %collective-permute-start = (bf16[16,112,256]{2,1,0:T(8,128)(2,1)}, bf16[16,112,256]{2,1,0:T(8,128)(2,1)S(1)}, u32[]{:S(2)}, u32[]{:S(2)}) collective-permute-start(bf16[16,112,256]{2,1,0:T(8,128)(2,1)} %dynamic-slice_bitcast_fusion), channel_id=1, source_target_pairs={{0,1},{1,0},{2,3},{3,2},{4,5},{5,4},{6,7},{7,6},{8,9},{9,8},{10,11... | collective-permute-start | bytes 2752520 | tf_op jit(solution)/shard_map/ppermute | solution.py:140
  52.3 2.1 %copy-start = (bf16[3584,256]{1,0:T(8,128)(2,1)S(1)}, bf16[3584,256]{1,0:T(8,128)(2,1)}, u32[]{:S(2)}) copy-start(bf16[3584,256]{1,0:T(8,128)(2,1)} %param.6) | copy-start | bytes 5505028
  55.9 12.0 %collective-permute-start.1 = (f32[16,2,8,512]{3,2,1,0:T(8,128)S(1)}, f32[16,2,8,512]{3,2,1,0:T(8,128)}, u32[]{:S(2)}, u32[]{:S(2)}) collective-permute-start(f32[16,2,8,512]{3,2,1,0:T(8,128)S(1)} %shard_map.85), channel_id=1, source_target_pairs={{0,32},{32,0},{1,33},{33,1},{2,34},{34,2},{3,35},{35,3},{4,36},{36... | collective-permute-start | bytes 1572872 | tf_op jit(solution)/shard_map/ppermute | solution.py:159
  64.8 1.5 %copy-start.1 = (bf16[3584,256]{1,0:T(8,128)(2,1)S(1)}, bf16[3584,256]{1,0:T(8,128)(2,1)}, u32[]{:S(2)}) copy-start(bf16[3584,256]{1,0:T(8,128)(2,1)} %param.6) | copy-start | bytes 5505028
  67.8 12.4 %copy-start.3 = (s32[32]{0:T(128)S(1)}, s32[32]{0:T(128)}, u32[]{:S(2)}) copy-start(s32[32]{0:T(128)} %param.8) | copy-start | bytes 388
  71.2 9.6 %collective-permute-start.2 = (f32[3,8,512]{2,1,0:T(8,128)S(1)}, f32[3,8,512]{2,1,0:T(8,128)S(1)}, u32[]{:S(2)}, u32[]{:S(2)}) collective-permute-start(f32[3,8,512]{2,1,0:T(8,128)S(1)} %pad_maximum_fusion.4), channel_id=1, source_target_pairs={{0,1},{1,0},{2,3},{3,2},{4,5},{5,4},{6,7},{7,6},{8,9},{9,8},{10,11... | collective-permute-start | bytes 147464 | tf_op jit(solution)/shard_map/ppermute | solution.py:168
  73.2 14.8 %all-to-all-start = ((f16[16,2,8,512]{3,2,1,0:T(8,128)(2,1)}), f16[16,2,8,512]{3,2,1,0:T(8,128)(2,1)S(1)}, u32[]{:S(2)}, u32[]{:S(2)}) async-start(f16[16,2,8,512]{3,2,1,0:T(8,128)(2,1)} %multiply_convert_fusion.1), calls=%async_computation | async-start | bytes 524288 | tf_op jit(solution)/shard_map/all_to_all | solution.py:28
  132.9 14.0 %collective-permute-start.3 = (f32[16,3,8,512]{3,2,1,0:T(8,128)S(1)}, f32[16,3,8,512]{3,2,1,0:T(8,128)S(1)}, u32[]{:S(2)}, u32[]{:S(2)}) collective-permute-start(f32[16,3,8,512]{3,2,1,0:T(8,128)S(1)} %all_to_all.10.source_ref), channel_id=1, source_target_pairs={{0,32},{32,0},{1,33},{33,1},{2,34},{34,2},{3,35},{35,3},{4,36},{36... | collective-permute-start | bytes 2359304 | tf_op jit(solution)/shard_map/ppermute | solution.py:185

commit v8 on v5

--- a/solution.py
+++ b/solution.py
@@ -20,8 +20,6 @@
 PLANE = ("c", "xl", "y", "xh")
 SWAP = [(0, 1), (1, 0)]
 KEY_SCALE = 2.0**21
-REST_SCALE = 2.0**11
-SECOND_SCALE = 2.0**-6
 PARTIAL_SCALE = 2.0**7
 
 
@@ -33,17 +31,6 @@
     return lax.dynamic_index_in_dim(
         array, index, axis=axis, keepdims=False, allow_negative_indices=False
     )
-
-
-def split_halves(values):
-    high = lax.reduce_precision(values, exponent_bits=5, mantissa_bits=10)
-    rest = (values - high) * REST_SCALE
-    return jnp.stack((high.astype(jnp.float16), rest.astype(jnp.float16)))
-
-
-def join_halves(halves):
-    wide = halves.astype(jnp.float32)
-    return wide[0] + wide[1] * (1.0 / REST_SCALE)
 
 
 def adam_update(weight, first_moment, second_moment, gradient):
@@ -123,6 +110,24 @@
     return tuple(item.reshape(256, 512) for item in outs)
 
 
+def pick_kernel(partners_ref, spread_ref, out_ref):
+    for j in range(32):
+        out_ref[j] = spread_ref[partners_ref[j]]
+
+
+def pick_blocks(spread, partners):
+    return pl.pallas_call(
+        pick_kernel,
+        out_shape=jax.ShapeDtypeStruct(spread.shape, spread.dtype),
+        in_specs=[
+            pl.BlockSpec(memory_space=pltpu.SMEM),
+            pl.BlockSpec(memory_space=pltpu.VMEM),
+        ],
+        out_specs=pl.BlockSpec(memory_space=pltpu.VMEM),
+        compiler_params=pltpu.CompilerParams(vmem_limit_bytes=40 * 1024 * 1024),
+    )(partners, spread)
+
+
 def on_device(activations, key_grads, partners, master_weight, first_moment, second_moment):
     mine = lax.axis_index("xh")
     other = 1 - mine
@@ -137,42 +142,40 @@
 
     first_row = 128 * core + 16 * column
 
-    def eight(side):
+    def eight(side, states):
         return jnp.stack(
             [
                 lax.dynamic_slice_in_dim(
                     item, first_row + 8 * side, 8, axis=0, allow_negative_indices=False
                 )
-                for item in (master_weight, first_moment, second_moment)
+                for item in states
             ]
         )
 
     scaled = (key_grads.astype(jnp.float32) * KEY_SCALE).astype(jnp.float16)
     cotangents = lax.all_gather(scaled, "z", axis=0, tiled=True)
-    own_rows, outgoing, cotangents = lax.optimization_barrier(
-        (eight(mine), eight(other), cotangents)
+    cotangents = (cotangents.astype(jnp.float32) * (1.0 / KEY_SCALE)).astype(jnp.bfloat16)
+
+    partial = products(mine, tokens, got.reshape(1792, 256), cotangents)
+    states, partial = lax.optimization_barrier(
+        ((master_weight, first_moment, second_moment), partial)
     )
-    peer_rows = lax.ppermute(outgoing, "xh", SWAP)
-    cotangents = (cotangents.astype(jnp.float32) * (1.0 / KEY_SCALE)).astype(jnp.bfloat16)
-
-    partial = products(mine, tokens, got.reshape(1792, 256), cotangents)
     pieces = exchange((partial * PARTIAL_SCALE).astype(jnp.float16), PLANE)
     gradient = jnp.sum(pieces.astype(jnp.float32), axis=0) * (1.0 / PARTIAL_SCALE)
 
+    own_rows = eight(mine, states)
+    peer_rows = lax.ppermute(eight(other, states), "xh", SWAP)
     old = jnp.stack(by_block(own_rows, peer_rows), axis=1)
-    weight, moment_one, moment_two = adam_update(old[0], old[1], old[2], gradient)
-
-    slices = jnp.stack((weight, moment_one, moment_two * SECOND_SCALE), axis=1)
-    along = lax.all_gather(split_halves(slices), "z", axis=0, tiled=False)
-    here = 2 * lax.axis_index("z")
-
-    scales = jnp.array([1.0, 1.0, 1.0 / SECOND_SCALE], jnp.float32).reshape(3, 1, 1)
-
-    def wanted(index):
-        place = pick(partners, index, 0)
-        return join_halves(pick(pick(along, place >> 1, 0), place & 1, 1)) * scales
-
-    placed = jnp.stack([wanted(here + i) for i in range(2)]).reshape(1, 2, 3, 8, 512)
+    new = jnp.stack(adam_update(old[0], old[1], old[2], gradient))
+
+    pieces = new.reshape(3, 2, 8, 2, 2, 128).transpose(2, 3, 1, 0, 4, 5).reshape(16, 2, 6, 128)
+    pieces = jnp.pad(pieces, ((0, 0), (0, 0), (0, 2), (0, 0))).reshape(16, 16, 128)
+    spread = exchange(pieces, "z").reshape(32, 8, 128)
+    picked = pick_blocks(spread, partners).reshape(16, 16, 128)
+    arrived = exchange(picked, "z").reshape(16, 2, 8, 128)[:, :, :6]
+    placed = arrived.reshape(8, 2, 2, 3, 2, 128).transpose(2, 3, 0, 1, 4, 5)
+
+    placed = placed.reshape(1, 2, 3, 8, 512)
     half = exchange(jnp.broadcast_to(placed, (8, 2, 3, 8, 512)).reshape(16, 3, 8, 512), CHIPS)
     sibling = lax.ppermute(half, "c", SWAP)
     return assemble(core, half, sibling)

time: 136 us -> 139 us (1.022)
  blocking collectives: 86.4 us -> 91.2 us
  between operations: 3.41 us -> 0.8 us
  starting transfers between devices: 31.3 us -> 29.3 us
  waiting for transfers between devices: 5.78 us -> 7.47 us
    all_to_all x1 -> x3, blocking collectives: 13.6 us -> 49.4 us  [exchange(): return lax.all_to_all(array, axes, split_axis=0, concat_axis=0, tiled=True)]
    all_gather x1 -> x0, blocking collectives: 31.1 us -> none  [on_device(): along = lax.all_gather(split_halves(slices), 'z', axis=0, tiled=False)]
    ppermute x1, starting transfers between devices: 8.73 us -> 6.64 us  [on_device(): sibling = lax.ppermute(half, 'c', SWAP)]
    ppermute x1, waiting for transfers between devices: 2.39 us -> 4.08 us  [on_device(): peer_rows = lax.ppermute(eight(other, states), 'xh', SWAP)]
  transfers between devices with their start and end apart: 4 -> 4, of which waited for: 3 -> 3; matrix products, arithmetic and copies ran while one was open for 2% -> 1% of each run, Pallas kernels for 0% -> 0%
where the time goes in v8:
time: 139 us; the launch traced here: 138 us
  blocking collectives  91.2 us (66%)
  starting transfers between devices  29.3 us (21%)
  waiting for transfers between devices  7.47 us (5%)
  local copies, waits for them, and re-layouts  5.09 us (4%)
  Pallas kernels  3.17 us (2%)
  other arithmetic  1.5 us (1%)
    all_to_all x3, blocking collectives, exchange(): return lax.all_to_all(array, axes, split_axis=0, concat_axis=0, tiled=True)  49.4 us
    all_gather x1, blocking collectives, on_device(): cotangents = lax.all_gather(scaled, 'z', axis=0, tiled=True)  41.7 us
    all_to_all x1, starting transfers between devices, exchange(): return lax.all_to_all(array, axes, split_axis=0, concat_axis=0, tiled=True)  12.4 us
    ppermute x1, starting transfers between devices, on_device(): sibling = lax.ppermute(half, 'c', SWAP)  6.64 us
    ppermute x1, starting transfers between devices, on_device(): got = lax.ppermute(pick(tokens, other, 1), 'xh', SWAP)  5.47 us
    ppermute x1, starting transfers between devices, on_device(): peer_rows = lax.ppermute(eight(other, states), 'xh', SWAP)  4.79 us
    ppermute x1, waiting for transfers between devices, on_device(): peer_rows = lax.ppermute(eight(other, states), 'xh', SWAP)  4.08 us
  transfers between devices with their start and end apart: 4, of which 3 were waited for; matrix products, arithmetic and copies ran while one was open for 1% of the time, Pallas kernels for 0%

profile of v8, /device:TPU:1, one launch (start us, length us, event | category | flops | bytes accessed | tf_op | source)
XLA Modules:
  0.0 138.5 jit_solution(11077632133985380023)
XLA Ops:
  0.6 0.0 copy-start.2
  0.6 2.2 %dynamic-slice_bitcast_fusion = bf16[16,112,256]{2,1,0:T(8,128)(2,1)} fusion(bf16[16,2,112,256]{3,2,1,0:T(8,128)(2,1)} %bitcast.48, s32[]{:T(128)S(6)} %sub.7), kind=kLoop, calls=%fused_computation.3 | loop fusion | bytes 1835012 | tf_op jit(solution)/shard_map/jit(dynamic_index_in_dim)/squeeze | solution.py:31
  2.9 5.5 %collective-permute-start = (bf16[16,112,256]{2,1,0:T(8,128)(2,1)}, bf16[16,112,256]{2,1,0:T(8,128)(2,1)S(1)}, u32[]{:S(2)}, u32[]{:S(2)}) collective-permute-start(bf16[16,112,256]{2,1,0:T(8,128)(2,1)} %dynamic-slice_bitcast_fusion), channel_id=1, source_target_pairs={{0,1},{1,0},{2,3},{3,2},{4,5},{5,4},{6,7},{7,6},{8,9},{9,8},{10,11... | collective-permute-start | bytes 2752520 | tf_op jit(solution)/shard_map/ppermute | solution.py:141
  8.3 0.0 copy-done.2
  8.4 41.7 %all-gather.1 = f16[1792,512]{1,0:T(8,128)(2,1)S(1)} all-gather(f16[112,512]{1,0:T(8,128)(2,1)S(1)} %multiply_convert_fusion.2), channel_id=1, replica_groups=mesh['xl'=2,'y'=4,'c'=2,'z'=16,'xh'=2] {'z'}, dimensions={0}, use_global_device_ids=true | all-gather | bytes 1949696 | tf_op jit(solution)/shard_map/all_gather | solution.py:156
  50.1 0.0 copy-start
  50.1 0.4 multiply_convert_fusion.cotangents_ref
  50.5 0.0 collective-permute-done
  50.5 1.1 copy-done
  51.6 1.4 %shard_map.85 = f32[32,2,8,512]{3,2,1,0:T(8,128)S(1)} custom-call(s32[1]{0:T(128)} %bitcast.1.mine_ref, bf16[16,2,112,256]{3,2,1,0:T(8,128)(2,1)S(1)} %bitcast.49, bf16[1792,256]{1,0:T(8,128)(2,1)S(1)} %bitcast.50, bf16[1792,512]{1,0:T(8,128)(2,1)S(1)} %multiply_convert_fusion.cotangents_ref), custom_call_target="tpu_custom_call" | custom-call | flops 939524096 | bytes 6291456 | tf_op jit(solution)/shard_map/pallas_call | solution.py:64
  53.0 0.9 multiply_convert_fusion.1
  54.0 0.0 copy-start.1
  54.0 12.4 %all-to-all-start = ((f16[32,2,8,512]{3,2,1,0:T(8,128)(2,1)}), f16[32,2,8,512]{3,2,1,0:T(8,128)(2,1)S(1)}, u32[]{:S(2)}, u32[]{:S(2)}) async-start(f16[32,2,8,512]{3,2,1,0:T(8,128)(2,1)} %multiply_convert_fusion.1), calls=%async_computation | async-start | bytes 1048576 | tf_op jit(solution)/shard_map/all_to_all | solution.py:27
  66.4 0.7 dynamic-slice_bitcast_fusion.6
  67.1 0.8 dynamic-slice_bitcast_fusion.4
  67.9 4.8 %collective-permute-start.1 = (f32[3,8,512]{2,1,0:T(8,128)S(1)}, f32[3,8,512]{2,1,0:T(8,128)S(1)}, u32[]{:S(2)}, u32[]{:S(2)}) collective-permute-start(f32[3,8,512]{2,1,0:T(8,128)S(1)} %pad_maximum_fusion.1), channel_id=1, source_target_pairs={{0,1},{1,0},{2,3},{3,2},{4,5},{5,4},{6,7},{7,6},{8,9},{9,8},{10,11... | collective-permute-start | bytes 147464 | tf_op jit(solution)/shard_map/ppermute | solution.py:167
  72.7 4.1 %collective-permute-done.1 = f32[3,8,512]{2,1,0:T(8,128)S(1)} collective-permute-done((f32[3,8,512]{2,1,0:T(8,128)S(1)}, f32[3,8,512]{2,1,0:T(8,128)S(1)}, u32[]{:S(2)}, u32[]{:S(2)}) %collective-permute-start.1) | collective-permute-done | bytes 49184 | tf_op jit(solution)/shard_map/ppermute | solution.py:167
  76.8 1.5 %all-to-all-done = f16[32,2,8,512]{3,2,1,0:T(8,128)(2,1)S(1)} async-done(((f16[32,2,8,512]{3,2,1,0:T(8,128)(2,1)}), f16[32,2,8,512]{3,2,1,0:T(8,128)(2,1)S(1)}, u32[]{:S(2)}, u32[]{:S(2)}) %all-to-all-start) | async-done | bytes 524320 | tf_op jit(solution)/shard_map/all_to_all | solution.py:27
  78.3 0.1 convert_reduce_fusion
  78.4 0.1 copy.17
  78.6 18.6 %all_to_all.20 = f32[16,16,128]{2,1,0:T(8,128)S(1)} all-to-all(f32[16,16,128]{2,1,0:T(8,128)S(1)} %copy.18), channel_id=1, replica_groups=mesh['xl'=2,'y'=4,'c'=2,'z'=16,'xh'=2] {'z'}, dimensions={0} | all-to-all | bytes 262144 | tf_op jit(solution)/shard_map/all_to_all | solution.py:27
  97.1 0.0 copy-done.1
  97.1 0.6 shard_map.86
  97.7 17.8 %all_to_all.21 = f32[16,16,128]{2,1,0:T(8,128)S(1)} all-to-all(f32[16,16,128]{2,1,0:T(8,128)S(1)} %bitcast.52), channel_id=1, replica_groups=mesh['xl'=2,'y'=4,'c'=2,'z'=16,'xh'=2] {'z'}, dimensions={0} | all-to-all | bytes 262144 | tf_op jit(solution)/shard_map/all_to_all | solution.py:27
  115.6 0.1 broadcast_in_dim.8
  115.7 13.1 %all_to_all.22.half_ref = f32[16,3,8,512]{3,2,1,0:T(8,128)S(1)} all-to-all(f32[16,3,8,512]{3,2,1,0:T(8,128)S(1)} %bitcast.53), channel_id=1, replica_groups=mesh['xl'=2,'y'=4,'c'=2,'z'=16,'xh'=2] {'xl','y','xh'}, dimensions={0} | all-to-all | bytes 1572864 | tf_op jit(solution)/shard_map/all_to_all | solution.py:27
  128.7 6.6 %collective-permute-start.2 = (f32[16,3,8,512]{3,2,1,0:T(8,128)S(1)}, f32[16,3,8,512]{3,2,1,0:T(8,128)S(1)}, u32[]{:S(2)}, u32[]{:S(2)}) collective-permute-start(f32[16,3,8,512]{3,2,1,0:T(8,128)S(1)} %all_to_all.22.half_ref), channel_id=1, source_target_pairs={{0,32},{32,0},{1,33},{33,1},{2,34},{34,2},{3,35},{35,3},{4,36},{36... | collective-permute-start | bytes 2359304 | tf_op jit(solution)/shard_map/ppermute | solution.py:180
  135.4 1.9 %collective-permute-done.2.sibling_ref = f32[16,3,8,512]{3,2,1,0:T(8,128)S(1)} collective-permute-done((f32[16,3,8,512]{3,2,1,0:T(8,128)S(1)}, f32[16,3,8,512]{3,2,1,0:T(8,128)S(1)}, u32[]{:S(2)}, u32[]{:S(2)}) %collective-permute-start.2) | collective-permute-done | bytes 786464 | tf_op jit(solution)/shard_map/ppermute | solution.py:180
  137.3 1.2 shard_map.87
  (10 shorter events, 0.2 us)
Async XLA Ops:
  0.6 7.7 %copy-start.2 = (bf16[112,512]{1,0:T(8,128)(2,1)S(1)}, bf16[112,512]{1,0:T(8,128)(2,1)}, u32[]{:S(2)}) copy-start(bf16[112,512]{1,0:T(8,128)(2,1)} %param.7) | copy-start | bytes 344068
  2.9 47.6 %collective-permute-start = (bf16[16,112,256]{2,1,0:T(8,128)(2,1)}, bf16[16,112,256]{2,1,0:T(8,128)(2,1)S(1)}, u32[]{:S(2)}, u32[]{:S(2)}) collective-permute-start(bf16[16,112,256]{2,1,0:T(8,128)(2,1)} %dynamic-slice_bitcast_fusion), channel_id=1, source_target_pairs={{0,1},{1,0},{2,3},{3,2},{4,5},{5,4},{6,7},{7,6},{8,9},{9,8},{10,11... | collective-permute-start | bytes 2752520 | tf_op jit(solution)/shard_map/ppermute | solution.py:141
  50.1 1.5 %copy-start = (bf16[3584,256]{1,0:T(8,128)(2,1)S(1)}, bf16[3584,256]{1,0:T(8,128)(2,1)}, u32[]{:S(2)}) copy-start(bf16[3584,256]{1,0:T(8,128)(2,1)} %param.6) | copy-start | bytes 5505028
  54.0 43.2 %copy-start.1 = (s32[32]{0:T(128)S(1)}, s32[32]{0:T(128)}, u32[]{:S(2)}) copy-start(s32[32]{0:T(128)} %partners_ref.1) | copy-start | bytes 388
  54.0 24.3 %all-to-all-start = ((f16[32,2,8,512]{3,2,1,0:T(8,128)(2,1)}), f16[32,2,8,512]{3,2,1,0:T(8,128)(2,1)S(1)}, u32[]{:S(2)}, u32[]{:S(2)}) async-start(f16[32,2,8,512]{3,2,1,0:T(8,128)(2,1)} %multiply_convert_fusion.1), calls=%async_computation | async-start | bytes 1048576 | tf_op jit(solution)/shard_map/all_to_all | solution.py:27
  67.9 8.9 %collective-permute-start.1 = (f32[3,8,512]{2,1,0:T(8,128)S(1)}, f32[3,8,512]{2,1,0:T(8,128)S(1)}, u32[]{:S(2)}, u32[]{:S(2)}) collective-permute-start(f32[3,8,512]{2,1,0:T(8,128)S(1)} %pad_maximum_fusion.1), channel_id=1, source_target_pairs={{0,1},{1,0},{2,3},{3,2},{4,5},{5,4},{6,7},{7,6},{8,9},{9,8},{10,11... | collective-permute-start | bytes 147464 | tf_op jit(solution)/shard_map/ppermute | solution.py:167
  128.7 8.5 %collective-permute-start.2 = (f32[16,3,8,512]{3,2,1,0:T(8,128)S(1)}, f32[16,3,8,512]{3,2,1,0:T(8,128)S(1)}, u32[]{:S(2)}, u32[]{:S(2)}) collective-permute-start(f32[16,3,8,512]{3,2,1,0:T(8,128)S(1)} %all_to_all.22.half_ref), channel_id=1, source_target_pairs={{0,32},{32,0},{1,33},{33,1},{2,34},{34,2},{3,35},{35,3},{4,36},{36... | collective-permute-start | bytes 2359304 | tf_op jit(solution)/shard_map/ppermute | solution.py:180

commit v9 on v5

--- a/solution.py
+++ b/solution.py
@@ -52,6 +52,42 @@
     step_size = new_first / correct_first / (jnp.sqrt(new_second / correct_second) + 1e-08)
     new_weight = weight - learn_rate * (step_size + weight_decay * weight)
     return (new_weight, new_first, new_second)
+
+
+def outgoing_kernel(other_ref, tokens_ref, out_ref, held, read, sent):
+    other = other_ref[0]
+    reads, sends = [], []
+    for i in range(4):
+        part = pl.ds(4 * i, 4)
+        reads.append(
+            pltpu.make_async_copy(tokens_ref.at[part, other], held.at[part], read.at[i])
+        )
+        sends.append(pltpu.make_async_copy(held.at[part], out_ref.at[part], sent.at[i]))
+    for copy in reads:
+        copy.start()
+    for arriving, leaving in zip(reads, sends):
+        arriving.wait()
+        leaving.start()
+    for copy in sends:
+        copy.wait()
+
+
+def outgoing(other, tokens):
+    return pl.pallas_call(
+        outgoing_kernel,
+        out_shape=jax.ShapeDtypeStruct((16, 112, 256), jnp.bfloat16),
+        in_specs=[
+            pl.BlockSpec(memory_space=pltpu.SMEM),
+            pl.BlockSpec(memory_space=pl.ANY),
+        ],
+        out_specs=pl.BlockSpec(memory_space=pl.ANY),
+        scratch_shapes=[
+            pltpu.VMEM((16, 112, 256), jnp.bfloat16),
+            pltpu.SemaphoreType.DMA((4,)),
+            pltpu.SemaphoreType.DMA((4,)),
+        ],
+        compiler_params=pltpu.CompilerParams(vmem_limit_bytes=56 * 1024 * 1024),
+    )(other.reshape(1), tokens)
 
 
 def products_kernel(mine_ref, tokens_ref, got_ref, cotangents_ref, out_ref, kept, arrived):
@@ -133,32 +169,31 @@
         return jnp.where(mine == 0, own, peer), jnp.where(mine == 0, peer, own)
 
     tokens = activations.reshape(16, 2, 112, 256)
-    got = lax.ppermute(pick(tokens, other, 1), "xh", SWAP)
+    got = lax.ppermute(outgoing(other, tokens), "xh", SWAP)
 
     first_row = 128 * core + 16 * column
 
-    def eight(side):
+    def eight(side, states):
         return jnp.stack(
             [
                 lax.dynamic_slice_in_dim(
                     item, first_row + 8 * side, 8, axis=0, allow_negative_indices=False
                 )
-                for item in (master_weight, first_moment, second_moment)
+                for item in states
             ]
         )
 
     scaled = (key_grads.astype(jnp.float32) * KEY_SCALE).astype(jnp.float16)
     cotangents = lax.all_gather(scaled, "z", axis=0, tiled=True)
-    own_rows, outgoing, cotangents = lax.optimization_barrier(
-        (eight(mine), eight(other), cotangents)
-    )
-    peer_rows = lax.ppermute(outgoing, "xh", SWAP)
     cotangents = (cotangents.astype(jnp.float32) * (1.0 / KEY_SCALE)).astype(jnp.bfloat16)
 
     partial = products(mine, tokens, got.reshape(1792, 256), cotangents)
+    states = (master_weight, first_moment, second_moment)
     pieces = exchange((partial * PARTIAL_SCALE).astype(jnp.float16), PLANE)
     gradient = jnp.sum(pieces.astype(jnp.float32), axis=0) * (1.0 / PARTIAL_SCALE)
 
+    own_rows = eight(mine, states)
+    peer_rows = lax.ppermute(eight(other, states), "xh", SWAP)
     old = jnp.stack(by_block(own_rows, peer_rows), axis=1)
     weight, moment_one, moment_two = adam_update(old[0], old[1], old[2], gradient)
 

time: 136 us -> 136 us (level)
  Pallas kernels: 2.6 us -> 4.66 us
  waiting for transfers between devices: 5.78 us -> 4.24 us
    pallas_call x0 -> x1, Pallas kernels: none -> 2.06 us  [outgoing(): pl.pallas_call(outgoing_kernel, out_shape=jax.ShapeDtypeStruct((16, 112,...]
    ppermute x2, waiting for transfers between devices: 2.4 us -> 0.86 us  [the longest x1 0.86 us: on_device(): peer_rows = lax.ppermute(eight(other, states), 'xh', SWAP)]
where the time goes in v9:
time: 136 us; the launch traced here: 135 us
  blocking collectives  85.7 us (63%)
  starting transfers between devices  32 us (24%)
  Pallas kernels  4.66 us (3%)
  waiting for transfers between devices  4.24 us (3%)
  local copies, waits for them, and re-layouts  3.38 us (2%)
  between operations  3.35 us (2%)
  other arithmetic  1.69 us (1%)
    all_gather x1, blocking collectives, on_device(): cotangents = lax.all_gather(scaled, 'z', axis=0, tiled=True)  41.7 us
    all_gather x1, blocking collectives, on_device(): along = lax.all_gather(split_halves(slices), 'z', axis=0, tiled=False)  31.1 us
    all_to_all x1, blocking collectives, exchange(): return lax.all_to_all(array, axes, split_axis=0, concat_axis=0, tiled=True)  12.9 us
    all_to_all x1, starting transfers between devices, exchange(): return lax.all_to_all(array, axes, split_axis=0, concat_axis=0, tiled=True)  12.3 us
    ppermute x1, starting transfers between devices, on_device(): sibling = lax.ppermute(half, 'c', SWAP)  9.45 us
    ppermute x1, starting transfers between devices, on_device(): got = lax.ppermute(outgoing(other, tokens), 'xh', SWAP)  5.48 us
    ppermute x1, starting transfers between devices, on_device(): peer_rows = lax.ppermute(eight(other, states), 'xh', SWAP)  4.79 us
  transfers between devices with their start and end apart: 4, of which 3 were waited for; matrix products, arithmetic and copies ran while one was open for 2% of the time, Pallas kernels for 0%

profile of v9, /device:TPU:1, one launch (start us, length us, event | category | flops | bytes accessed | tf_op | source)
XLA Modules:
  0.0 135.0 jit_solution(13435242295408314065)
XLA Ops:
  0.6 0.0 copy-start.1
  0.6 2.1 %shard_map.94 = bf16[16,112,256]{2,1,0:T(8,128)(2,1)} custom-call(s32[1]{0:T(128)} %bitcast.14.other_ref, bf16[16,2,112,256]{3,2,1,0:T(8,128)(2,1)} %bitcast.76), custom_call_target="tpu_custom_call" | custom-call | tf_op jit(solution)/shard_map/pallas_call | solution.py:76
  2.7 5.5 %collective-permute-start.1 = (bf16[16,112,256]{2,1,0:T(8,128)(2,1)}, bf16[16,112,256]{2,1,0:T(8,128)(2,1)S(1)}, u32[]{:S(2)}, u32[]{:S(2)}) collective-permute-start(bf16[16,112,256]{2,1,0:T(8,128)(2,1)} %shard_map.94), channel_id=1, source_target_pairs={{0,1},{1,0},{2,3},{3,2},{4,5},{5,4},{6,7},{7,6},{8,9},{9,8},{10,11... | collective-permute-start | bytes 2752520 | tf_op jit(solution)/shard_map/ppermute | solution.py:172
  8.2 0.0 copy-done.1
  8.2 41.7 %all-gather.3 = f16[1792,512]{1,0:T(8,128)(2,1)S(1)} all-gather(f16[112,512]{1,0:T(8,128)(2,1)S(1)} %multiply_convert_fusion.2), channel_id=1, replica_groups=mesh['xl'=2,'y'=4,'c'=2,'z'=16,'xh'=2] {'z'}, dimensions={0}, use_global_device_ids=true | all-gather | bytes 1949696 | tf_op jit(solution)/shard_map/all_gather | solution.py:187
  50.0 0.0 copy-start
  50.0 0.4 multiply_convert_fusion.cotangents_ref
  50.4 0.0 collective-permute-done.1
  50.4 1.1 copy-done
  51.5 1.4 %shard_map.95 = f32[32,2,8,512]{3,2,1,0:T(8,128)S(1)} custom-call(s32[1]{0:T(128)} %bitcast.12.mine_ref, bf16[16,2,112,256]{3,2,1,0:T(8,128)(2,1)S(1)} %bitcast.77, bf16[1792,256]{1,0:T(8,128)(2,1)S(1)} %bitcast.78, bf16[1792,512]{1,0:T(8,128)(2,1)S(1)} %multiply_convert_fusion.cotangents_ref), custom_call_target="tpu_custom_call" | custom-call | flops 939524096 | bytes 6291456 | tf_op jit(solution)/shard_map/pallas_call | solution.py:113
  52.9 0.0 copy-start.2
  52.9 0.9 multiply_convert_fusion.1
  53.8 12.3 %all-to-all-start = ((f16[32,2,8,512]{3,2,1,0:T(8,128)(2,1)}), f16[32,2,8,512]{3,2,1,0:T(8,128)(2,1)S(1)}, u32[]{:S(2)}, u32[]{:S(2)}) async-start(f16[32,2,8,512]{3,2,1,0:T(8,128)(2,1)} %multiply_convert_fusion.1), calls=%async_computation | async-start | bytes 1048576 | tf_op jit(solution)/shard_map/all_to_all | solution.py:29
  66.1 0.7 dynamic-slice_bitcast_fusion.5
  66.9 0.0 copy-start.3
  66.9 0.8 dynamic-slice_bitcast_fusion.3
  67.7 4.8 %collective-permute-start = (f32[3,8,512]{2,1,0:T(8,128)S(1)}, f32[3,8,512]{2,1,0:T(8,128)S(1)}, u32[]{:S(2)}, u32[]{:S(2)}) collective-permute-start(f32[3,8,512]{2,1,0:T(8,128)S(1)} %pad_maximum_fusion.4), channel_id=1, source_target_pairs={{0,1},{1,0},{2,3},{3,2},{4,5},{5,4},{6,7},{7,6},{8,9},{9,8},{10,11... | collective-permute-start | bytes 147464 | tf_op jit(solution)/shard_map/ppermute | solution.py:196
  72.5 0.0 copy-done.2
  72.5 0.7 fusion.19
  75.7 0.9 collective-permute-done
  76.5 1.5 %all-to-all-done = f16[32,2,8,512]{3,2,1,0:T(8,128)(2,1)S(1)} async-done(((f16[32,2,8,512]{3,2,1,0:T(8,128)(2,1)}), f16[32,2,8,512]{3,2,1,0:T(8,128)(2,1)S(1)}, u32[]{:S(2)}, u32[]{:S(2)}) %all-to-all-start) | async-done | bytes 524320 | tf_op jit(solution)/shard_map/all_to_all | solution.py:29
  78.0 0.1 convert_reduce_fusion
  78.2 0.1 reduce-precision_convert_fusion
  78.3 31.1 %all-gather.4 = f16[32,2,3,8,512]{4,3,2,1,0:T(8,128)(2,1)S(1)} all-gather(f16[2,2,3,8,512]{4,3,2,1,0:T(8,128)(2,1)S(1)} %pad_maximum_fusion.1), channel_id=2, replica_groups=mesh['xl'=2,'y'=4,'c'=2,'z'=16,'xh'=2] {'z'}, dimensions={0}, use_global_device_ids=true | all-gather | bytes 1671168 | tf_op jit(solution)/shard_map/all_gather | solution.py:201
  109.4 0.0 copy-done.3
  109.4 0.1 fusion.7
  109.5 0.1 broadcast_in_dim.2
  109.6 12.9 %all_to_all.10.half_ref = f32[16,3,8,512]{3,2,1,0:T(8,128)S(1)} all-to-all(f32[16,3,8,512]{3,2,1,0:T(8,128)S(1)} %bitcast.79), channel_id=1, replica_groups=mesh['xl'=2,'y'=4,'c'=2,'z'=16,'xh'=2] {'xl','y','xh'}, dimensions={0} | all-to-all | bytes 1572864 | tf_op jit(solution)/shard_map/all_to_all | solution.py:29
  122.4 9.4 %collective-permute-start.2 = (f32[16,3,8,512]{3,2,1,0:T(8,128)S(1)}, f32[16,3,8,512]{3,2,1,0:T(8,128)S(1)}, u32[]{:S(2)}, u32[]{:S(2)}) collective-permute-start(f32[16,3,8,512]{3,2,1,0:T(8,128)S(1)} %all_to_all.10.half_ref), channel_id=1, source_target_pairs={{0,32},{32,0},{1,33},{33,1},{2,34},{34,2},{3,35},{35,3},{4,36},{36... | collective-permute-start | bytes 2359304 | tf_op jit(solution)/shard_map/ppermute | solution.py:212
  131.9 1.9 %collective-permute-done.2.sibling_ref = f32[16,3,8,512]{3,2,1,0:T(8,128)S(1)} collective-permute-done((f32[16,3,8,512]{3,2,1,0:T(8,128)S(1)}, f32[16,3,8,512]{3,2,1,0:T(8,128)S(1)}, u32[]{:S(2)}, u32[]{:S(2)}) %collective-permute-start.2) | collective-permute-done | bytes 786464 | tf_op jit(solution)/shard_map/ppermute | solution.py:212
  133.8 1.2 shard_map.96
  (8 shorter events, 0.1 us)
Async XLA Ops:
  0.6 7.6 %copy-start.1 = (bf16[112,512]{1,0:T(8,128)(2,1)S(1)}, bf16[112,512]{1,0:T(8,128)(2,1)}, u32[]{:S(2)}) copy-start(bf16[112,512]{1,0:T(8,128)(2,1)} %param.8) | copy-start | bytes 344068
  2.7 47.7 %collective-permute-start.1 = (bf16[16,112,256]{2,1,0:T(8,128)(2,1)}, bf16[16,112,256]{2,1,0:T(8,128)(2,1)S(1)}, u32[]{:S(2)}, u32[]{:S(2)}) collective-permute-start(bf16[16,112,256]{2,1,0:T(8,128)(2,1)} %shard_map.94), channel_id=1, source_target_pairs={{0,1},{1,0},{2,3},{3,2},{4,5},{5,4},{6,7},{7,6},{8,9},{9,8},{10,11... | collective-permute-start | bytes 2752520 | tf_op jit(solution)/shard_map/ppermute | solution.py:172
  50.0 1.5 %copy-start = (bf16[3584,256]{1,0:T(8,128)(2,1)S(1)}, bf16[3584,256]{1,0:T(8,128)(2,1)}, u32[]{:S(2)}) copy-start(bf16[3584,256]{1,0:T(8,128)(2,1)} %param.7) | copy-start | bytes 5505028
  52.9 19.6 %copy-start.2 = (s32[32]{0:T(128)S(1)}, s32[32]{0:T(128)}, u32[]{:S(2)}) copy-start(s32[32]{0:T(128)} %param.9) | copy-start | bytes 388
  53.8 24.2 %all-to-all-start = ((f16[32,2,8,512]{3,2,1,0:T(8,128)(2,1)}), f16[32,2,8,512]{3,2,1,0:T(8,128)(2,1)S(1)}, u32[]{:S(2)}, u32[]{:S(2)}) async-start(f16[32,2,8,512]{3,2,1,0:T(8,128)(2,1)} %multiply_convert_fusion.1), calls=%async_computation | async-start | bytes 1048576 | tf_op jit(solution)/shard_map/all_to_all | solution.py:29
  66.9 42.5 %copy-start.3 = (f32[3]{0:T(128)S(1)}, f32[3]{0:T(128)}, u32[]{:S(2)}) copy-start(f32[3]{0:T(128)} %constant.152.clone) | copy-start | bytes 40
  67.7 8.9 %collective-permute-start = (f32[3,8,512]{2,1,0:T(8,128)S(1)}, f32[3,8,512]{2,1,0:T(8,128)S(1)}, u32[]{:S(2)}, u32[]{:S(2)}) collective-permute-start(f32[3,8,512]{2,1,0:T(8,128)S(1)} %pad_maximum_fusion.4), channel_id=1, source_target_pairs={{0,1},{1,0},{2,3},{3,2},{4,5},{5,4},{6,7},{7,6},{8,9},{9,8},{10,11... | collective-permute-start | bytes 147464 | tf_op jit(solution)/shard_map/ppermute | solution.py:196
  122.4 11.3 %collective-permute-start.2 = (f32[16,3,8,512]{3,2,1,0:T(8,128)S(1)}, f32[16,3,8,512]{3,2,1,0:T(8,128)S(1)}, u32[]{:S(2)}, u32[]{:S(2)}) collective-permute-start(f32[16,3,8,512]{3,2,1,0:T(8,128)S(1)} %all_to_all.10.half_ref), channel_id=1, source_target_pairs={{0,32},{32,0},{1,33},{33,1},{2,34},{34,2},{3,35},{35,3},{4,36},{36... | collective-permute-start | bytes 2359304 | tf_op jit(solution)/shard_map/ppermute | solution.py:212

commit v10 on v8

--- a/solution.py
+++ b/solution.py
@@ -13,9 +13,10 @@
 correct_first = 1.0 - 0.9**10
 correct_second = 1.0 - 0.95**10
 
-PARTS = (("xl", 2), ("y", 4), ("c", 2), ("z", 16), ("xh", 2))
+PARTS = (("xl", 2), ("y", 4), ("c", 2), ("zb", 4), ("za", 4), ("xh", 2))
 DP = ("xl", "y", "c")
-FSDP = ("z", "xh")
+FSDP = ("zb", "za", "xh")
+Z = ("zb", "za")
 CHIPS = ("xl", "y", "xh")
 PLANE = ("c", "xl", "y", "xh")
 SWAP = [(0, 1), (1, 0)]
@@ -110,22 +111,30 @@
     return tuple(item.reshape(256, 512) for item in outs)
 
 
-def pick_kernel(partners_ref, spread_ref, out_ref):
-    for j in range(32):
-        out_ref[j] = spread_ref[partners_ref[j]]
-
-
-def pick_blocks(spread, partners):
+def offer_kernel(group_ref, partners_ref, held_ref, out_ref):
+    for i in range(8):
+        partner = partners_ref[8 * group_ref[0] + i]
+        out_ref[i] = held_ref[2 * (partner >> 3) + (partner & 1)]
+
+
+def take_kernel(place_ref, partners_ref, offered_ref, out_ref):
+    for i in range(2):
+        partner = partners_ref[2 * place_ref[0] + i]
+        block = offered_ref[(partner >> 1) & 3, i]
+        for k in range(8):
+            out_ref[k, i] = block
+
+
+def pick_blocks(kernel, position, partners, source, shape):
+    in_smem = pl.BlockSpec(memory_space=pltpu.SMEM)
+    in_vmem = pl.BlockSpec(memory_space=pltpu.VMEM)
     return pl.pallas_call(
-        pick_kernel,
-        out_shape=jax.ShapeDtypeStruct(spread.shape, spread.dtype),
-        in_specs=[
-            pl.BlockSpec(memory_space=pltpu.SMEM),
-            pl.BlockSpec(memory_space=pltpu.VMEM),
-        ],
-        out_specs=pl.BlockSpec(memory_space=pltpu.VMEM),
+        kernel,
+        out_shape=jax.ShapeDtypeStruct(shape, source.dtype),
+        in_specs=[in_smem, in_smem, in_vmem],
+        out_specs=in_vmem,
         compiler_params=pltpu.CompilerParams(vmem_limit_bytes=40 * 1024 * 1024),
-    )(partners, spread)
+    )(position.reshape(1), partners, source)
 
 
 def on_device(activations, key_grads, partners, master_weight, first_moment, second_moment):
@@ -153,30 +162,25 @@
         )
 
     scaled = (key_grads.astype(jnp.float32) * KEY_SCALE).astype(jnp.float16)
-    cotangents = lax.all_gather(scaled, "z", axis=0, tiled=True)
+    cotangents = lax.all_gather(scaled, Z, axis=0, tiled=True)
     cotangents = (cotangents.astype(jnp.float32) * (1.0 / KEY_SCALE)).astype(jnp.bfloat16)
 
     partial = products(mine, tokens, got.reshape(1792, 256), cotangents)
-    states, partial = lax.optimization_barrier(
-        ((master_weight, first_moment, second_moment), partial)
-    )
+    states = (master_weight, first_moment, second_moment)
     pieces = exchange((partial * PARTIAL_SCALE).astype(jnp.float16), PLANE)
     gradient = jnp.sum(pieces.astype(jnp.float32), axis=0) * (1.0 / PARTIAL_SCALE)
 
     own_rows = eight(mine, states)
     peer_rows = lax.ppermute(eight(other, states), "xh", SWAP)
     old = jnp.stack(by_block(own_rows, peer_rows), axis=1)
-    new = jnp.stack(adam_update(old[0], old[1], old[2], gradient))
-
-    pieces = new.reshape(3, 2, 8, 2, 2, 128).transpose(2, 3, 1, 0, 4, 5).reshape(16, 2, 6, 128)
-    pieces = jnp.pad(pieces, ((0, 0), (0, 0), (0, 2), (0, 0))).reshape(16, 16, 128)
-    spread = exchange(pieces, "z").reshape(32, 8, 128)
-    picked = pick_blocks(spread, partners).reshape(16, 16, 128)
-    arrived = exchange(picked, "z").reshape(16, 2, 8, 128)[:, :, :6]
-    placed = arrived.reshape(8, 2, 2, 3, 2, 128).transpose(2, 3, 0, 1, 4, 5)
-
-    placed = placed.reshape(1, 2, 3, 8, 512)
-    half = exchange(jnp.broadcast_to(placed, (8, 2, 3, 8, 512)).reshape(16, 3, 8, 512), CHIPS)
+    results = jnp.stack(adam_update(old[0], old[1], old[2], gradient), axis=1)
+
+    held = lax.all_gather(results.reshape(2, 24, 512), "zb", axis=0, tiled=True)
+    offers = pick_blocks(offer_kernel, lax.axis_index("zb"), partners, held, (8, 24, 512))
+    offered = exchange(offers.reshape(4, 2, 24, 512), "za")
+    placed = pick_blocks(take_kernel, lax.axis_index(Z), partners, offered, (8, 2, 24, 512))
+
+    half = exchange(placed.reshape(16, 3, 8, 512), CHIPS)
     sibling = lax.ppermute(half, "c", SWAP)
     return assemble(core, half, sibling)
 

time: 139 us -> 142 us (1.022)
  waiting for transfers between devices: 7.47 us -> 18.3 us
  blocking collectives: 91.2 us -> 80.7 us
  starting transfers between devices: 29.3 us -> 31.1 us
    all_to_all x3 -> x1, blocking collectives: 49.4 us -> 16.1 us  [exchange(): return lax.all_to_all(array, axes, split_axis=0, concat_axis=0, tiled=True)]
    all_gather x1 -> x2, blocking collectives: 41.7 us -> 64.6 us  [the longest x1 41.7 us: on_device(): cotangents = lax.all_gather(scaled, Z, axis=0, tiled=True)]
    all_to_all x1 -> x2, waiting for transfers between devices: 1.49 us -> 12.3 us  [exchange(): return lax.all_to_all(array, axes, split_axis=0, concat_axis=0, tiled=True)]
    all_to_all x1 -> x2, starting transfers between devices: 12.4 us -> 15.8 us  [exchange(): return lax.all_to_all(array, axes, split_axis=0, concat_axis=0, tiled=True)]
    ppermute x1, starting transfers between devices: 6.64 us -> 4.98 us  [on_device(): sibling = lax.ppermute(half, 'c', SWAP)]
  transfers between devices with their start and end apart: 4 -> 5, of which waited for: 3 -> 4; matrix products, arithmetic and copies ran while one was open for 1% -> 1% of each run, Pallas kernels for 0% -> 0%
where the time goes in v10:
time: 142 us
  blocking collectives  80.7 us (57%)
  starting transfers between devices  31.1 us (22%)
  waiting for transfers between devices  18.3 us (13%)
  local copies, waits for them, and re-layouts  4.83 us (3%)
  Pallas kernels  4.52 us (3%)
  other arithmetic  1.5 us (1%)
    all_gather x1, blocking collectives, on_device(): cotangents = lax.all_gather(scaled, Z, axis=0, tiled=True)  41.7 us
    all_gather x1, blocking collectives, on_device(): held = lax.all_gather(results.reshape(2, 24, 512), 'zb', axis=0, tiled=True)  22.9 us
    all_to_all x1, blocking collectives, exchange(): return lax.all_to_all(array, axes, split_axis=0, concat_axis=0, tiled=True)  16.1 us
    all_to_all x2, starting transfers between devices, exchange(): return lax.all_to_all(array, axes, split_axis=0, concat_axis=0, tiled=True)  15.8 us
    all_to_all x2, waiting for transfers between devices, exchange(): return lax.all_to_all(array, axes, split_axis=0, concat_axis=0, tiled=True)  12.3 us
    ppermute x1, starting transfers between devices, on_device(): got = lax.ppermute(pick(tokens, other, 1), 'xh', SWAP)  5.47 us
    ppermute x1, starting transfers between devices, on_device(): sibling = lax.ppermute(half, 'c', SWAP)  4.98 us
    ppermute x1, starting transfers between devices, on_device(): peer_rows = lax.ppermute(eight(other, states), 'xh', SWAP)  4.79 us
  transfers between devices with their start and end apart: 5, of which 4 were waited for; matrix products, arithmetic and copies ran while one was open for 1% of the time, Pallas kernels for 0%

profile of v10, /device:TPU:1, one launch (start us, length us, event | category | flops | bytes accessed | tf_op | source)
XLA Modules:
  0.0 141.7 jit_solution(16988071973321145942)
XLA Ops:
  0.6 0.0 copy-start.2
  0.6 2.2 %dynamic-slice_bitcast_fusion = bf16[16,112,256]{2,1,0:T(8,128)(2,1)} fusion(bf16[16,2,112,256]{3,2,1,0:T(8,128)(2,1)} %bitcast.73, s32[]{:T(128)S(6)} %sub.13), kind=kLoop, calls=%fused_computation.3 | loop fusion | bytes 1835012 | tf_op jit(solution)/shard_map/jit(dynamic_index_in_dim)/squeeze | solution.py:32
  2.8 5.5 %collective-permute-start.1 = (bf16[16,112,256]{2,1,0:T(8,128)(2,1)}, bf16[16,112,256]{2,1,0:T(8,128)(2,1)S(1)}, u32[]{:S(2)}, u32[]{:S(2)}) collective-permute-start(bf16[16,112,256]{2,1,0:T(8,128)(2,1)} %dynamic-slice_bitcast_fusion), channel_id=1, source_target_pairs={{0,1},{1,0},{2,3},{3,2},{4,5},{5,4},{6,7},{7,6},{8,9},{9,8},{10,11... | collective-permute-start | bytes 2752520 | tf_op jit(solution)/shard_map/ppermute | solution.py:150
  8.3 0.0 copy-done.2
  8.4 41.7 %all-gather.1 = f16[1792,512]{1,0:T(8,128)(2,1)S(1)} all-gather(f16[112,512]{1,0:T(8,128)(2,1)S(1)} %multiply_convert_fusion.2), channel_id=1, replica_groups=mesh['xl'=2,'y'=4,'c'=2,'zb'=4,'za'=4,'xh'=2] {'zb','za'}, dimensions={0}, use_global_device_ids=true | all-gather | bytes 1949696 | tf_op jit(solution)/shard_map/all_gather | solution.py:165
  50.1 0.0 copy-start
  50.1 0.4 multiply_convert_fusion.cotangents_ref
  50.5 0.0 collective-permute-done.1
  50.5 1.1 copy-done
  51.6 1.4 %shard_map.85 = f32[32,2,8,512]{3,2,1,0:T(8,128)S(1)} custom-call(s32[1]{0:T(128)} %bitcast.14.mine_ref, bf16[16,2,112,256]{3,2,1,0:T(8,128)(2,1)S(1)} %bitcast.74, bf16[1792,256]{1,0:T(8,128)(2,1)S(1)} %bitcast.76, bf16[1792,512]{1,0:T(8,128)(2,1)S(1)} %multiply_convert_fusion.cotangents_ref), custom_call_target="tpu_custom_call" | custom-call | flops 939524096 | bytes 6291456 | tf_op jit(solution)/shard_map/pallas_call | solution.py:65
  53.0 0.9 multiply_convert_fusion.1
  54.0 0.0 copy-start.1
  54.0 12.4 %all-to-all-start = ((f16[32,2,8,512]{3,2,1,0:T(8,128)(2,1)}), f16[32,2,8,512]{3,2,1,0:T(8,128)(2,1)S(1)}, u32[]{:S(2)}, u32[]{:S(2)}) async-start(f16[32,2,8,512]{3,2,1,0:T(8,128)(2,1)} %multiply_convert_fusion.1), calls=%async_computation | async-start | bytes 1048576 | tf_op jit(solution)/shard_map/all_to_all | solution.py:28
  66.4 0.7 dynamic-slice_bitcast_fusion.6
  67.1 0.8 dynamic-slice_bitcast_fusion.4
  67.9 4.8 %collective-permute-start = (f32[3,8,512]{2,1,0:T(8,128)S(1)}, f32[3,8,512]{2,1,0:T(8,128)S(1)}, u32[]{:S(2)}, u32[]{:S(2)}) collective-permute-start(f32[3,8,512]{2,1,0:T(8,128)S(1)} %pad_maximum_fusion.1), channel_id=1, source_target_pairs={{0,1},{1,0},{2,3},{3,2},{4,5},{5,4},{6,7},{7,6},{8,9},{9,8},{10,11... | collective-permute-start | bytes 147464 | tf_op jit(solution)/shard_map/ppermute | solution.py:174
  72.7 4.1 %collective-permute-done = f32[3,8,512]{2,1,0:T(8,128)S(1)} collective-permute-done((f32[3,8,512]{2,1,0:T(8,128)S(1)}, f32[3,8,512]{2,1,0:T(8,128)S(1)}, u32[]{:S(2)}, u32[]{:S(2)}) %collective-permute-start) | collective-permute-done | bytes 49184 | tf_op jit(solution)/shard_map/ppermute | solution.py:174
  76.8 1.5 %all-to-all-done = f16[32,2,8,512]{3,2,1,0:T(8,128)(2,1)S(1)} async-done(((f16[32,2,8,512]{3,2,1,0:T(8,128)(2,1)}), f16[32,2,8,512]{3,2,1,0:T(8,128)(2,1)S(1)}, u32[]{:S(2)}, u32[]{:S(2)}) %all-to-all-start) | async-done | bytes 524320 | tf_op jit(solution)/shard_map/all_to_all | solution.py:28
  78.3 0.1 convert_reduce_fusion
  78.4 22.9 %all_gather.7.held_ref = f32[8,24,512]{2,1,0:T(8,128)S(1)} all-gather(f32[2,24,512]{2,1,0:T(8,128)S(1)} %maximum_bitcast_fusion), channel_id=1, replica_groups=mesh['xl'=2,'y'=4,'c'=2,'zb'=4,'za'=4,'xh'=2] {'zb'}, dimensions={0}, use_global_device_ids=true | all-gather | bytes 491520 | tf_op jit(solution)/shard_map/all_gather | solution.py:178
  101.3 0.0 copy-done.1
  101.3 1.3 shard_map.86
  102.6 3.5 %all-to-all-start.1 = ((f32[4,2,24,512]{3,2,1,0:T(8,128)}), f32[4,2,24,512]{3,2,1,0:T(8,128)S(1)}, u32[]{:S(2)}, u32[]{:S(2)}) async-start(f32[4,2,24,512]{3,2,1,0:T(8,128)} %bitcast.26), calls=%async_computation.1 | async-start | bytes 786432 | tf_op jit(solution)/shard_map/all_to_all | solution.py:28
  106.1 10.8 %all-to-all-done.1.offered_ref = f32[4,2,24,512]{3,2,1,0:T(8,128)S(1)} async-done(((f32[4,2,24,512]{3,2,1,0:T(8,128)}), f32[4,2,24,512]{3,2,1,0:T(8,128)S(1)}, u32[]{:S(2)}, u32[]{:S(2)}) %all-to-all-start.1) | async-done | bytes 393248 | tf_op jit(solution)/shard_map/all_to_all | solution.py:28
  117.0 0.6 shard_map.87
  117.6 16.1 %all_to_all.15.half_ref = f32[16,3,8,512]{3,2,1,0:T(8,128)S(1)} all-to-all(f32[16,3,8,512]{3,2,1,0:T(8,128)S(1)} %bitcast.75), channel_id=1, replica_groups=mesh['xl'=2,'y'=4,'c'=2,'zb'=4,'za'=4,'xh'=2] {'xl','y','xh'}, dimensions={0} | all-to-all | bytes 1572864 | tf_op jit(solution)/shard_map/all_to_all | solution.py:28
  133.6 5.0 %collective-permute-start.2 = (f32[16,3,8,512]{3,2,1,0:T(8,128)S(1)}, f32[16,3,8,512]{3,2,1,0:T(8,128)S(1)}, u32[]{:S(2)}, u32[]{:S(2)}) collective-permute-start(f32[16,3,8,512]{3,2,1,0:T(8,128)S(1)} %all_to_all.15.half_ref), channel_id=1, source_target_pairs={{0,32},{32,0},{1,33},{33,1},{2,34},{34,2},{3,35},{35,3},{4,36},{36... | collective-permute-start | bytes 2359304 | tf_op jit(solution)/shard_map/ppermute | solution.py:184
  138.6 1.9 %collective-permute-done.2.sibling_ref = f32[16,3,8,512]{3,2,1,0:T(8,128)S(1)} collective-permute-done((f32[16,3,8,512]{3,2,1,0:T(8,128)S(1)}, f32[16,3,8,512]{3,2,1,0:T(8,128)S(1)}, u32[]{:S(2)}, u32[]{:S(2)}) %collective-permute-start.2) | collective-permute-done | bytes 786464 | tf_op jit(solution)/shard_map/ppermute | solution.py:184
  140.5 1.2 shard_map.88
  (6 shorter events, 0.1 us)
Async XLA Ops:
  0.6 7.7 %copy-start.2 = (bf16[112,512]{1,0:T(8,128)(2,1)S(1)}, bf16[112,512]{1,0:T(8,128)(2,1)}, u32[]{:S(2)}) copy-start(bf16[112,512]{1,0:T(8,128)(2,1)} %param.7) | copy-start | bytes 344068
  2.8 47.6 %collective-permute-start.1 = (bf16[16,112,256]{2,1,0:T(8,128)(2,1)}, bf16[16,112,256]{2,1,0:T(8,128)(2,1)S(1)}, u32[]{:S(2)}, u32[]{:S(2)}) collective-permute-start(bf16[16,112,256]{2,1,0:T(8,128)(2,1)} %dynamic-slice_bitcast_fusion), channel_id=1, source_target_pairs={{0,1},{1,0},{2,3},{3,2},{4,5},{5,4},{6,7},{7,6},{8,9},{9,8},{10,11... | collective-permute-start | bytes 2752520 | tf_op jit(solution)/shard_map/ppermute | solution.py:150
  50.1 1.5 %copy-start = (bf16[3584,256]{1,0:T(8,128)(2,1)S(1)}, bf16[3584,256]{1,0:T(8,128)(2,1)}, u32[]{:S(2)}) copy-start(bf16[3584,256]{1,0:T(8,128)(2,1)} %param.6) | copy-start | bytes 5505028
  54.0 47.4 %copy-start.1 = (s32[32]{0:T(128)S(1)}, s32[32]{0:T(128)}, u32[]{:S(2)}) copy-start(s32[32]{0:T(128)} %partners_ref.3) | copy-start | bytes 388
  54.0 24.3 %all-to-all-start = ((f16[32,2,8,512]{3,2,1,0:T(8,128)(2,1)}), f16[32,2,8,512]{3,2,1,0:T(8,128)(2,1)S(1)}, u32[]{:S(2)}, u32[]{:S(2)}) async-start(f16[32,2,8,512]{3,2,1,0:T(8,128)(2,1)} %multiply_convert_fusion.1), calls=%async_computation | async-start | bytes 1048576 | tf_op jit(solution)/shard_map/all_to_all | solution.py:28
  67.9 8.9 %collective-permute-start = (f32[3,8,512]{2,1,0:T(8,128)S(1)}, f32[3,8,512]{2,1,0:T(8,128)S(1)}, u32[]{:S(2)}, u32[]{:S(2)}) collective-permute-start(f32[3,8,512]{2,1,0:T(8,128)S(1)} %pad_maximum_fusion.1), channel_id=1, source_target_pairs={{0,1},{1,0},{2,3},{3,2},{4,5},{5,4},{6,7},{7,6},{8,9},{9,8},{10,11... | collective-permute-start | bytes 147464 | tf_op jit(solution)/shard_map/ppermute | solution.py:174
  102.6 14.3 %all-to-all-start.1 = ((f32[4,2,24,512]{3,2,1,0:T(8,128)}), f32[4,2,24,512]{3,2,1,0:T(8,128)S(1)}, u32[]{:S(2)}, u32[]{:S(2)}) async-start(f32[4,2,24,512]{3,2,1,0:T(8,128)} %bitcast.26), calls=%async_computation.1 | async-start | bytes 786432 | tf_op jit(solution)/shard_map/all_to_all | solution.py:28
  133.6 6.9 %collective-permute-start.2 = (f32[16,3,8,512]{3,2,1,0:T(8,128)S(1)}, f32[16,3,8,512]{3,2,1,0:T(8,128)S(1)}, u32[]{:S(2)}, u32[]{:S(2)}) collective-permute-start(f32[16,3,8,512]{3,2,1,0:T(8,128)S(1)} %all_to_all.15.half_ref), channel_id=1, source_target_pairs={{0,32},{32,0},{1,33},{33,1},{2,34},{34,2},{3,35},{35,3},{4,36},{36... | collective-permute-start | bytes 2359304 | tf_op jit(solution)/shard_map/ppermute | solution.py:184

commit v11 on v5

--- a/solution.py
+++ b/solution.py
@@ -149,10 +149,9 @@
 
     scaled = (key_grads.astype(jnp.float32) * KEY_SCALE).astype(jnp.float16)
     cotangents = lax.all_gather(scaled, "z", axis=0, tiled=True)
-    own_rows, outgoing, cotangents = lax.optimization_barrier(
-        (eight(mine), eight(other), cotangents)
-    )
-    peer_rows = lax.ppermute(outgoing, "xh", SWAP)
+    got, cotangents = lax.optimization_barrier((got, cotangents))
+    own_rows = eight(mine)
+    peer_rows = lax.ppermute(eight(other), "xh", SWAP)
     cotangents = (cotangents.astype(jnp.float32) * (1.0 / KEY_SCALE)).astype(jnp.bfloat16)
 
     partial = products(mine, tokens, got.reshape(1792, 256), cotangents)

time: 136 us -> 135 us (level)
  waiting for transfers between devices: 5.78 us -> 4.25 us
    ppermute x1, waiting for transfers between devices: 2.39 us -> 0.86 us  [on_device(): peer_rows = lax.ppermute(eight(other), 'xh', SWAP)]
where the time goes in v11:
time: 135 us; the launch traced here: 134 us
  blocking collectives  85.7 us (63%)
  starting transfers between devices  32 us (24%)
  local copies, waits for them, and re-layouts  4.58 us (3%)
  waiting for transfers between devices  4.25 us (3%)
  between operations  3.38 us (3%)
  Pallas kernels  2.6 us (2%)
  other arithmetic  1.74 us (1%)
    all_gather x1, blocking collectives, on_device(): cotangents = lax.all_gather(scaled, 'z', axis=0, tiled=True)  41.7 us
    all_gather x1, blocking collectives, on_device(): along = lax.all_gather(split_halves(slices), 'z', axis=0, tiled=False)  31.1 us
    all_to_all x1, blocking collectives, exchange(): return lax.all_to_all(array, axes, split_axis=0, concat_axis=0, tiled=True)  12.9 us
    all_to_all x1, starting transfers between devices, exchange(): return lax.all_to_all(array, axes, split_axis=0, concat_axis=0, tiled=True)  12.3 us
    ppermute x1, starting transfers between devices, on_device(): sibling = lax.ppermute(half, 'c', SWAP)  9.45 us
    ppermute x1, starting transfers between devices, on_device(): got = lax.ppermute(pick(tokens, other, 1), 'xh', SWAP)  5.48 us
    ppermute x1, starting transfers between devices, on_device(): peer_rows = lax.ppermute(eight(other), 'xh', SWAP)  4.79 us
  transfers between devices with their start and end apart: 4, of which 3 were waited for; matrix products, arithmetic and copies ran while one was open for 2% of the time, Pallas kernels for 0%

profile of v11, /device:TPU:1, one launch (start us, length us, event | category | flops | bytes accessed | tf_op | source)
XLA Modules:
  0.0 134.2 jit_solution(15025903176542313123)
XLA Ops:
  0.6 0.0 copy-start.1
  0.6 1.3 dynamic-slice_bitcast_fusion
  1.9 5.5 %collective-permute-start.1 = (bf16[16,112,256]{2,1,0:T(8,128)(2,1)S(1)}, bf16[16,112,256]{2,1,0:T(8,128)(2,1)S(1)}, u32[]{:S(2)}, u32[]{:S(2)}) collective-permute-start(bf16[16,112,256]{2,1,0:T(8,128)(2,1)S(1)} %dynamic-slice_bitcast_fusion), channel_id=1, source_target_pairs={{0,1},{1,0},{2,3},{3,2},{4,5},{5,4},{6,7},{7,6},{8,9},{9,8},{10,11... | collective-permute-start | bytes 2752520 | tf_op jit(solution)/shard_map/ppermute | solution.py:136
  7.4 0.0 copy-done.1
  7.5 41.7 %all-gather.3 = f16[1792,512]{1,0:T(8,128)(2,1)S(1)} all-gather(f16[112,512]{1,0:T(8,128)(2,1)S(1)} %multiply_convert_fusion.2), channel_id=1, replica_groups=mesh['xl'=2,'y'=4,'c'=2,'z'=16,'xh'=2] {'z'}, dimensions={0}, use_global_device_ids=true | all-gather | bytes 1949696 | tf_op jit(solution)/shard_map/all_gather | solution.py:151
  49.2 0.0 copy-start
  49.2 0.0 collective-permute-done.1
  49.2 0.4 multiply_convert_fusion.cotangents_ref
  49.6 1.1 copy-done
  50.7 1.4 %shard_map.94 = f32[32,2,8,512]{3,2,1,0:T(8,128)S(1)} custom-call(s32[1]{0:T(128)} %bitcast.12.mine_ref, bf16[16,2,112,256]{3,2,1,0:T(8,128)(2,1)S(1)} %bitcast.78, bf16[1792,256]{1,0:T(8,128)(2,1)S(1)} %bitcast.79, bf16[1792,512]{1,0:T(8,128)(2,1)S(1)} %multiply_convert_fusion.cotangents_ref), custom_call_target="tpu_custom_call" | custom-call | flops 939524096 | bytes 6291456 | tf_op jit(solution)/shard_map/pallas_call | solution.py:77
  52.1 0.0 copy-start.2
  52.1 0.9 multiply_convert_fusion.1
  53.1 12.3 %all-to-all-start = ((f16[32,2,8,512]{3,2,1,0:T(8,128)(2,1)}), f16[32,2,8,512]{3,2,1,0:T(8,128)(2,1)S(1)}, u32[]{:S(2)}, u32[]{:S(2)}) async-start(f16[32,2,8,512]{3,2,1,0:T(8,128)(2,1)} %multiply_convert_fusion.1), calls=%async_computation | async-start | bytes 1048576 | tf_op jit(solution)/shard_map/all_to_all | solution.py:29
  65.3 0.7 dynamic-slice_bitcast_fusion.6
  66.1 0.0 copy-start.3
  66.1 0.8 dynamic-slice_bitcast_fusion.4
  66.9 4.8 %collective-permute-start = (f32[3,8,512]{2,1,0:T(8,128)S(1)}, f32[3,8,512]{2,1,0:T(8,128)S(1)}, u32[]{:S(2)}, u32[]{:S(2)}) collective-permute-start(f32[3,8,512]{2,1,0:T(8,128)S(1)} %pad_maximum_fusion.4), channel_id=1, source_target_pairs={{0,1},{1,0},{2,3},{3,2},{4,5},{5,4},{6,7},{7,6},{8,9},{9,8},{10,11... | collective-permute-start | bytes 147464 | tf_op jit(solution)/shard_map/ppermute | solution.py:154
  71.7 0.0 copy-done.2
  71.7 0.6 fusion.19
  74.9 0.9 collective-permute-done
  75.8 1.5 %all-to-all-done = f16[32,2,8,512]{3,2,1,0:T(8,128)(2,1)S(1)} async-done(((f16[32,2,8,512]{3,2,1,0:T(8,128)(2,1)}), f16[32,2,8,512]{3,2,1,0:T(8,128)(2,1)S(1)}, u32[]{:S(2)}, u32[]{:S(2)}) %all-to-all-start) | async-done | bytes 524320 | tf_op jit(solution)/shard_map/all_to_all | solution.py:29
  77.3 0.1 convert_reduce_fusion
  77.4 0.1 reduce-precision_convert_fusion
  77.5 31.1 %all-gather.4 = f16[32,2,3,8,512]{4,3,2,1,0:T(8,128)(2,1)S(1)} all-gather(f16[2,2,3,8,512]{4,3,2,1,0:T(8,128)(2,1)S(1)} %pad_maximum_fusion.1), channel_id=2, replica_groups=mesh['xl'=2,'y'=4,'c'=2,'z'=16,'xh'=2] {'z'}, dimensions={0}, use_global_device_ids=true | all-gather | bytes 1671168 | tf_op jit(solution)/shard_map/all_gather | solution.py:165
  108.6 0.0 copy-done.3
  108.6 0.1 fusion.7
  108.7 0.1 broadcast_in_dim.2
  108.8 12.9 %all_to_all.10.half_ref = f32[16,3,8,512]{3,2,1,0:T(8,128)S(1)} all-to-all(f32[16,3,8,512]{3,2,1,0:T(8,128)S(1)} %bitcast.80), channel_id=1, replica_groups=mesh['xl'=2,'y'=4,'c'=2,'z'=16,'xh'=2] {'xl','y','xh'}, dimensions={0} | all-to-all | bytes 1572864 | tf_op jit(solution)/shard_map/all_to_all | solution.py:29
  121.7 9.4 %collective-permute-start.2 = (f32[16,3,8,512]{3,2,1,0:T(8,128)S(1)}, f32[16,3,8,512]{3,2,1,0:T(8,128)S(1)}, u32[]{:S(2)}, u32[]{:S(2)}) collective-permute-start(f32[16,3,8,512]{3,2,1,0:T(8,128)S(1)} %all_to_all.10.half_ref), channel_id=1, source_target_pairs={{0,32},{32,0},{1,33},{33,1},{2,34},{34,2},{3,35},{35,3},{4,36},{36... | collective-permute-start | bytes 2359304 | tf_op jit(solution)/shard_map/ppermute | solution.py:176
  131.1 1.9 %collective-permute-done.2.sibling_ref = f32[16,3,8,512]{3,2,1,0:T(8,128)S(1)} collective-permute-done((f32[16,3,8,512]{3,2,1,0:T(8,128)S(1)}, f32[16,3,8,512]{3,2,1,0:T(8,128)S(1)}, u32[]{:S(2)}, u32[]{:S(2)}) %collective-permute-start.2) | collective-permute-done | bytes 786464 | tf_op jit(solution)/shard_map/ppermute | solution.py:176
  133.0 1.2 shard_map.95
  (8 shorter events, 0.1 us)
Async XLA Ops:
  0.6 6.8 %copy-start.1 = (bf16[112,512]{1,0:T(8,128)(2,1)S(1)}, bf16[112,512]{1,0:T(8,128)(2,1)}, u32[]{:S(2)}) copy-start(bf16[112,512]{1,0:T(8,128)(2,1)} %param.8) | copy-start | bytes 344068
  1.9 47.3 %collective-permute-start.1 = (bf16[16,112,256]{2,1,0:T(8,128)(2,1)S(1)}, bf16[16,112,256]{2,1,0:T(8,128)(2,1)S(1)}, u32[]{:S(2)}, u32[]{:S(2)}) collective-permute-start(bf16[16,112,256]{2,1,0:T(8,128)(2,1)S(1)} %dynamic-slice_bitcast_fusion), channel_id=1, source_target_pairs={{0,1},{1,0},{2,3},{3,2},{4,5},{5,4},{6,7},{7,6},{8,9},{9,8},{10,11... | collective-permute-start | bytes 2752520 | tf_op jit(solution)/shard_map/ppermute | solution.py:136
  49.2 1.5 %copy-start = (bf16[3584,256]{1,0:T(8,128)(2,1)S(1)}, bf16[3584,256]{1,0:T(8,128)(2,1)}, u32[]{:S(2)}) copy-start(bf16[3584,256]{1,0:T(8,128)(2,1)} %param.7) | copy-start | bytes 5505028
  52.1 19.6 %copy-start.2 = (s32[32]{0:T(128)S(1)}, s32[32]{0:T(128)}, u32[]{:S(2)}) copy-start(s32[32]{0:T(128)} %param.9) | copy-start | bytes 388
  53.1 24.2 %all-to-all-start = ((f16[32,2,8,512]{3,2,1,0:T(8,128)(2,1)}), f16[32,2,8,512]{3,2,1,0:T(8,128)(2,1)S(1)}, u32[]{:S(2)}, u32[]{:S(2)}) async-start(f16[32,2,8,512]{3,2,1,0:T(8,128)(2,1)} %multiply_convert_fusion.1), calls=%async_computation | async-start | bytes 1048576 | tf_op jit(solution)/shard_map/all_to_all | solution.py:29
  66.1 42.5 %copy-start.3 = (f32[3]{0:T(128)S(1)}, f32[3]{0:T(128)}, u32[]{:S(2)}) copy-start(f32[3]{0:T(128)} %constant.154.clone) | copy-start | bytes 40
  66.9 8.9 %collective-permute-start = (f32[3,8,512]{2,1,0:T(8,128)S(1)}, f32[3,8,512]{2,1,0:T(8,128)S(1)}, u32[]{:S(2)}, u32[]{:S(2)}) collective-permute-start(f32[3,8,512]{2,1,0:T(8,128)S(1)} %pad_maximum_fusion.4), channel_id=1, source_target_pairs={{0,1},{1,0},{2,3},{3,2},{4,5},{5,4},{6,7},{7,6},{8,9},{9,8},{10,11... | collective-permute-start | bytes 147464 | tf_op jit(solution)/shard_map/ppermute | solution.py:154
  121.7 11.3 %collective-permute-start.2 = (f32[16,3,8,512]{3,2,1,0:T(8,128)S(1)}, f32[16,3,8,512]{3,2,1,0:T(8,128)S(1)}, u32[]{:S(2)}, u32[]{:S(2)}) collective-permute-start(f32[16,3,8,512]{3,2,1,0:T(8,128)S(1)} %all_to_all.10.half_ref), channel_id=1, source_target_pairs={{0,32},{32,0},{1,33},{33,1},{2,34},{34,2},{3,35},{35,3},{4,36},{36... | collective-permute-start | bytes 2359304 | tf_op jit(solution)/shard_map/ppermute | solution.py:176

commit v12 on v11

--- a/solution.py
+++ b/solution.py
@@ -21,6 +21,7 @@
 SWAP = [(0, 1), (1, 0)]
 KEY_SCALE = 2.0**21
 REST_SCALE = 2.0**11
+FIRST_SCALE = 2.0**6
 SECOND_SCALE = 2.0**-6
 PARTIAL_SCALE = 2.0**7
 
@@ -35,15 +36,23 @@
     )
 
 
-def split_halves(values):
-    high = lax.reduce_precision(values, exponent_bits=5, mantissa_bits=10)
-    rest = (values - high) * REST_SCALE
-    return jnp.stack((high.astype(jnp.float16), rest.astype(jnp.float16)))
-
-
-def join_halves(halves):
-    wide = halves.astype(jnp.float32)
-    return wide[0] + wide[1] * (1.0 / REST_SCALE)
+def pack(weight, moment_one, moment_two):
+    high = lax.reduce_precision(weight, exponent_bits=5, mantissa_bits=10)
+    rest = (weight - high) * REST_SCALE
+    return jnp.stack((high, rest, moment_one * FIRST_SCALE, moment_two * SECOND_SCALE)).astype(
+        jnp.float16
+    )
+
+
+def unpack(packed):
+    wide = packed.astype(jnp.float32)
+    return jnp.stack(
+        (
+            wide[0] + wide[1] * (1.0 / REST_SCALE),
+            wide[2] * (1.0 / FIRST_SCALE),
+            wide[3] * (1.0 / SECOND_SCALE),
+        )
+    )
 
 
 def adam_update(weight, first_moment, second_moment, gradient):
@@ -159,17 +168,14 @@
     gradient = jnp.sum(pieces.astype(jnp.float32), axis=0) * (1.0 / PARTIAL_SCALE)
 
     old = jnp.stack(by_block(own_rows, peer_rows), axis=1)
-    weight, moment_one, moment_two = adam_update(old[0], old[1], old[2], gradient)
-
-    slices = jnp.stack((weight, moment_one, moment_two * SECOND_SCALE), axis=1)
-    along = lax.all_gather(split_halves(slices), "z", axis=0, tiled=False)
+    results = adam_update(old[0], old[1], old[2], gradient)
+
+    along = lax.all_gather(pack(*results), "z", axis=0, tiled=False)
     here = 2 * lax.axis_index("z")
-
-    scales = jnp.array([1.0, 1.0, 1.0 / SECOND_SCALE], jnp.float32).reshape(3, 1, 1)
 
     def wanted(index):
         place = pick(partners, index, 0)
-        return join_halves(pick(pick(along, place >> 1, 0), place & 1, 1)) * scales
+        return unpack(pick(pick(along, place >> 1, 0), place & 1, 1))
 
     placed = jnp.stack([wanted(here + i) for i in range(2)]).reshape(1, 2, 3, 8, 512)
     half = exchange(jnp.broadcast_to(placed, (8, 2, 3, 8, 512)).reshape(16, 3, 8, 512), CHIPS)

time: 135 us -> 132 us (0.978)
  blocking collectives: 85.7 us -> 81.4 us
    all_gather x1, blocking collectives: 31.1 us -> 26.8 us  [on_device(): along = lax.all_gather(pack(*results), 'z', axis=0, tiled=False)]
where the time goes in v12:
time: 132 us; the launch traced here: 131 us
  blocking collectives  81.4 us (62%)
  starting transfers between devices  33.2 us (25%)
  local copies, waits for them, and re-layouts  4.61 us (3%)
  waiting for transfers between devices  4.25 us (3%)
  between operations  3.38 us (3%)
  Pallas kernels  2.6 us (2%)
  other arithmetic  1.66 us (1%)
    all_gather x1, blocking collectives, on_device(): cotangents = lax.all_gather(scaled, 'z', axis=0, tiled=True)  41.7 us
    all_gather x1, blocking collectives, on_device(): along = lax.all_gather(pack(*results), 'z', axis=0, tiled=False)  26.8 us
    all_to_all x1, blocking collectives, exchange(): return lax.all_to_all(array, axes, split_axis=0, concat_axis=0, tiled=True)  12.9 us
    all_to_all x1, starting transfers between devices, exchange(): return lax.all_to_all(array, axes, split_axis=0, concat_axis=0, tiled=True)  12.3 us
    ppermute x1, starting transfers between devices, on_device(): sibling = lax.ppermute(half, 'c', SWAP)  10.7 us
    ppermute x1, starting transfers between devices, on_device(): got = lax.ppermute(pick(tokens, other, 1), 'xh', SWAP)  5.48 us
    ppermute x1, starting transfers between devices, on_device(): peer_rows = lax.ppermute(eight(other), 'xh', SWAP)  4.79 us
  transfers between devices with their start and end apart: 4, of which 3 were waited for; matrix products, arithmetic and copies ran while one was open for 2% of the time, Pallas kernels for 0%

profile of v12, /device:TPU:1, one launch (start us, length us, event | category | flops | bytes accessed | tf_op | source)
XLA Modules:
  0.0 131.1 jit_solution(12136586934307245731)
XLA Ops:
  0.6 0.0 copy-start.1
  0.6 1.3 dynamic-slice_bitcast_fusion
  1.9 5.5 %collective-permute-start.1 = (bf16[16,112,256]{2,1,0:T(8,128)(2,1)S(1)}, bf16[16,112,256]{2,1,0:T(8,128)(2,1)S(1)}, u32[]{:S(2)}, u32[]{:S(2)}) collective-permute-start(bf16[16,112,256]{2,1,0:T(8,128)(2,1)S(1)} %dynamic-slice_bitcast_fusion), channel_id=1, source_target_pairs={{0,1},{1,0},{2,3},{3,2},{4,5},{5,4},{6,7},{7,6},{8,9},{9,8},{10,11... | collective-permute-start | bytes 2752520 | tf_op jit(solution)/shard_map/ppermute | solution.py:145
  7.4 0.0 copy-done.1
  7.5 41.7 %all-gather.2 = f16[1792,512]{1,0:T(8,128)(2,1)S(1)} all-gather(f16[112,512]{1,0:T(8,128)(2,1)S(1)} %multiply_convert_fusion.2), channel_id=1, replica_groups=mesh['xl'=2,'y'=4,'c'=2,'z'=16,'xh'=2] {'z'}, dimensions={0}, use_global_device_ids=true | all-gather | bytes 1949696 | tf_op jit(solution)/shard_map/all_gather | solution.py:160
  49.2 0.0 copy-start
  49.2 0.0 collective-permute-done.1
  49.2 0.4 multiply_convert_fusion.cotangents_ref
  49.6 1.1 copy-done
  50.7 1.4 %shard_map.85 = f32[32,2,8,512]{3,2,1,0:T(8,128)S(1)} custom-call(s32[1]{0:T(128)} %bitcast.10.mine_ref, bf16[16,2,112,256]{3,2,1,0:T(8,128)(2,1)S(1)} %bitcast.67, bf16[1792,256]{1,0:T(8,128)(2,1)S(1)} %bitcast.68, bf16[1792,512]{1,0:T(8,128)(2,1)S(1)} %multiply_convert_fusion.cotangents_ref), custom_call_target="tpu_custom_call" | custom-call | flops 939524096 | bytes 6291456 | tf_op jit(solution)/shard_map/pallas_call | solution.py:86
  52.1 0.0 copy-start.2
  52.1 0.9 multiply_convert_fusion.1
  53.1 12.3 %all-to-all-start = ((f16[32,2,8,512]{3,2,1,0:T(8,128)(2,1)}), f16[32,2,8,512]{3,2,1,0:T(8,128)(2,1)S(1)}, u32[]{:S(2)}, u32[]{:S(2)}) async-start(f16[32,2,8,512]{3,2,1,0:T(8,128)(2,1)} %multiply_convert_fusion.1), calls=%async_computation | async-start | bytes 1048576 | tf_op jit(solution)/shard_map/all_to_all | solution.py:30
  65.3 0.7 dynamic-slice_bitcast_fusion.6
  66.1 0.8 dynamic-slice_bitcast_fusion.4
  66.9 4.8 %collective-permute-start = (f32[3,8,512]{2,1,0:T(8,128)S(1)}, f32[3,8,512]{2,1,0:T(8,128)S(1)}, u32[]{:S(2)}, u32[]{:S(2)}) collective-permute-start(f32[3,8,512]{2,1,0:T(8,128)S(1)} %pad_maximum_fusion.3), channel_id=1, source_target_pairs={{0,1},{1,0},{2,3},{3,2},{4,5},{5,4},{6,7},{7,6},{8,9},{9,8},{10,11... | collective-permute-start | bytes 147464 | tf_op jit(solution)/shard_map/ppermute | solution.py:163
  71.7 0.0 copy-done.2
  71.7 0.7 fusion.21
  74.9 0.9 collective-permute-done
  75.8 1.5 %all-to-all-done = f16[32,2,8,512]{3,2,1,0:T(8,128)(2,1)S(1)} async-done(((f16[32,2,8,512]{3,2,1,0:T(8,128)(2,1)}), f16[32,2,8,512]{3,2,1,0:T(8,128)(2,1)S(1)}, u32[]{:S(2)}, u32[]{:S(2)}) %all-to-all-start) | async-done | bytes 524320 | tf_op jit(solution)/shard_map/all_to_all | solution.py:30
  77.3 0.1 convert_reduce_fusion
  77.3 0.1 fusion.11
  77.5 26.8 %all-gather.3 = f16[16,4,2,8,512]{4,3,2,1,0:T(8,128)(2,1)S(1)} all-gather(f16[1,4,2,8,512]{4,3,2,1,0:T(8,128)(2,1)S(1)} %pad_maximum_fusion.1), channel_id=1, replica_groups=mesh['xl'=2,'y'=4,'c'=2,'z'=16,'xh'=2] {'z'}, dimensions={0}, use_global_device_ids=true | all-gather | bytes 1114112 | tf_op jit(solution)/shard_map/all_gather | solution.py:173
  104.4 0.1 broadcast_in_dim.2
  104.4 12.9 %all_to_all.10.half_ref = f32[16,3,8,512]{3,2,1,0:T(8,128)S(1)} all-to-all(f32[16,3,8,512]{3,2,1,0:T(8,128)S(1)} %bitcast.69), channel_id=1, replica_groups=mesh['xl'=2,'y'=4,'c'=2,'z'=16,'xh'=2] {'xl','y','xh'}, dimensions={0} | all-to-all | bytes 1572864 | tf_op jit(solution)/shard_map/all_to_all | solution.py:30
  117.3 10.7 %collective-permute-start.2 = (f32[16,3,8,512]{3,2,1,0:T(8,128)S(1)}, f32[16,3,8,512]{3,2,1,0:T(8,128)S(1)}, u32[]{:S(2)}, u32[]{:S(2)}) collective-permute-start(f32[16,3,8,512]{3,2,1,0:T(8,128)S(1)} %all_to_all.10.half_ref), channel_id=1, source_target_pairs={{0,32},{32,0},{1,33},{33,1},{2,34},{34,2},{3,35},{35,3},{4,36},{36... | collective-permute-start | bytes 2359304 | tf_op jit(solution)/shard_map/ppermute | solution.py:182
  128.0 1.9 %collective-permute-done.2.sibling_ref = f32[16,3,8,512]{3,2,1,0:T(8,128)S(1)} collective-permute-done((f32[16,3,8,512]{3,2,1,0:T(8,128)S(1)}, f32[16,3,8,512]{3,2,1,0:T(8,128)S(1)}, u32[]{:S(2)}, u32[]{:S(2)}) %collective-permute-start.2) | collective-permute-done | bytes 786464 | tf_op jit(solution)/shard_map/ppermute | solution.py:182
  129.9 1.2 shard_map.86
  (12 shorter events, 0.2 us)
Async XLA Ops:
  0.6 6.8 %copy-start.1 = (bf16[112,512]{1,0:T(8,128)(2,1)S(1)}, bf16[112,512]{1,0:T(8,128)(2,1)}, u32[]{:S(2)}) copy-start(bf16[112,512]{1,0:T(8,128)(2,1)} %param.7) | copy-start | bytes 344068
  1.9 47.3 %collective-permute-start.1 = (bf16[16,112,256]{2,1,0:T(8,128)(2,1)S(1)}, bf16[16,112,256]{2,1,0:T(8,128)(2,1)S(1)}, u32[]{:S(2)}, u32[]{:S(2)}) collective-permute-start(bf16[16,112,256]{2,1,0:T(8,128)(2,1)S(1)} %dynamic-slice_bitcast_fusion), channel_id=1, source_target_pairs={{0,1},{1,0},{2,3},{3,2},{4,5},{5,4},{6,7},{7,6},{8,9},{9,8},{10,11... | collective-permute-start | bytes 2752520 | tf_op jit(solution)/shard_map/ppermute | solution.py:145
  49.2 1.5 %copy-start = (bf16[3584,256]{1,0:T(8,128)(2,1)S(1)}, bf16[3584,256]{1,0:T(8,128)(2,1)}, u32[]{:S(2)}) copy-start(bf16[3584,256]{1,0:T(8,128)(2,1)} %param.6) | copy-start | bytes 5505028
  52.1 19.5 %copy-start.2 = (s32[32]{0:T(128)S(1)}, s32[32]{0:T(128)}, u32[]{:S(2)}) copy-start(s32[32]{0:T(128)} %param.8) | copy-start | bytes 388
  53.1 24.2 %all-to-all-start = ((f16[32,2,8,512]{3,2,1,0:T(8,128)(2,1)}), f16[32,2,8,512]{3,2,1,0:T(8,128)(2,1)S(1)}, u32[]{:S(2)}, u32[]{:S(2)}) async-start(f16[32,2,8,512]{3,2,1,0:T(8,128)(2,1)} %multiply_convert_fusion.1), calls=%async_computation | async-start | bytes 1048576 | tf_op jit(solution)/shard_map/all_to_all | solution.py:30
  66.9 8.9 %collective-permute-start = (f32[3,8,512]{2,1,0:T(8,128)S(1)}, f32[3,8,512]{2,1,0:T(8,128)S(1)}, u32[]{:S(2)}, u32[]{:S(2)}) collective-permute-start(f32[3,8,512]{2,1,0:T(8,128)S(1)} %pad_maximum_fusion.3), channel_id=1, source_target_pairs={{0,1},{1,0},{2,3},{3,2},{4,5},{5,4},{6,7},{7,6},{8,9},{9,8},{10,11... | collective-permute-start | bytes 147464 | tf_op jit(solution)/shard_map/ppermute | solution.py:163
  117.3 12.6 %collective-permute-start.2 = (f32[16,3,8,512]{3,2,1,0:T(8,128)S(1)}, f32[16,3,8,512]{3,2,1,0:T(8,128)S(1)}, u32[]{:S(2)}, u32[]{:S(2)}) collective-permute-start(f32[16,3,8,512]{3,2,1,0:T(8,128)S(1)} %all_to_all.10.half_ref), channel_id=1, source_target_pairs={{0,32},{32,0},{1,33},{33,1},{2,34},{34,2},{3,35},{35,3},{4,36},{36... | collective-permute-start | bytes 2359304 | tf_op jit(solution)/shard_map/ppermute | solution.py:182

commit v13 on v12

--- a/solution.py
+++ b/solution.py
@@ -48,10 +48,11 @@
     wide = packed.astype(jnp.float32)
     return jnp.stack(
         (
-            wide[0] + wide[1] * (1.0 / REST_SCALE),
-            wide[2] * (1.0 / FIRST_SCALE),
-            wide[3] * (1.0 / SECOND_SCALE),
-        )
+            wide[:, 0] + wide[:, 1] * (1.0 / REST_SCALE),
+            wide[:, 2] * (1.0 / FIRST_SCALE),
+            wide[:, 3] * (1.0 / SECOND_SCALE),
+        ),
+        axis=1,
     )
 
 
@@ -175,10 +176,11 @@
 
     def wanted(index):
         place = pick(partners, index, 0)
-        return unpack(pick(pick(along, place >> 1, 0), place & 1, 1))
-
-    placed = jnp.stack([wanted(here + i) for i in range(2)]).reshape(1, 2, 3, 8, 512)
-    half = exchange(jnp.broadcast_to(placed, (8, 2, 3, 8, 512)).reshape(16, 3, 8, 512), CHIPS)
+        return pick(pick(along, place >> 1, 0), place & 1, 1)
+
+    placed = jnp.stack([wanted(here + i) for i in range(2)]).reshape(1, 2, 4, 8, 512)
+    shared = jnp.broadcast_to(placed, (8, 2, 4, 8, 512)).reshape(16, 4, 8, 512)
+    half = unpack(exchange(shared, CHIPS))
     sibling = lax.ppermute(half, "c", SWAP)
     return assemble(core, half, sibling)
 

time: 132 us -> 130 us (0.985)
  blocking collectives: 81.4 us -> 79.6 us
    all_to_all x1, blocking collectives: 12.9 us -> 11.1 us  [exchange(): return lax.all_to_all(array, axes, split_axis=0, concat_axis=0, tiled=True)]
where the time goes in v13:
time: 130 us
  blocking collectives  79.6 us (61%)
  starting transfers between devices  33.2 us (26%)
  local copies, waits for them, and re-layouts  4.56 us (4%)
  waiting for transfers between devices  4.26 us (3%)
  between operations  3.39 us (3%)
  Pallas kernels  2.6 us (2%)
  other arithmetic  1.92 us (1%)
    all_gather x1, blocking collectives, on_device(): cotangents = lax.all_gather(scaled, 'z', axis=0, tiled=True)  41.7 us
    all_gather x1, blocking collectives, on_device(): along = lax.all_gather(pack(*results), 'z', axis=0, tiled=False)  26.8 us
    all_to_all x1, starting transfers between devices, exchange(): return lax.all_to_all(array, axes, split_axis=0, concat_axis=0, tiled=True)  12.3 us
    all_to_all x1, blocking collectives, exchange(): return lax.all_to_all(array, axes, split_axis=0, concat_axis=0, tiled=True)  11.1 us
    ppermute x1, starting transfers between devices, on_device(): sibling = lax.ppermute(half, 'c', SWAP)  10.7 us
    ppermute x1, starting transfers between devices, on_device(): got = lax.ppermute(pick(tokens, other, 1), 'xh', SWAP)  5.48 us
    ppermute x1, starting transfers between devices, on_device(): peer_rows = lax.ppermute(eight(other), 'xh', SWAP)  4.79 us
  transfers between devices with their start and end apart: 4, of which 3 were waited for; matrix products, arithmetic and copies ran while one was open for 2% of the time, Pallas kernels for 0%

profile of v13, /device:TPU:1, one launch (start us, length us, event | category | flops | bytes accessed | tf_op | source)
XLA Modules:
  0.0 129.5 jit_solution(1523357075646177428)
XLA Ops:
  0.6 0.0 copy-start.1
  0.6 1.3 dynamic-slice_bitcast_fusion
  1.9 5.5 %collective-permute-start.1 = (bf16[16,112,256]{2,1,0:T(8,128)(2,1)S(1)}, bf16[16,112,256]{2,1,0:T(8,128)(2,1)S(1)}, u32[]{:S(2)}, u32[]{:S(2)}) collective-permute-start(bf16[16,112,256]{2,1,0:T(8,128)(2,1)S(1)} %dynamic-slice_bitcast_fusion), channel_id=1, source_target_pairs={{0,1},{1,0},{2,3},{3,2},{4,5},{5,4},{6,7},{7,6},{8,9},{9,8},{10,11... | collective-permute-start | bytes 2752520 | tf_op jit(solution)/shard_map/ppermute | solution.py:146
  7.4 0.0 copy-done.1
  7.5 41.7 %all-gather.2 = f16[1792,512]{1,0:T(8,128)(2,1)S(1)} all-gather(f16[112,512]{1,0:T(8,128)(2,1)S(1)} %multiply_convert_fusion.2), channel_id=1, replica_groups=mesh['xl'=2,'y'=4,'c'=2,'z'=16,'xh'=2] {'z'}, dimensions={0}, use_global_device_ids=true | all-gather | bytes 1949696 | tf_op jit(solution)/shard_map/all_gather | solution.py:161
  49.2 0.0 copy-start
  49.2 0.0 collective-permute-done.1
  49.2 0.4 multiply_convert_fusion.cotangents_ref
  49.6 1.1 copy-done
  50.7 1.4 %shard_map.85 = f32[32,2,8,512]{3,2,1,0:T(8,128)S(1)} custom-call(s32[1]{0:T(128)} %bitcast.10.mine_ref, bf16[16,2,112,256]{3,2,1,0:T(8,128)(2,1)S(1)} %bitcast.55, bf16[1792,256]{1,0:T(8,128)(2,1)S(1)} %bitcast.56, bf16[1792,512]{1,0:T(8,128)(2,1)S(1)} %multiply_convert_fusion.cotangents_ref), custom_call_target="tpu_custom_call" | custom-call | flops 939524096 | bytes 6291456 | tf_op jit(solution)/shard_map/pallas_call | solution.py:87
  52.1 0.0 copy-start.2
  52.1 0.9 multiply_convert_fusion.1
  53.1 12.3 %all-to-all-start = ((f16[32,2,8,512]{3,2,1,0:T(8,128)(2,1)}), f16[32,2,8,512]{3,2,1,0:T(8,128)(2,1)S(1)}, u32[]{:S(2)}, u32[]{:S(2)}) async-start(f16[32,2,8,512]{3,2,1,0:T(8,128)(2,1)} %multiply_convert_fusion.1), calls=%async_computation | async-start | bytes 1048576 | tf_op jit(solution)/shard_map/all_to_all | solution.py:30
  65.3 0.7 dynamic-slice_bitcast_fusion.8
  66.1 0.8 dynamic-slice_bitcast_fusion.6
  66.9 4.8 %collective-permute-start = (f32[3,8,512]{2,1,0:T(8,128)S(1)}, f32[3,8,512]{2,1,0:T(8,128)S(1)}, u32[]{:S(2)}, u32[]{:S(2)}) collective-permute-start(f32[3,8,512]{2,1,0:T(8,128)S(1)} %pad_maximum_fusion.4), channel_id=1, source_target_pairs={{0,1},{1,0},{2,3},{3,2},{4,5},{5,4},{6,7},{7,6},{8,9},{9,8},{10,11... | collective-permute-start | bytes 147464 | tf_op jit(solution)/shard_map/ppermute | solution.py:164
  71.7 0.0 copy-done.2
  71.7 0.6 fusion.14
  74.9 0.9 collective-permute-done
  75.8 1.5 %all-to-all-done = f16[32,2,8,512]{3,2,1,0:T(8,128)(2,1)S(1)} async-done(((f16[32,2,8,512]{3,2,1,0:T(8,128)(2,1)}), f16[32,2,8,512]{3,2,1,0:T(8,128)(2,1)S(1)}, u32[]{:S(2)}, u32[]{:S(2)}) %all-to-all-start) | async-done | bytes 524320 | tf_op jit(solution)/shard_map/all_to_all | solution.py:30
  77.3 0.1 convert_reduce_fusion
  77.3 0.1 fusion.12
  77.5 26.8 %all-gather.3 = f16[16,4,2,8,512]{4,3,2,1,0:T(8,128)(2,1)S(1)} all-gather(f16[1,4,2,8,512]{4,3,2,1,0:T(8,128)(2,1)S(1)} %pad_maximum_fusion.1), channel_id=1, replica_groups=mesh['xl'=2,'y'=4,'c'=2,'z'=16,'xh'=2] {'z'}, dimensions={0}, use_global_device_ids=true | all-gather | bytes 1114112 | tf_op jit(solution)/shard_map/all_gather | solution.py:174
  104.4 11.1 %all_to_all.10 = f16[16,4,8,512]{3,2,1,0:T(8,128)(2,1)S(1)} all-to-all(f16[16,4,8,512]{3,2,1,0:T(8,128)(2,1)S(1)} %bitcast.57), channel_id=1, replica_groups=mesh['xl'=2,'y'=4,'c'=2,'z'=16,'xh'=2] {'xl','y','xh'}, dimensions={0} | all-to-all | bytes 1048576 | tf_op jit(solution)/shard_map/all_to_all | solution.py:30
  115.5 0.1 convert_element_type.35
  115.6 0.1 fusion
  115.7 0.1 pad_maximum_fusion.half_ref
  115.8 10.7 %collective-permute-start.2 = (f32[16,3,8,512]{3,2,1,0:T(8,128)S(1)}, f32[16,3,8,512]{3,2,1,0:T(8,128)S(1)}, u32[]{:S(2)}, u32[]{:S(2)}) collective-permute-start(f32[16,3,8,512]{3,2,1,0:T(8,128)S(1)} %pad_maximum_fusion.half_ref), channel_id=1, source_target_pairs={{0,32},{32,0},{1,33},{33,1},{2,34},{34,2},{3,35},{35,3},{4,36},{36... | collective-permute-start | bytes 2359304 | tf_op jit(solution)/shard_map/ppermute | solution.py:184
  126.5 1.9 %collective-permute-done.2.sibling_ref = f32[16,3,8,512]{3,2,1,0:T(8,128)S(1)} collective-permute-done((f32[16,3,8,512]{3,2,1,0:T(8,128)S(1)}, f32[16,3,8,512]{3,2,1,0:T(8,128)S(1)}, u32[]{:S(2)}, u32[]{:S(2)}) %collective-permute-start.2) | collective-permute-done | bytes 786464 | tf_op jit(solution)/shard_map/ppermute | solution.py:184
  128.3 1.2 shard_map.86
  (9 shorter events, 0.2 us)
Async XLA Ops:
  0.6 6.8 %copy-start.1 = (bf16[112,512]{1,0:T(8,128)(2,1)S(1)}, bf16[112,512]{1,0:T(8,128)(2,1)}, u32[]{:S(2)}) copy-start(bf16[112,512]{1,0:T(8,128)(2,1)} %param.7) | copy-start | bytes 344068
  1.9 47.3 %collective-permute-start.1 = (bf16[16,112,256]{2,1,0:T(8,128)(2,1)S(1)}, bf16[16,112,256]{2,1,0:T(8,128)(2,1)S(1)}, u32[]{:S(2)}, u32[]{:S(2)}) collective-permute-start(bf16[16,112,256]{2,1,0:T(8,128)(2,1)S(1)} %dynamic-slice_bitcast_fusion), channel_id=1, source_target_pairs={{0,1},{1,0},{2,3},{3,2},{4,5},{5,4},{6,7},{7,6},{8,9},{9,8},{10,11... | collective-permute-start | bytes 2752520 | tf_op jit(solution)/shard_map/ppermute | solution.py:146
  49.2 1.5 %copy-start = (bf16[3584,256]{1,0:T(8,128)(2,1)S(1)}, bf16[3584,256]{1,0:T(8,128)(2,1)}, u32[]{:S(2)}) copy-start(bf16[3584,256]{1,0:T(8,128)(2,1)} %param.6) | copy-start | bytes 5505028
  52.1 19.5 %copy-start.2 = (s32[32]{0:T(128)S(1)}, s32[32]{0:T(128)}, u32[]{:S(2)}) copy-start(s32[32]{0:T(128)} %param.8) | copy-start | bytes 388
  53.1 24.2 %all-to-all-start = ((f16[32,2,8,512]{3,2,1,0:T(8,128)(2,1)}), f16[32,2,8,512]{3,2,1,0:T(8,128)(2,1)S(1)}, u32[]{:S(2)}, u32[]{:S(2)}) async-start(f16[32,2,8,512]{3,2,1,0:T(8,128)(2,1)} %multiply_convert_fusion.1), calls=%async_computation | async-start | bytes 1048576 | tf_op jit(solution)/shard_map/all_to_all | solution.py:30
  66.9 8.9 %collective-permute-start = (f32[3,8,512]{2,1,0:T(8,128)S(1)}, f32[3,8,512]{2,1,0:T(8,128)S(1)}, u32[]{:S(2)}, u32[]{:S(2)}) collective-permute-start(f32[3,8,512]{2,1,0:T(8,128)S(1)} %pad_maximum_fusion.4), channel_id=1, source_target_pairs={{0,1},{1,0},{2,3},{3,2},{4,5},{5,4},{6,7},{7,6},{8,9},{9,8},{10,11... | collective-permute-start | bytes 147464 | tf_op jit(solution)/shard_map/ppermute | solution.py:164
  115.8 12.6 %collective-permute-start.2 = (f32[16,3,8,512]{3,2,1,0:T(8,128)S(1)}, f32[16,3,8,512]{3,2,1,0:T(8,128)S(1)}, u32[]{:S(2)}, u32[]{:S(2)}) collective-permute-start(f32[16,3,8,512]{3,2,1,0:T(8,128)S(1)} %pad_maximum_fusion.half_ref), channel_id=1, source_target_pairs={{0,32},{32,0},{1,33},{33,1},{2,34},{34,2},{3,35},{35,3},{4,36},{36... | collective-permute-start | bytes 2359304 | tf_op jit(solution)/shard_map/ppermute | solution.py:184

commit v14 on v13

--- a/solution.py
+++ b/solution.py
@@ -64,45 +64,55 @@
     return (new_weight, new_first, new_second)
 
 
-def products_kernel(mine_ref, tokens_ref, got_ref, cotangents_ref, out_ref, kept, arrived):
+def product_of(features, cotangents_ref):
+    return lax.dot_general(
+        features,
+        cotangents_ref[...],
+        (((0,), (0,)), ((), ())),
+        preferred_element_type=jnp.float32,
+    ).reshape(32, 8, 512)
+
+
+def arrived_kernel(got_ref, cotangents_ref, out_ref):
+    out_ref[...] = product_of(got_ref[...], cotangents_ref)
+
+
+def own_kernel(mine_ref, tokens_ref, cotangents_ref, half_ref, out_ref, kept, arrived):
     mine = mine_ref[0]
     fetch = pltpu.make_async_copy(tokens_ref.at[:, mine], kept, arrived)
     fetch.start()
-
-    def product(features):
-        return lax.dot_general(
-            features,
-            cotangents_ref[...],
-            (((0,), (0,)), ((), ())),
-            preferred_element_type=jnp.float32,
-        ).reshape(32, 8, 512)
-
-    out_ref[:, 1 - mine] = product(got_ref[...])
+    out_ref[:, 1 - mine] = half_ref[...]
     fetch.wait()
-    out_ref[:, mine] = product(kept[...].reshape(1792, 256))
+    out_ref[:, mine] = product_of(kept[...].reshape(1792, 256), cotangents_ref)
 
 
 def products(mine, tokens, got, cotangents):
+    in_smem = pl.BlockSpec(memory_space=pltpu.SMEM)
     in_vmem = pl.BlockSpec(memory_space=pltpu.VMEM)
+    in_any = pl.BlockSpec(memory_space=pl.ANY)
+    shared = dict(
+        out_specs=in_vmem,
+        compiler_params=pltpu.CompilerParams(vmem_limit_bytes=40 * 1024 * 1024),
+        cost_estimate=pl.CostEstimate(
+            flops=2 * 1792 * 256 * 512, bytes_accessed=3 * 1024 * 1024, transcendentals=0
+        ),
+    )
+    half = pl.pallas_call(
+        arrived_kernel,
+        out_shape=jax.ShapeDtypeStruct((32, 8, 512), jnp.float32),
+        in_specs=[in_vmem, in_vmem],
+        **shared,
+    )(got, cotangents)
     return pl.pallas_call(
-        products_kernel,
+        own_kernel,
         out_shape=jax.ShapeDtypeStruct((32, 2, 8, 512), jnp.float32),
-        in_specs=[
-            pl.BlockSpec(memory_space=pltpu.SMEM),
-            pl.BlockSpec(memory_space=pl.ANY),
-            in_vmem,
-            in_vmem,
-        ],
-        out_specs=in_vmem,
+        in_specs=[in_smem, in_any, in_vmem, in_vmem],
         scratch_shapes=[
             pltpu.VMEM((16, 112, 256), jnp.bfloat16),
             pltpu.SemaphoreType.DMA,
         ],
-        compiler_params=pltpu.CompilerParams(vmem_limit_bytes=40 * 1024 * 1024),
-        cost_estimate=pl.CostEstimate(
-            flops=2 * 2 * 1792 * 256 * 512, bytes_accessed=6 * 1024 * 1024, transcendentals=0
-        ),
-    )(mine.reshape(1), tokens, got, cotangents)
+        **shared,
+    )(mine.reshape(1), tokens, cotangents, half)
 
 
 def assemble_kernel(core_ref, half_ref, sibling_ref, *refs):

time: 130 us -> 130 us (level)
  no operation moved by 1% of the time
where the time goes in v14:
time: 130 us; the launch traced here: 129 us
  blocking collectives  79.6 us (61%)
  starting transfers between devices  33.2 us (26%)
  local copies, waits for them, and re-layouts  4.33 us (3%)
  waiting for transfers between devices  4.26 us (3%)
  between operations  3.41 us (3%)
  Pallas kernels  2.63 us (2%)
  other arithmetic  1.92 us (1%)
    all_gather x1, blocking collectives, on_device(): cotangents = lax.all_gather(scaled, 'z', axis=0, tiled=True)  41.7 us
    all_gather x1, blocking collectives, on_device(): along = lax.all_gather(pack(*results), 'z', axis=0, tiled=False)  26.8 us
    all_to_all x1, starting transfers between devices, exchange(): return lax.all_to_all(array, axes, split_axis=0, concat_axis=0, tiled=True)  12.3 us
    all_to_all x1, blocking collectives, exchange(): return lax.all_to_all(array, axes, split_axis=0, concat_axis=0, tiled=True)  11.1 us
    ppermute x1, starting transfers between devices, on_device(): sibling = lax.ppermute(half, 'c', SWAP)  10.7 us
    ppermute x1, starting transfers between devices, on_device(): got = lax.ppermute(pick(tokens, other, 1), 'xh', SWAP)  5.48 us
    ppermute x1, starting transfers between devices, on_device(): peer_rows = lax.ppermute(eight(other), 'xh', SWAP)  4.79 us
  transfers between devices with their start and end apart: 4, of which 3 were waited for; matrix products, arithmetic and copies ran while one was open for 2% of the time, Pallas kernels for 0%

profile of v14, /device:TPU:1, one launch (start us, length us, event | category | flops | bytes accessed | tf_op | source)
XLA Modules:
  0.0 129.3 jit_solution(12043100050764446655)
XLA Ops:
  0.6 0.0 copy-start.1
  0.6 1.3 dynamic-slice_bitcast_fusion
  1.9 5.5 %collective-permute-start.1 = (bf16[16,112,256]{2,1,0:T(8,128)(2,1)S(1)}, bf16[16,112,256]{2,1,0:T(8,128)(2,1)S(1)}, u32[]{:S(2)}, u32[]{:S(2)}) collective-permute-start(bf16[16,112,256]{2,1,0:T(8,128)(2,1)S(1)} %dynamic-slice_bitcast_fusion), channel_id=1, source_target_pairs={{0,1},{1,0},{2,3},{3,2},{4,5},{5,4},{6,7},{7,6},{8,9},{9,8},{10,11... | collective-permute-start | bytes 2752520 | tf_op jit(solution)/shard_map/ppermute | solution.py:156
  7.4 0.0 copy-done.1
  7.5 41.7 %all-gather.2 = f16[1792,512]{1,0:T(8,128)(2,1)S(1)} all-gather(f16[112,512]{1,0:T(8,128)(2,1)S(1)} %multiply_convert_fusion.2), channel_id=1, replica_groups=mesh['xl'=2,'y'=4,'c'=2,'z'=16,'xh'=2] {'z'}, dimensions={0}, use_global_device_ids=true | all-gather | bytes 1949696 | tf_op jit(solution)/shard_map/all_gather | solution.py:171
  49.2 0.0 collective-permute-done.1
  49.2 0.4 multiply_convert_fusion.cotangents_ref
  49.6 0.0 copy-start
  49.7 0.7 shard_map.85.half_ref
  50.3 0.8 copy-done
  51.1 0.8 shard_map.86
  51.9 0.0 copy-start.2
  52.0 0.9 multiply_convert_fusion.1
  52.9 12.3 %all-to-all-start = ((f16[32,2,8,512]{3,2,1,0:T(8,128)(2,1)}), f16[32,2,8,512]{3,2,1,0:T(8,128)(2,1)S(1)}, u32[]{:S(2)}, u32[]{:S(2)}) async-start(f16[32,2,8,512]{3,2,1,0:T(8,128)(2,1)} %multiply_convert_fusion.1), calls=%async_computation | async-start | bytes 1048576 | tf_op jit(solution)/shard_map/all_to_all | solution.py:30
  65.1 0.7 dynamic-slice_bitcast_fusion.8
  65.9 0.8 dynamic-slice_bitcast_fusion.6
  66.7 4.8 %collective-permute-start = (f32[3,8,512]{2,1,0:T(8,128)S(1)}, f32[3,8,512]{2,1,0:T(8,128)S(1)}, u32[]{:S(2)}, u32[]{:S(2)}) collective-permute-start(f32[3,8,512]{2,1,0:T(8,128)S(1)} %pad_maximum_fusion.4), channel_id=1, source_target_pairs={{0,1},{1,0},{2,3},{3,2},{4,5},{5,4},{6,7},{7,6},{8,9},{9,8},{10,11... | collective-permute-start | bytes 147464 | tf_op jit(solution)/shard_map/ppermute | solution.py:174
  71.5 0.0 copy-done.2
  71.5 0.6 fusion.14
  74.7 0.9 collective-permute-done
  75.6 1.5 %all-to-all-done = f16[32,2,8,512]{3,2,1,0:T(8,128)(2,1)S(1)} async-done(((f16[32,2,8,512]{3,2,1,0:T(8,128)(2,1)}), f16[32,2,8,512]{3,2,1,0:T(8,128)(2,1)S(1)}, u32[]{:S(2)}, u32[]{:S(2)}) %all-to-all-start) | async-done | bytes 524320 | tf_op jit(solution)/shard_map/all_to_all | solution.py:30
  77.1 0.1 convert_reduce_fusion
  77.2 0.1 fusion.12
  77.3 26.8 %all-gather.3 = f16[16,4,2,8,512]{4,3,2,1,0:T(8,128)(2,1)S(1)} all-gather(f16[1,4,2,8,512]{4,3,2,1,0:T(8,128)(2,1)S(1)} %pad_maximum_fusion.1), channel_id=1, replica_groups=mesh['xl'=2,'y'=4,'c'=2,'z'=16,'xh'=2] {'z'}, dimensions={0}, use_global_device_ids=true | all-gather | bytes 1114112 | tf_op jit(solution)/shard_map/all_gather | solution.py:184
  104.2 11.1 %all_to_all.10 = f16[16,4,8,512]{3,2,1,0:T(8,128)(2,1)S(1)} all-to-all(f16[16,4,8,512]{3,2,1,0:T(8,128)(2,1)S(1)} %bitcast.57), channel_id=1, replica_groups=mesh['xl'=2,'y'=4,'c'=2,'z'=16,'xh'=2] {'xl','y','xh'}, dimensions={0} | all-to-all | bytes 1048576 | tf_op jit(solution)/shard_map/all_to_all | solution.py:30
  115.3 0.1 convert_element_type.35
  115.4 0.1 fusion
  115.5 0.1 pad_maximum_fusion.half_ref
  115.6 10.7 %collective-permute-start.2 = (f32[16,3,8,512]{3,2,1,0:T(8,128)S(1)}, f32[16,3,8,512]{3,2,1,0:T(8,128)S(1)}, u32[]{:S(2)}, u32[]{:S(2)}) collective-permute-start(f32[16,3,8,512]{3,2,1,0:T(8,128)S(1)} %pad_maximum_fusion.half_ref), channel_id=1, source_target_pairs={{0,32},{32,0},{1,33},{33,1},{2,34},{34,2},{3,35},{35,3},{4,36},{36... | collective-permute-start | bytes 2359304 | tf_op jit(solution)/shard_map/ppermute | solution.py:194
  126.3 1.9 %collective-permute-done.2.sibling_ref = f32[16,3,8,512]{3,2,1,0:T(8,128)S(1)} collective-permute-done((f32[16,3,8,512]{3,2,1,0:T(8,128)S(1)}, f32[16,3,8,512]{3,2,1,0:T(8,128)S(1)}, u32[]{:S(2)}, u32[]{:S(2)}) %collective-permute-start.2) | collective-permute-done | bytes 786464 | tf_op jit(solution)/shard_map/ppermute | solution.py:194
  128.1 1.2 shard_map.87
  (9 shorter events, 0.2 us)
Async XLA Ops:
  0.6 6.8 %copy-start.1 = (bf16[112,512]{1,0:T(8,128)(2,1)S(1)}, bf16[112,512]{1,0:T(8,128)(2,1)}, u32[]{:S(2)}) copy-start(bf16[112,512]{1,0:T(8,128)(2,1)} %param.7) | copy-start | bytes 344068
  1.9 47.3 %collective-permute-start.1 = (bf16[16,112,256]{2,1,0:T(8,128)(2,1)S(1)}, bf16[16,112,256]{2,1,0:T(8,128)(2,1)S(1)}, u32[]{:S(2)}, u32[]{:S(2)}) collective-permute-start(bf16[16,112,256]{2,1,0:T(8,128)(2,1)S(1)} %dynamic-slice_bitcast_fusion), channel_id=1, source_target_pairs={{0,1},{1,0},{2,3},{3,2},{4,5},{5,4},{6,7},{7,6},{8,9},{9,8},{10,11... | collective-permute-start | bytes 2752520 | tf_op jit(solution)/shard_map/ppermute | solution.py:156
  49.6 1.5 %copy-start = (bf16[3584,256]{1,0:T(8,128)(2,1)S(1)}, bf16[3584,256]{1,0:T(8,128)(2,1)}, u32[]{:S(2)}) copy-start(bf16[3584,256]{1,0:T(8,128)(2,1)} %param.6) | copy-start | bytes 5505028
  51.9 19.5 %copy-start.2 = (s32[32]{0:T(128)S(1)}, s32[32]{0:T(128)}, u32[]{:S(2)}) copy-start(s32[32]{0:T(128)} %param.8) | copy-start | bytes 388
  52.9 24.2 %all-to-all-start = ((f16[32,2,8,512]{3,2,1,0:T(8,128)(2,1)}), f16[32,2,8,512]{3,2,1,0:T(8,128)(2,1)S(1)}, u32[]{:S(2)}, u32[]{:S(2)}) async-start(f16[32,2,8,512]{3,2,1,0:T(8,128)(2,1)} %multiply_convert_fusion.1), calls=%async_computation | async-start | bytes 1048576 | tf_op jit(solution)/shard_map/all_to_all | solution.py:30
  66.7 8.9 %collective-permute-start = (f32[3,8,512]{2,1,0:T(8,128)S(1)}, f32[3,8,512]{2,1,0:T(8,128)S(1)}, u32[]{:S(2)}, u32[]{:S(2)}) collective-permute-start(f32[3,8,512]{2,1,0:T(8,128)S(1)} %pad_maximum_fusion.4), channel_id=1, source_target_pairs={{0,1},{1,0},{2,3},{3,2},{4,5},{5,4},{6,7},{7,6},{8,9},{9,8},{10,11... | collective-permute-start | bytes 147464 | tf_op jit(solution)/shard_map/ppermute | solution.py:174
  115.6 12.6 %collective-permute-start.2 = (f32[16,3,8,512]{3,2,1,0:T(8,128)S(1)}, f32[16,3,8,512]{3,2,1,0:T(8,128)S(1)}, u32[]{:S(2)}, u32[]{:S(2)}) collective-permute-start(f32[16,3,8,512]{3,2,1,0:T(8,128)S(1)} %pad_maximum_fusion.half_ref), channel_id=1, source_target_pairs={{0,32},{32,0},{1,33},{33,1},{2,34},{34,2},{3,35},{35,3},{4,36},{36... | collective-permute-start | bytes 2359304 | tf_op jit(solution)/shard_map/ppermute | solution.py:194

commit v15 on v13

--- a/solution.py
+++ b/solution.py
@@ -17,7 +17,7 @@
 DP = ("xl", "y", "c")
 FSDP = ("z", "xh")
 CHIPS = ("xl", "y", "xh")
-PLANE = ("c", "xl", "y", "xh")
+PLANE = ("xl", "y", "c", "xh")
 SWAP = [(0, 1), (1, 0)]
 KEY_SCALE = 2.0**21
 REST_SCALE = 2.0**11
@@ -112,7 +112,9 @@
     for i in range(3):
         for j, (source, place) in enumerate(((half_ref, core), (sibling_ref, 1 - core))):
             copies.append(
-                pltpu.make_async_copy(source.at[:, i], outs[i].at[place], done.at[2 * i + j])
+                pltpu.make_async_copy(
+                    source.at[:, :, i], outs[i].at[:, place], done.at[2 * i + j]
+                )
             )
     for copy in copies:
         copy.start()
@@ -124,7 +126,7 @@
     in_vmem = pl.BlockSpec(memory_space=pltpu.VMEM)
     outs = pl.pallas_call(
         assemble_kernel,
-        out_shape=[jax.ShapeDtypeStruct((2, 16, 8, 512), jnp.float32)] * 3,
+        out_shape=[jax.ShapeDtypeStruct((8, 2, 2, 8, 512), jnp.float32)] * 3,
         in_specs=[pl.BlockSpec(memory_space=pltpu.SMEM), in_vmem, in_vmem],
         out_specs=[pl.BlockSpec(memory_space=pl.ANY)] * 3,
         scratch_shapes=[pltpu.SemaphoreType.DMA((6,))],
@@ -145,7 +147,7 @@
     tokens = activations.reshape(16, 2, 112, 256)
     got = lax.ppermute(pick(tokens, other, 1), "xh", SWAP)
 
-    first_row = 128 * core + 16 * column
+    first_row = 32 * column + 16 * core
 
     def eight(side):
         return jnp.stack(
@@ -180,7 +182,7 @@
 
     placed = jnp.stack([wanted(here + i) for i in range(2)]).reshape(1, 2, 4, 8, 512)
     shared = jnp.broadcast_to(placed, (8, 2, 4, 8, 512)).reshape(16, 4, 8, 512)
-    half = unpack(exchange(shared, CHIPS))
+    half = unpack(exchange(shared, CHIPS)).reshape(8, 2, 3, 8, 512)
     sibling = lax.ppermute(half, "c", SWAP)
     return assemble(core, half, sibling)
 

time: 130 us -> 130 us (level)
  no operation moved by 1% of the time
where the time goes in v15:
time: 130 us
  blocking collectives  78.9 us (61%)
  starting transfers between devices  34.2 us (26%)
  local copies, waits for them, and re-layouts  4.56 us (4%)
  waiting for transfers between devices  4.12 us (3%)
  between operations  3.39 us (3%)
  Pallas kernels  2.6 us (2%)
  other arithmetic  1.92 us (1%)
    all_gather x1, blocking collectives, on_device(): cotangents = lax.all_gather(scaled, 'z', axis=0, tiled=True)  41.7 us
    all_gather x1, blocking collectives, on_device(): along = lax.all_gather(pack(*results), 'z', axis=0, tiled=False)  26.1 us
    all_to_all x1, starting transfers between devices, exchange(): return lax.all_to_all(array, axes, split_axis=0, concat_axis=0, tiled=True)  12.2 us
    ppermute x1, starting transfers between devices, on_device(): sibling = lax.ppermute(half, 'c', SWAP)  11.7 us
    all_to_all x1, blocking collectives, exchange(): return lax.all_to_all(array, axes, split_axis=0, concat_axis=0, tiled=True)  11.1 us
    ppermute x1, starting transfers between devices, on_device(): got = lax.ppermute(pick(tokens, other, 1), 'xh', SWAP)  5.48 us
    ppermute x1, starting transfers between devices, on_device(): peer_rows = lax.ppermute(eight(other), 'xh', SWAP)  4.8 us
  transfers between devices with their start and end apart: 4, of which 3 were waited for; matrix products, arithmetic and copies ran while one was open for 2% of the time, Pallas kernels for 0%

profile of v15, /device:TPU:1, one launch (start us, length us, event | category | flops | bytes accessed | tf_op | source)
XLA Modules:
  0.0 129.7 jit_solution(3661498077318208507)
XLA Ops:
  0.6 0.0 copy-start.1
  0.6 1.3 dynamic-slice_bitcast_fusion
  1.9 5.5 %collective-permute-start.1 = (bf16[16,112,256]{2,1,0:T(8,128)(2,1)S(1)}, bf16[16,112,256]{2,1,0:T(8,128)(2,1)S(1)}, u32[]{:S(2)}, u32[]{:S(2)}) collective-permute-start(bf16[16,112,256]{2,1,0:T(8,128)(2,1)S(1)} %dynamic-slice_bitcast_fusion), channel_id=1, source_target_pairs={{0,1},{1,0},{2,3},{3,2},{4,5},{5,4},{6,7},{7,6},{8,9},{9,8},{10,11... | collective-permute-start | bytes 2752520 | tf_op jit(solution)/shard_map/ppermute | solution.py:148
  7.4 0.0 copy-done.1
  7.5 41.7 %all-gather.2 = f16[1792,512]{1,0:T(8,128)(2,1)S(1)} all-gather(f16[112,512]{1,0:T(8,128)(2,1)S(1)} %multiply_convert_fusion.2), channel_id=1, replica_groups=mesh['xl'=2,'y'=4,'c'=2,'z'=16,'xh'=2] {'z'}, dimensions={0}, use_global_device_ids=true | all-gather | bytes 1949696 | tf_op jit(solution)/shard_map/all_gather | solution.py:163
  49.2 0.0 copy-start
  49.2 0.0 collective-permute-done.1
  49.2 0.4 multiply_convert_fusion.cotangents_ref
  49.6 1.1 copy-done
  50.7 1.4 %shard_map.85 = f32[32,2,8,512]{3,2,1,0:T(8,128)S(1)} custom-call(s32[1]{0:T(128)} %bitcast.10.mine_ref, bf16[16,2,112,256]{3,2,1,0:T(8,128)(2,1)S(1)} %bitcast.58, bf16[1792,256]{1,0:T(8,128)(2,1)S(1)} %bitcast.59, bf16[1792,512]{1,0:T(8,128)(2,1)S(1)} %multiply_convert_fusion.cotangents_ref), custom_call_target="tpu_custom_call" | custom-call | flops 939524096 | bytes 6291456 | tf_op jit(solution)/shard_map/pallas_call | solution.py:87
  52.1 0.0 copy-start.2
  52.1 0.9 multiply_convert_fusion.1
  53.1 12.2 %all-to-all-start = ((f16[32,2,8,512]{3,2,1,0:T(8,128)(2,1)}), f16[32,2,8,512]{3,2,1,0:T(8,128)(2,1)S(1)}, u32[]{:S(2)}, u32[]{:S(2)}) async-start(f16[32,2,8,512]{3,2,1,0:T(8,128)(2,1)} %multiply_convert_fusion.1), calls=%async_computation | async-start | bytes 1048576 | tf_op jit(solution)/shard_map/all_to_all | solution.py:30
  65.3 0.7 dynamic-slice_bitcast_fusion.8
  66.1 0.8 dynamic-slice_bitcast_fusion.6
  66.9 4.8 %collective-permute-start = (f32[3,8,512]{2,1,0:T(8,128)S(1)}, f32[3,8,512]{2,1,0:T(8,128)S(1)}, u32[]{:S(2)}, u32[]{:S(2)}) collective-permute-start(f32[3,8,512]{2,1,0:T(8,128)S(1)} %pad_maximum_fusion.4), channel_id=1, source_target_pairs={{0,1},{1,0},{2,3},{3,2},{4,5},{5,4},{6,7},{7,6},{8,9},{9,8},{10,11... | collective-permute-start | bytes 147464 | tf_op jit(solution)/shard_map/ppermute | solution.py:166
  71.7 0.0 copy-done.2
  71.7 0.6 fusion.14
  74.9 0.9 collective-permute-done
  75.8 1.4 %all-to-all-done = f16[32,2,8,512]{3,2,1,0:T(8,128)(2,1)S(1)} async-done(((f16[32,2,8,512]{3,2,1,0:T(8,128)(2,1)}), f16[32,2,8,512]{3,2,1,0:T(8,128)(2,1)S(1)}, u32[]{:S(2)}, u32[]{:S(2)}) %all-to-all-start) | async-done | bytes 524320 | tf_op jit(solution)/shard_map/all_to_all | solution.py:30
  77.1 0.1 convert_reduce_fusion
  77.2 0.1 fusion.12
  77.4 26.1 %all-gather.3 = f16[16,4,2,8,512]{4,3,2,1,0:T(8,128)(2,1)S(1)} all-gather(f16[1,4,2,8,512]{4,3,2,1,0:T(8,128)(2,1)S(1)} %pad_maximum_fusion.1), channel_id=1, replica_groups=mesh['xl'=2,'y'=4,'c'=2,'z'=16,'xh'=2] {'z'}, dimensions={0}, use_global_device_ids=true | all-gather | bytes 1114112 | tf_op jit(solution)/shard_map/all_gather | solution.py:176
  103.5 11.1 %all_to_all.10 = f16[16,4,8,512]{3,2,1,0:T(8,128)(2,1)S(1)} all-to-all(f16[16,4,8,512]{3,2,1,0:T(8,128)(2,1)S(1)} %bitcast.60), channel_id=1, replica_groups=mesh['xl'=2,'y'=4,'c'=2,'z'=16,'xh'=2] {'xl','y','xh'}, dimensions={0} | all-to-all | bytes 1048576 | tf_op jit(solution)/shard_map/all_to_all | solution.py:30
  114.6 0.1 convert_element_type.35
  114.8 0.1 fusion
  114.9 0.1 pad_maximum_fusion.half_ref
  115.0 11.7 %collective-permute-start.2 = (f32[8,2,3,8,512]{4,3,2,1,0:T(8,128)S(1)}, f32[8,2,3,8,512]{4,3,2,1,0:T(8,128)S(1)}, u32[]{:S(2)}, u32[]{:S(2)}) collective-permute-start(f32[8,2,3,8,512]{4,3,2,1,0:T(8,128)S(1)} %pad_maximum_fusion.half_ref), channel_id=1, source_target_pairs={{0,32},{32,0},{1,33},{33,1},{2,34},{34,2},{3,35},{35,3},{4,36},{36... | collective-permute-start | bytes 2359304 | tf_op jit(solution)/shard_map/ppermute | solution.py:186
  126.6 1.9 %collective-permute-done.2.sibling_ref = f32[8,2,3,8,512]{4,3,2,1,0:T(8,128)S(1)} collective-permute-done((f32[8,2,3,8,512]{4,3,2,1,0:T(8,128)S(1)}, f32[8,2,3,8,512]{4,3,2,1,0:T(8,128)S(1)}, u32[]{:S(2)}, u32[]{:S(2)}) %collective-permute-start.2) | collective-permute-done | bytes 786464 | tf_op jit(solution)/shard_map/ppermute | solution.py:186
  128.5 1.2 shard_map.86
  (9 shorter events, 0.2 us)
Async XLA Ops:
  0.6 6.8 %copy-start.1 = (bf16[112,512]{1,0:T(8,128)(2,1)S(1)}, bf16[112,512]{1,0:T(8,128)(2,1)}, u32[]{:S(2)}) copy-start(bf16[112,512]{1,0:T(8,128)(2,1)} %param.7) | copy-start | bytes 344068
  1.9 47.3 %collective-permute-start.1 = (bf16[16,112,256]{2,1,0:T(8,128)(2,1)S(1)}, bf16[16,112,256]{2,1,0:T(8,128)(2,1)S(1)}, u32[]{:S(2)}, u32[]{:S(2)}) collective-permute-start(bf16[16,112,256]{2,1,0:T(8,128)(2,1)S(1)} %dynamic-slice_bitcast_fusion), channel_id=1, source_target_pairs={{0,1},{1,0},{2,3},{3,2},{4,5},{5,4},{6,7},{7,6},{8,9},{9,8},{10,11... | collective-permute-start | bytes 2752520 | tf_op jit(solution)/shard_map/ppermute | solution.py:148
  49.2 1.5 %copy-start = (bf16[3584,256]{1,0:T(8,128)(2,1)S(1)}, bf16[3584,256]{1,0:T(8,128)(2,1)}, u32[]{:S(2)}) copy-start(bf16[3584,256]{1,0:T(8,128)(2,1)} %param.6) | copy-start | bytes 5505028
  52.1 19.5 %copy-start.2 = (s32[32]{0:T(128)S(1)}, s32[32]{0:T(128)}, u32[]{:S(2)}) copy-start(s32[32]{0:T(128)} %param.8) | copy-start | bytes 388
  53.1 24.0 %all-to-all-start = ((f16[32,2,8,512]{3,2,1,0:T(8,128)(2,1)}), f16[32,2,8,512]{3,2,1,0:T(8,128)(2,1)S(1)}, u32[]{:S(2)}, u32[]{:S(2)}) async-start(f16[32,2,8,512]{3,2,1,0:T(8,128)(2,1)} %multiply_convert_fusion.1), calls=%async_computation | async-start | bytes 1048576 | tf_op jit(solution)/shard_map/all_to_all | solution.py:30
  66.9 8.9 %collective-permute-start = (f32[3,8,512]{2,1,0:T(8,128)S(1)}, f32[3,8,512]{2,1,0:T(8,128)S(1)}, u32[]{:S(2)}, u32[]{:S(2)}) collective-permute-start(f32[3,8,512]{2,1,0:T(8,128)S(1)} %pad_maximum_fusion.4), channel_id=1, source_target_pairs={{0,1},{1,0},{2,3},{3,2},{4,5},{5,4},{6,7},{7,6},{8,9},{9,8},{10,11... | collective-permute-start | bytes 147464 | tf_op jit(solution)/shard_map/ppermute | solution.py:166
  115.0 13.6 %collective-permute-start.2 = (f32[8,2,3,8,512]{4,3,2,1,0:T(8,128)S(1)}, f32[8,2,3,8,512]{4,3,2,1,0:T(8,128)S(1)}, u32[]{:S(2)}, u32[]{:S(2)}) collective-permute-start(f32[8,2,3,8,512]{4,3,2,1,0:T(8,128)S(1)} %pad_maximum_fusion.half_ref), channel_id=1, source_target_pairs={{0,32},{32,0},{1,33},{33,1},{2,34},{34,2},{3,35},{35,3},{4,36},{36... | collective-permute-start | bytes 2359304 | tf_op jit(solution)/shard_map/ppermute | solution.py:186

commit v16 on v13

--- a/solution.py
+++ b/solution.py
@@ -180,9 +180,9 @@
 
     placed = jnp.stack([wanted(here + i) for i in range(2)]).reshape(1, 2, 4, 8, 512)
     shared = jnp.broadcast_to(placed, (8, 2, 4, 8, 512)).reshape(16, 4, 8, 512)
-    half = unpack(exchange(shared, CHIPS))
-    sibling = lax.ppermute(half, "c", SWAP)
-    return assemble(core, half, sibling)
+    packed = exchange(shared, CHIPS)
+    sibling = lax.ppermute(packed, "c", SWAP)
+    return assemble(core, unpack(packed), unpack(sibling))
 
 
 def solution(mesh):

time: 130 us -> 130 us (level)
  no operation moved by 1% of the time
where the time goes in v16:
time: 130 us; the launch traced here: 129 us
  blocking collectives  79.6 us (61%)
  starting transfers between devices  33.2 us (26%)
  local copies, waits for them, and re-layouts  4.59 us (4%)
  waiting for transfers between devices  3.57 us (3%)
  between operations  3.4 us (3%)
  Pallas kernels  2.61 us (2%)
  other arithmetic  2.2 us (2%)
    all_gather x1, blocking collectives, on_device(): cotangents = lax.all_gather(scaled, 'z', axis=0, tiled=True)  41.7 us
    all_gather x1, blocking collectives, on_device(): along = lax.all_gather(pack(*results), 'z', axis=0, tiled=False)  26.8 us
    all_to_all x1, starting transfers between devices, exchange(): return lax.all_to_all(array, axes, split_axis=0, concat_axis=0, tiled=True)  12.3 us
    all_to_all x1, blocking collectives, exchange(): return lax.all_to_all(array, axes, split_axis=0, concat_axis=0, tiled=True)  11.1 us
    ppermute x1, starting transfers between devices, on_device(): sibling = lax.ppermute(packed, 'c', SWAP)  10.7 us
    ppermute x1, starting transfers between devices, on_device(): got = lax.ppermute(pick(tokens, other, 1), 'xh', SWAP)  5.48 us
    ppermute x1, starting transfers between devices, on_device(): peer_rows = lax.ppermute(eight(other), 'xh', SWAP)  4.79 us
  transfers between devices with their start and end apart: 4, of which 3 were waited for; matrix products, arithmetic and copies ran while one was open for 2% of the time, Pallas kernels for 0%

profile of v16, /device:TPU:1, one launch (start us, length us, event | category | flops | bytes accessed | tf_op | source)
XLA Modules:
  0.0 129.1 jit_solution(2496095919998166956)
XLA Ops:
  0.6 0.0 copy-start.1
  0.6 1.3 dynamic-slice_bitcast_fusion
  1.9 5.5 %collective-permute-start.1 = (bf16[16,112,256]{2,1,0:T(8,128)(2,1)S(1)}, bf16[16,112,256]{2,1,0:T(8,128)(2,1)S(1)}, u32[]{:S(2)}, u32[]{:S(2)}) collective-permute-start(bf16[16,112,256]{2,1,0:T(8,128)(2,1)S(1)} %dynamic-slice_bitcast_fusion), channel_id=1, source_target_pairs={{0,1},{1,0},{2,3},{3,2},{4,5},{5,4},{6,7},{7,6},{8,9},{9,8},{10,11... | collective-permute-start | bytes 2752520 | tf_op jit(solution)/shard_map/ppermute | solution.py:146
  7.4 0.0 copy-done.1
  7.5 41.7 %all-gather.2 = f16[1792,512]{1,0:T(8,128)(2,1)S(1)} all-gather(f16[112,512]{1,0:T(8,128)(2,1)S(1)} %multiply_convert_fusion.2), channel_id=1, replica_groups=mesh['xl'=2,'y'=4,'c'=2,'z'=16,'xh'=2] {'z'}, dimensions={0}, use_global_device_ids=true | all-gather | bytes 1949696 | tf_op jit(solution)/shard_map/all_gather | solution.py:161
  49.2 0.0 copy-start
  49.2 0.0 collective-permute-done.1
  49.2 0.4 multiply_convert_fusion.cotangents_ref
  49.6 1.1 copy-done
  50.7 1.4 %shard_map.85 = f32[32,2,8,512]{3,2,1,0:T(8,128)S(1)} custom-call(s32[1]{0:T(128)} %bitcast.10.mine_ref, bf16[16,2,112,256]{3,2,1,0:T(8,128)(2,1)S(1)} %bitcast.55, bf16[1792,256]{1,0:T(8,128)(2,1)S(1)} %bitcast.56, bf16[1792,512]{1,0:T(8,128)(2,1)S(1)} %multiply_convert_fusion.cotangents_ref), custom_call_target="tpu_custom_call" | custom-call | flops 939524096 | bytes 6291456 | tf_op jit(solution)/shard_map/pallas_call | solution.py:87
  52.1 0.0 copy-start.2
  52.1 0.9 multiply_convert_fusion.1
  53.1 12.3 %all-to-all-start = ((f16[32,2,8,512]{3,2,1,0:T(8,128)(2,1)}), f16[32,2,8,512]{3,2,1,0:T(8,128)(2,1)S(1)}, u32[]{:S(2)}, u32[]{:S(2)}) async-start(f16[32,2,8,512]{3,2,1,0:T(8,128)(2,1)} %multiply_convert_fusion.1), calls=%async_computation | async-start | bytes 1048576 | tf_op jit(solution)/shard_map/all_to_all | solution.py:30
  65.3 0.7 dynamic-slice_bitcast_fusion.8
  66.1 0.8 dynamic-slice_bitcast_fusion.6
  66.9 4.8 %collective-permute-start = (f32[3,8,512]{2,1,0:T(8,128)S(1)}, f32[3,8,512]{2,1,0:T(8,128)S(1)}, u32[]{:S(2)}, u32[]{:S(2)}) collective-permute-start(f32[3,8,512]{2,1,0:T(8,128)S(1)} %pad_maximum_fusion.5), channel_id=1, source_target_pairs={{0,1},{1,0},{2,3},{3,2},{4,5},{5,4},{6,7},{7,6},{8,9},{9,8},{10,11... | collective-permute-start | bytes 147464 | tf_op jit(solution)/shard_map/ppermute | solution.py:164
  71.7 0.0 copy-done.2
  71.7 0.7 fusion.15
  74.9 0.9 collective-permute-done
  75.8 1.5 %all-to-all-done = f16[32,2,8,512]{3,2,1,0:T(8,128)(2,1)S(1)} async-done(((f16[32,2,8,512]{3,2,1,0:T(8,128)(2,1)}), f16[32,2,8,512]{3,2,1,0:T(8,128)(2,1)S(1)}, u32[]{:S(2)}, u32[]{:S(2)}) %all-to-all-start) | async-done | bytes 524320 | tf_op jit(solution)/shard_map/all_to_all | solution.py:30
  77.3 0.1 convert_reduce_fusion
  77.3 0.1 fusion.13
  77.5 26.8 %all-gather.3 = f16[16,4,2,8,512]{4,3,2,1,0:T(8,128)(2,1)S(1)} all-gather(f16[1,4,2,8,512]{4,3,2,1,0:T(8,128)(2,1)S(1)} %pad_maximum_fusion.2), channel_id=1, replica_groups=mesh['xl'=2,'y'=4,'c'=2,'z'=16,'xh'=2] {'z'}, dimensions={0}, use_global_device_ids=true | all-gather | bytes 1114112 | tf_op jit(solution)/shard_map/all_gather | solution.py:174
  104.4 11.1 %all_to_all.10 = f16[16,4,8,512]{3,2,1,0:T(8,128)(2,1)S(1)} all-to-all(f16[16,4,8,512]{3,2,1,0:T(8,128)(2,1)S(1)} %bitcast.57), channel_id=1, replica_groups=mesh['xl'=2,'y'=4,'c'=2,'z'=16,'xh'=2] {'xl','y','xh'}, dimensions={0} | all-to-all | bytes 1048576 | tf_op jit(solution)/shard_map/all_to_all | solution.py:30
  115.5 10.7 %collective-permute-start.2 = (f16[16,4,8,512]{3,2,1,0:T(8,128)(2,1)S(1)}, f16[16,4,8,512]{3,2,1,0:T(8,128)(2,1)S(1)}, u32[]{:S(2)}, u32[]{:S(2)}) collective-permute-start(f16[16,4,8,512]{3,2,1,0:T(8,128)(2,1)S(1)} %all_to_all.10), channel_id=1, source_target_pairs={{0,32},{32,0},{1,33},{33,1},{2,34},{34,2},{3,35},{35,3},{4,36},{36... | collective-permute-start | bytes 1572872 | tf_op jit(solution)/shard_map/ppermute | solution.py:184
  126.1 0.1 convert_element_type.38
  126.3 0.1 fusion.1
  126.4 0.1 pad_maximum_fusion.half_ref
  126.4 1.2 collective-permute-done.2
  127.7 0.1 convert_element_type.39
  127.8 0.1 fusion
  127.9 0.1 pad_maximum_fusion.1.sibling_ref
  128.0 1.2 shard_map.86
  (9 shorter events, 0.2 us)
Async XLA Ops:
  0.6 6.8 %copy-start.1 = (bf16[112,512]{1,0:T(8,128)(2,1)S(1)}, bf16[112,512]{1,0:T(8,128)(2,1)}, u32[]{:S(2)}) copy-start(bf16[112,512]{1,0:T(8,128)(2,1)} %param.7) | copy-start | bytes 344068
  1.9 47.3 %collective-permute-start.1 = (bf16[16,112,256]{2,1,0:T(8,128)(2,1)S(1)}, bf16[16,112,256]{2,1,0:T(8,128)(2,1)S(1)}, u32[]{:S(2)}, u32[]{:S(2)}) collective-permute-start(bf16[16,112,256]{2,1,0:T(8,128)(2,1)S(1)} %dynamic-slice_bitcast_fusion), channel_id=1, source_target_pairs={{0,1},{1,0},{2,3},{3,2},{4,5},{5,4},{6,7},{7,6},{8,9},{9,8},{10,11... | collective-permute-start | bytes 2752520 | tf_op jit(solution)/shard_map/ppermute | solution.py:146
  49.2 1.5 %copy-start = (bf16[3584,256]{1,0:T(8,128)(2,1)S(1)}, bf16[3584,256]{1,0:T(8,128)(2,1)}, u32[]{:S(2)}) copy-start(bf16[3584,256]{1,0:T(8,128)(2,1)} %param.6) | copy-start | bytes 5505028
  52.1 19.5 %copy-start.2 = (s32[32]{0:T(128)S(1)}, s32[32]{0:T(128)}, u32[]{:S(2)}) copy-start(s32[32]{0:T(128)} %param.8) | copy-start | bytes 388
  53.1 24.2 %all-to-all-start = ((f16[32,2,8,512]{3,2,1,0:T(8,128)(2,1)}), f16[32,2,8,512]{3,2,1,0:T(8,128)(2,1)S(1)}, u32[]{:S(2)}, u32[]{:S(2)}) async-start(f16[32,2,8,512]{3,2,1,0:T(8,128)(2,1)} %multiply_convert_fusion.1), calls=%async_computation | async-start | bytes 1048576 | tf_op jit(solution)/shard_map/all_to_all | solution.py:30
  66.9 8.9 %collective-permute-start = (f32[3,8,512]{2,1,0:T(8,128)S(1)}, f32[3,8,512]{2,1,0:T(8,128)S(1)}, u32[]{:S(2)}, u32[]{:S(2)}) collective-permute-start(f32[3,8,512]{2,1,0:T(8,128)S(1)} %pad_maximum_fusion.5), channel_id=1, source_target_pairs={{0,1},{1,0},{2,3},{3,2},{4,5},{5,4},{6,7},{7,6},{8,9},{9,8},{10,11... | collective-permute-start | bytes 147464 | tf_op jit(solution)/shard_map/ppermute | solution.py:164
  115.5 12.2 %collective-permute-start.2 = (f16[16,4,8,512]{3,2,1,0:T(8,128)(2,1)S(1)}, f16[16,4,8,512]{3,2,1,0:T(8,128)(2,1)S(1)}, u32[]{:S(2)}, u32[]{:S(2)}) collective-permute-start(f16[16,4,8,512]{3,2,1,0:T(8,128)(2,1)S(1)} %all_to_all.10), channel_id=1, source_target_pairs={{0,32},{32,0},{1,33},{33,1},{2,34},{34,2},{3,35},{35,3},{4,36},{36... | collective-permute-start | bytes 1572872 | tf_op jit(solution)/shard_map/ppermute | solution.py:184

commit v17 on v16

--- a/solution.py
+++ b/solution.py
@@ -105,32 +105,36 @@
     )(mine.reshape(1), tokens, got, cotangents)
 
 
-def assemble_kernel(core_ref, half_ref, sibling_ref, *refs):
-    outs, done = refs[:3], refs[3]
-    core = core_ref[0]
-    copies = []
-    for i in range(3):
-        for j, (source, place) in enumerate(((half_ref, core), (sibling_ref, 1 - core))):
-            copies.append(
-                pltpu.make_async_copy(source.at[:, i], outs[i].at[place], done.at[2 * i + j])
-            )
+def place_kernel(where_ref, source_ref, *refs):
+    outs, done = refs[-4:-1], refs[-1]
+    half = where_ref[0]
+    copies = [
+        pltpu.make_async_copy(source_ref.at[:, i], outs[i].at[half], done.at[i])
+        for i in range(3)
+    ]
     for copy in copies:
         copy.start()
     for copy in copies:
         copy.wait()
 
 
-def assemble(core, half, sibling):
-    in_vmem = pl.BlockSpec(memory_space=pltpu.VMEM)
-    outs = pl.pallas_call(
-        assemble_kernel,
+def place(half, source, outs=()):
+    return pl.pallas_call(
+        place_kernel,
         out_shape=[jax.ShapeDtypeStruct((2, 16, 8, 512), jnp.float32)] * 3,
-        in_specs=[pl.BlockSpec(memory_space=pltpu.SMEM), in_vmem, in_vmem],
-        out_specs=[pl.BlockSpec(memory_space=pl.ANY)] * 3,
-        scratch_shapes=[pltpu.SemaphoreType.DMA((6,))],
+        in_specs=[
+            pl.BlockSpec(memory_space=pltpu.SMEM),
+            pl.BlockSpec(memory_space=pltpu.VMEM),
+        ]
+        + [pl.BlockSpec(memory_space=pltpu.HBM)] * len(outs),
+        out_specs=[pl.BlockSpec(memory_space=pltpu.HBM)] * 3,
+        input_output_aliases={2 + i: i for i in range(len(outs))},
+        scratch_shapes=[pltpu.SemaphoreType.DMA((3,))],
         compiler_params=pltpu.CompilerParams(vmem_limit_bytes=40 * 1024 * 1024),
-    )(core.reshape(1), half, sibling)
-    return tuple(item.reshape(256, 512) for item in outs)
+        cost_estimate=pl.CostEstimate(
+            flops=0, bytes_accessed=2 * 1024 * 1024, transcendentals=0
+        ),
+    )(half.reshape(1), source, *outs)
 
 
 def on_device(activations, key_grads, partners, master_weight, first_moment, second_moment):
@@ -182,7 +186,8 @@
     shared = jnp.broadcast_to(placed, (8, 2, 4, 8, 512)).reshape(16, 4, 8, 512)
     packed = exchange(shared, CHIPS)
     sibling = lax.ppermute(packed, "c", SWAP)
-    return assemble(core, unpack(packed), unpack(sibling))
+    outs = place(1 - core, unpack(sibling), place(core, unpack(packed)))
+    return tuple(item.reshape(256, 512) for item in outs)
 
 
 def solution(mesh):

time: 130 us -> 130 us (level)
  transfers between devices with their start and end apart: 4 -> 4, of which waited for: 3 -> 3; matrix products, arithmetic and copies ran while one was open for 2% -> 2% of each run, Pallas kernels for 0% -> 1%
where the time goes in v17:
time: 130 us; the launch traced here: 129 us
  blocking collectives  79.6 us (61%)
  starting transfers between devices  33.2 us (26%)
  local copies, waits for them, and re-layouts  4.55 us (4%)
  between operations  3.43 us (3%)
  Pallas kernels  3.23 us (2%)
  waiting for transfers between devices  2.67 us (2%)
  other arithmetic  2.19 us (2%)
    all_gather x1, blocking collectives, on_device(): cotangents = lax.all_gather(scaled, 'z', axis=0, tiled=True)  41.7 us
    all_gather x1, blocking collectives, on_device(): along = lax.all_gather(pack(*results), 'z', axis=0, tiled=False)  26.8 us
    all_to_all x1, starting transfers between devices, exchange(): return lax.all_to_all(array, axes, split_axis=0, concat_axis=0, tiled=True)  12.3 us
    all_to_all x1, blocking collectives, exchange(): return lax.all_to_all(array, axes, split_axis=0, concat_axis=0, tiled=True)  11.1 us
    ppermute x1, starting transfers between devices, on_device(): sibling = lax.ppermute(packed, 'c', SWAP)  10.7 us
    ppermute x1, starting transfers between devices, on_device(): got = lax.ppermute(pick(tokens, other, 1), 'xh', SWAP)  5.48 us
    ppermute x1, starting transfers between devices, on_device(): peer_rows = lax.ppermute(eight(other), 'xh', SWAP)  4.79 us
  transfers between devices with their start and end apart: 4, of which 3 were waited for; matrix products, arithmetic and copies ran while one was open for 2% of the time, Pallas kernels for 1%

profile of v17, /device:TPU:1, one launch (start us, length us, event | category | flops | bytes accessed | tf_op | source)
XLA Modules:
  0.0 128.9 jit_solution(1383245841480194865)
XLA Ops:
  0.6 0.0 copy-start.1
  0.6 1.3 dynamic-slice_bitcast_fusion
  1.9 5.5 %collective-permute-start.1 = (bf16[16,112,256]{2,1,0:T(8,128)(2,1)S(1)}, bf16[16,112,256]{2,1,0:T(8,128)(2,1)S(1)}, u32[]{:S(2)}, u32[]{:S(2)}) collective-permute-start(bf16[16,112,256]{2,1,0:T(8,128)(2,1)S(1)} %dynamic-slice_bitcast_fusion), channel_id=1, source_target_pairs={{0,1},{1,0},{2,3},{3,2},{4,5},{5,4},{6,7},{7,6},{8,9},{9,8},{10,11... | collective-permute-start | bytes 2752520 | tf_op jit(solution)/shard_map/ppermute | solution.py:150
  7.4 0.0 copy-done.1
  7.5 41.7 %all-gather.2 = f16[1792,512]{1,0:T(8,128)(2,1)S(1)} all-gather(f16[112,512]{1,0:T(8,128)(2,1)S(1)} %multiply_convert_fusion.2), channel_id=1, replica_groups=mesh['xl'=2,'y'=4,'c'=2,'z'=16,'xh'=2] {'z'}, dimensions={0}, use_global_device_ids=true | all-gather | bytes 1949696 | tf_op jit(solution)/shard_map/all_gather | solution.py:165
  49.2 0.0 copy-start
  49.2 0.0 collective-permute-done.1
  49.2 0.4 multiply_convert_fusion.cotangents_ref
  49.6 1.1 copy-done
  50.7 1.4 %shard_map.85 = f32[32,2,8,512]{3,2,1,0:T(8,128)S(1)} custom-call(s32[1]{0:T(128)} %bitcast.10.mine_ref, bf16[16,2,112,256]{3,2,1,0:T(8,128)(2,1)S(1)} %bitcast.56, bf16[1792,256]{1,0:T(8,128)(2,1)S(1)} %bitcast.57, bf16[1792,512]{1,0:T(8,128)(2,1)S(1)} %multiply_convert_fusion.cotangents_ref), custom_call_target="tpu_custom_call" | custom-call | flops 939524096 | bytes 6291456 | tf_op jit(solution)/shard_map/pallas_call | solution.py:87
  52.1 0.0 copy-start.2
  52.1 0.9 multiply_convert_fusion.1
  53.1 12.3 %all-to-all-start = ((f16[32,2,8,512]{3,2,1,0:T(8,128)(2,1)}), f16[32,2,8,512]{3,2,1,0:T(8,128)(2,1)S(1)}, u32[]{:S(2)}, u32[]{:S(2)}) async-start(f16[32,2,8,512]{3,2,1,0:T(8,128)(2,1)} %multiply_convert_fusion.1), calls=%async_computation | async-start | bytes 1048576 | tf_op jit(solution)/shard_map/all_to_all | solution.py:30
  65.3 0.7 dynamic-slice_bitcast_fusion.8
  66.1 0.8 dynamic-slice_bitcast_fusion.6
  66.9 4.8 %collective-permute-start = (f32[3,8,512]{2,1,0:T(8,128)S(1)}, f32[3,8,512]{2,1,0:T(8,128)S(1)}, u32[]{:S(2)}, u32[]{:S(2)}) collective-permute-start(f32[3,8,512]{2,1,0:T(8,128)S(1)} %pad_maximum_fusion.5), channel_id=1, source_target_pairs={{0,1},{1,0},{2,3},{3,2},{4,5},{5,4},{6,7},{7,6},{8,9},{9,8},{10,11... | collective-permute-start | bytes 147464 | tf_op jit(solution)/shard_map/ppermute | solution.py:168
  71.7 0.0 copy-done.2
  71.7 0.6 fusion.15
  74.9 0.9 collective-permute-done
  75.8 1.5 %all-to-all-done = f16[32,2,8,512]{3,2,1,0:T(8,128)(2,1)S(1)} async-done(((f16[32,2,8,512]{3,2,1,0:T(8,128)(2,1)}), f16[32,2,8,512]{3,2,1,0:T(8,128)(2,1)S(1)}, u32[]{:S(2)}, u32[]{:S(2)}) %all-to-all-start) | async-done | bytes 524320 | tf_op jit(solution)/shard_map/all_to_all | solution.py:30
  77.3 0.1 convert_reduce_fusion
  77.3 0.1 fusion.13
  77.5 26.8 %all-gather.3 = f16[16,4,2,8,512]{4,3,2,1,0:T(8,128)(2,1)S(1)} all-gather(f16[1,4,2,8,512]{4,3,2,1,0:T(8,128)(2,1)S(1)} %pad_maximum_fusion.2), channel_id=1, replica_groups=mesh['xl'=2,'y'=4,'c'=2,'z'=16,'xh'=2] {'z'}, dimensions={0}, use_global_device_ids=true | all-gather | bytes 1114112 | tf_op jit(solution)/shard_map/all_gather | solution.py:178
  104.4 11.1 %all_to_all.10 = f16[16,4,8,512]{3,2,1,0:T(8,128)(2,1)S(1)} all-to-all(f16[16,4,8,512]{3,2,1,0:T(8,128)(2,1)S(1)} %bitcast.58), channel_id=1, replica_groups=mesh['xl'=2,'y'=4,'c'=2,'z'=16,'xh'=2] {'xl','y','xh'}, dimensions={0} | all-to-all | bytes 1048576 | tf_op jit(solution)/shard_map/all_to_all | solution.py:30
  115.5 10.7 %collective-permute-start.2 = (f16[16,4,8,512]{3,2,1,0:T(8,128)(2,1)S(1)}, f16[16,4,8,512]{3,2,1,0:T(8,128)(2,1)S(1)}, u32[]{:S(2)}, u32[]{:S(2)}) collective-permute-start(f16[16,4,8,512]{3,2,1,0:T(8,128)(2,1)S(1)} %all_to_all.10), channel_id=1, source_target_pairs={{0,32},{32,0},{1,33},{33,1},{2,34},{34,2},{3,35},{35,3},{4,36},{36... | collective-permute-start | bytes 1572872 | tf_op jit(solution)/shard_map/ppermute | solution.py:188
  126.1 0.1 convert_element_type.39
  126.3 0.1 fusion
  126.4 0.1 pad_maximum_fusion.1.source_ref
  126.4 0.9 shard_map.86
  127.4 0.3 collective-permute-done.2
  127.7 0.1 convert_element_type.38
  127.8 0.1 fusion.1
  127.9 0.1 pad_maximum_fusion.source_ref
  128.0 0.9 shard_map.87
  (9 shorter events, 0.2 us)
Async XLA Ops:
  0.6 6.8 %copy-start.1 = (bf16[112,512]{1,0:T(8,128)(2,1)S(1)}, bf16[112,512]{1,0:T(8,128)(2,1)}, u32[]{:S(2)}) copy-start(bf16[112,512]{1,0:T(8,128)(2,1)} %param.7) | copy-start | bytes 344068
  1.9 47.3 %collective-permute-start.1 = (bf16[16,112,256]{2,1,0:T(8,128)(2,1)S(1)}, bf16[16,112,256]{2,1,0:T(8,128)(2,1)S(1)}, u32[]{:S(2)}, u32[]{:S(2)}) collective-permute-start(bf16[16,112,256]{2,1,0:T(8,128)(2,1)S(1)} %dynamic-slice_bitcast_fusion), channel_id=1, source_target_pairs={{0,1},{1,0},{2,3},{3,2},{4,5},{5,4},{6,7},{7,6},{8,9},{9,8},{10,11... | collective-permute-start | bytes 2752520 | tf_op jit(solution)/shard_map/ppermute | solution.py:150
  49.2 1.5 %copy-start = (bf16[3584,256]{1,0:T(8,128)(2,1)S(1)}, bf16[3584,256]{1,0:T(8,128)(2,1)}, u32[]{:S(2)}) copy-start(bf16[3584,256]{1,0:T(8,128)(2,1)} %param.6) | copy-start | bytes 5505028
  52.1 19.5 %copy-start.2 = (s32[32]{0:T(128)S(1)}, s32[32]{0:T(128)}, u32[]{:S(2)}) copy-start(s32[32]{0:T(128)} %param.8) | copy-start | bytes 388
  53.1 24.2 %all-to-all-start = ((f16[32,2,8,512]{3,2,1,0:T(8,128)(2,1)}), f16[32,2,8,512]{3,2,1,0:T(8,128)(2,1)S(1)}, u32[]{:S(2)}, u32[]{:S(2)}) async-start(f16[32,2,8,512]{3,2,1,0:T(8,128)(2,1)} %multiply_convert_fusion.1), calls=%async_computation | async-start | bytes 1048576 | tf_op jit(solution)/shard_map/all_to_all | solution.py:30
  66.9 8.9 %collective-permute-start = (f32[3,8,512]{2,1,0:T(8,128)S(1)}, f32[3,8,512]{2,1,0:T(8,128)S(1)}, u32[]{:S(2)}, u32[]{:S(2)}) collective-permute-start(f32[3,8,512]{2,1,0:T(8,128)S(1)} %pad_maximum_fusion.5), channel_id=1, source_target_pairs={{0,1},{1,0},{2,3},{3,2},{4,5},{5,4},{6,7},{7,6},{8,9},{9,8},{10,11... | collective-permute-start | bytes 147464 | tf_op jit(solution)/shard_map/ppermute | solution.py:168
  115.5 12.2 %collective-permute-start.2 = (f16[16,4,8,512]{3,2,1,0:T(8,128)(2,1)S(1)}, f16[16,4,8,512]{3,2,1,0:T(8,128)(2,1)S(1)}, u32[]{:S(2)}, u32[]{:S(2)}) collective-permute-start(f16[16,4,8,512]{3,2,1,0:T(8,128)(2,1)S(1)} %all_to_all.10), channel_id=1, source_target_pairs={{0,32},{32,0},{1,33},{33,1},{2,34},{34,2},{3,35},{35,3},{4,36},{36... | collective-permute-start | bytes 1572872 | tf_op jit(solution)/shard_map/ppermute | solution.py:188
